TPU v7x, 32 devices: a whole 2x2x4 slice. The times are simulated.
32 devices in a mesh: gx: 8 (over z, x), gy: 4 (over y, core).
Axes of the slice: x: 2, y: 2, z: 4, core: 2. Of those that a mesh axis runs over, the one named last changes fastest.
Arguments:
- misfit: float32 [2, 16, 256, 1024], P(None, None, 'gx', 'gy'), may hold values from -6 to 6
- viscosity: float32 [16, 256, 1024], P(None, 'gx', 'gy'), may hold values from 0.1 to 10
- friction: float32 [256, 1024], P('gx', 'gy'), may hold values from 0.5 to 50
- ice_mask: int32 [256, 1024], P('gx', 'gy'), may hold values 0 or 1
- grounded: int32 [256, 1024], P('gx', 'gy'), may hold values 0 or 1
Outputs:
- adjoint_velocity: float32 [2, 16, 256, 1024], P(None, None, 'gx', 'gy')
All inputs are finite; a program needn't handle non-finite values. No bound on the sum of `ice_mask` or of `grounded` on one device may be relied on, other than what follows from the above.
Results may differ from a plain program's by a relative error of at most 0.00002.
Values sent between devices are 32-bit elements; how exact they have to be, the bound alone decides.
No kernel may reach another device: no remote copies, remote signals or barrier semaphores. Data moves between devices by JAX's collectives and lax.ppermute only.
A program may use at most 128 MiB of HBM per device.

v0:
```python
import functools

import jax
import jax.numpy as jnp
from jax import lax
from jax.experimental import pallas as pl
from jax.experimental.pallas import tpu as pltpu
from jax.sharding import PartitionSpec as P

LEVELS = 4
COARSE_ITERS = 20
OMEGA = 0.6
CROSS = 0.75
NP = 56
LANES = 128
RIM0 = 4
RIM1 = 13
RIM2 = 6
RIM3 = 2
STRIP1 = 16
NC = 15
VMEM_LIMIT = 60 * 1024 * 1024
F32 = jnp.float32


def rows_loop(first, last, body, unroll):
    count = (last - first) // unroll

    def step(i, carry):
        for j in range(unroll):
            body(first + i * unroll + j)
        return carry

    if count:
        lax.fori_loop(0, count, step, 0)
    for r in range(first + count * unroll, last):
        body(r)


def lane_ids(rows=8):
    return lax.broadcasted_iota(jnp.int32, (rows, LANES), 1)


def shifted(tiles, closed):
    lane = lax.broadcasted_iota(jnp.int32, tiles[0].shape, 1)
    up = [pltpu.roll(v, LANES - 1, 1) for v in tiles]
    down = [pltpu.roll(v, 1, 1) for v in tiles]
    n = len(tiles)
    if closed:
        zero = jnp.zeros_like(tiles[0])
        return (
            [jnp.where(lane == LANES - 1, zero, v) for v in up],
            [jnp.where(lane == 0, zero, v) for v in down],
        )
    if n == 1:
        return up, down
    return (
        [jnp.where(lane == LANES - 1, up[(t + 1) % n], up[t]) for t in range(n)],
        [jnp.where(lane == 0, down[(t - 1) % n], down[t]) for t in range(n)],
    )


def twice(v):
    return jnp.concatenate([v, v], 0)


def make_coefs(data, coef, scaled, diag, first, last, horizontal, closed, unroll):
    nt = data.shape[1]
    sub = lax.broadcasted_iota(jnp.int32, (8, LANES), 0)

    def row(r):
        mids = [data[r, t, 32:48, :] for t in range(nt)]
        norths, souths = shifted(mids, closed)
        for t in range(nt):
            mid = mids[t]
            west = (0.5 * horizontal) * (mid + data[r - 1, t, 32:48, :])
            east = (0.5 * horizontal) * (mid + data[r + 1, t, 32:48, :])
            north = (0.5 * horizontal) * (mid + norths[t])
            south = (0.5 * horizontal) * (mid + souths[t])
            low, high = mid[:8], mid[8:]
            inner = 2.0 * (low + high)
            outer = jnp.where(sub == 7, 0.0, 2.0 * (high + pltpu.roll(low, 7, 0)))
            outer_down = pltpu.roll(outer, 1, 0)
            coef[r, t, 0:16, :] = west
            coef[r, t, 16:32, :] = north
            coef[r, t, 32:48, :] = south
            coef[r, t, 48:64, :] = (CROSS * horizontal) * mid
            coef[r, t, 64:72, :] = inner
            coef[r, t, 72:80, :] = outer
            coef[r, t, 80:88, :] = outer_down
            ice = data[r, t, 48:49, :]
            drag = data[r, t, 49:50, :]
            bottom = jnp.where(sub == 0, drag, 0.0)
            upright = jnp.concatenate([inner + outer_down + bottom, inner + outer], 0)
            along_x = east + west
            along_y = north + south
            rest = 1.0 - ice
            for c, lateral in enumerate((4.0 * along_x + along_y, along_x + 4.0 * along_y)):
                diagonal = ice * (lateral + upright) + rest
                inverse = OMEGA / diagonal
                coef[r, t, 88 + 16 * c : 104 + 16 * c, :] = ice * inverse
                scaled[r, t, 16 * c : 16 * c + 16, :] = inverse * data[r, t, 16 * c : 16 * c + 16, :]
                if diag is not None:
                    diag[r, t, 16 * c : 16 * c + 16, :] = diagonal

    rows_loop(first, last, row, unroll)


def prepare(w, coef, slope, across, first, last, closed, unroll):
    nt = w.shape[1]

    def row(r):
        norths, souths = shifted([w[r, t] for t in range(nt)], closed)
        for t in range(nt):
            slope[r, t] = norths[t] - souths[t]
            across[r, t] = twice(coef[r, t, 16:32, :]) * norths[t] + twice(coef[r, t, 32:48, :]) * souths[t]

    rows_loop(first, last, row, unroll)


def off_diagonal(w, coef, slope, across, r, t):
    here = w[r, t]
    along = twice(coef[r + 1, t, 0:16, :]) * w[r + 1, t] + twice(coef[r, t, 0:16, :]) * w[r - 1, t]
    side = across[r, t]
    mixed = slope[r + 1, t] - slope[r - 1, t]
    cross = coef[r, t, 48:64, :]
    inner = coef[r, t, 64:72, :]
    outer = coef[r, t, 72:80, :]
    outer_down = coef[r, t, 80:88, :]
    parts = []
    for c in range(2):
        mine = slice(16 * c, 16 * c + 16)
        other = slice(16 - 16 * c, 32 - 16 * c)
        low, high = here[16 * c : 16 * c + 8], here[16 * c + 8 : 16 * c + 16]
        column = jnp.concatenate(
            [inner * high + outer_down * pltpu.roll(high, 1, 0), inner * low + outer * pltpu.roll(low, 7, 0)], 0
        )
        if c == 0:
            lateral = 4.0 * along[mine] + side[mine]
        else:
            lateral = along[mine] + 4.0 * side[mine]
        parts.append(lateral + cross * mixed[other] + column)
    return here, jnp.concatenate(parts, 0)


def sweep(w, new, coef, scaled, slope, across, first, last, closed, unroll, tiles=None, emit=None):
    nt = w.shape[1]
    prepare(w, coef, slope, across, first - 1, last + 1, closed, unroll)

    def row(r):
        for t in range(nt if tiles is None else tiles):
            here, total = off_diagonal(w, coef, slope, across, r, t)
            value = (1.0 - OMEGA) * here + scaled[r, t] + coef[r, t, 88:120, :] * total
            if emit is None:
                new[r, t] = value
            else:
                emit(r, t, value)

    rows_loop(first, last, row, unroll)


def remainders(w, out, data, diag, coef, slope, across, first, last, unroll, tiles):
    prepare(w, coef, slope, across, first - 1, last + 1, False, unroll)

    def row(r):
        for t in range(tiles):
            here, total = off_diagonal(w, coef, slope, across, r, t)
            out[r, t] = data[r, t, 0:32, :] + data[r, t, 48:49, :] * total - diag[r, t] * here

    rows_loop(first, last, row, unroll)


def gather_lanes(v, index):
    return jnp.take_along_axis(v, index, axis=1, mode="promise_in_bounds")


def halve(first, second):
    lane = lax.broadcasted_iota(jnp.int32, first.shape, 1)
    even = (2 * lane) % LANES
    low = gather_lanes(first + pltpu.roll(first, LANES - 1, 1), even)
    if second is None:
        return low
    high = gather_lanes(second + pltpu.roll(second, LANES - 1, 1), even)
    return jnp.where(lane < LANES // 2, low, high)


def restrict_row(source, planes, r):
    both = [source[r, t, planes, :] + source[r + 1, t, planes, :] for t in range(min(2, source.shape[1]))]
    return 0.25 * halve(both[0], both[1] if len(both) > 1 else None)


def prolong_row(tiles, fine_tiles):
    lane = lax.broadcasted_iota(jnp.int32, tiles[0].shape, 1)
    low = lane // 2
    high = LANES // 2 + lane // 2
    first = tiles[0]
    last = tiles[-1]
    out = [gather_lanes(first, low)]
    if fine_tiles == 2:
        out.append(gather_lanes(first, high))
    else:
        out.append(gather_lanes(first, high))
        out.append(gather_lanes(last, jnp.where(lane < LANES // 2, low, high)))
    return out


def put(strip, v, shift, width, at):
    lane = lax.broadcasted_iota(jnp.int32, v.shape, 1)
    rolled = pltpu.roll(v, shift % LANES, 1) if shift % LANES else v
    return jnp.where((lane >= at) & (lane < at + width), rolled, strip)


def unpack_rim(left, right, at, width):
    lane = lax.broadcasted_iota(jnp.int32, left.shape, 1)
    to_low = pltpu.roll(right, (LANES - at) % LANES, 1) if at else right
    shift = (2 * LANES - width - at) % LANES
    to_high = pltpu.roll(left, shift, 1) if shift else left
    return jnp.where(lane < LANES // 2, to_low, to_high)


def arrange_kernel(misfit, viscosity, friction, ice_mask, grounded, data, strips, misfit_half, viscosity_half, sems):
    rows = friction.shape[0]
    copies = []
    for t in range(2):
        lanes = pl.ds(t * LANES, LANES)
        copies.append(pltpu.make_async_copy(misfit.at[:, lanes], misfit_half.at[t], sems.at[t]))
        copies.append(pltpu.make_async_copy(viscosity.at[:, lanes], viscosity_half.at[t], sems.at[2 + t]))
    for copy in copies:
        copy.start()
    for copy in copies:
        copy.wait()
    sub = lax.broadcasted_iota(jnp.int32, (8, LANES), 0)
    stride = 2 * rows

    def eight(i, carry):
        block = pl.ds(pl.multiple_of(8 * i, 8), 8)
        for t in range(2):
            lanes = pl.ds(t * LANES, LANES)
            ices = ice_mask[block, lanes].astype(F32)
            drags = friction[block, lanes] * grounded[block, lanes].astype(F32)
            for j in range(8):
                r = 8 * i + j
                ice, drag = ices[j : j + 1], drags[j : j + 1]
                for c in range(2):
                    for p in range(2):
                        v = misfit_half[t, pl.ds(c * 16 * rows + p * rows + r, 8, stride=stride), :]
                        data[r, t, 16 * c + 8 * p : 16 * c + 8 * p + 8, :] = v * ice
                for p in range(2):
                    data[r, t, 32 + 8 * p : 40 + 8 * p, :] = viscosity_half[t, pl.ds(p * rows + r, 8, stride=stride), :]
                data[r, t, 48:56, :] = jnp.where(sub == 0, ice, jnp.where(sub == 1, drag, 0.0))
        return carry

    lax.fori_loop(0, rows // 8, eight, 0)
    for side in range(2):
        for first in range(0, NP, 8):
            planes = slice(first, first + 8)
            strip = jnp.zeros((8, LANES), F32)
            for r in range(rows):
                at = r * RIM0
                strip = put(strip, data[r, side, planes, :], at if side == 0 else at + RIM0, RIM0, at)
            strips[side, planes, :] = strip


def down0_kernel(own, sent, from_low, from_high, coarse, strips1, w_out, coef_out, scaled_out,
                 data, coef, scaled, diag, wa, slope, across, sems):
    rows = own.shape[0]
    total = rows + 2 * RIM0

    def copy_row(r):
        for t in range(2):
            data[RIM0 + r, t] = own[r, t]

    rows_loop(0, rows, copy_row, 4)
    for r in range(rows):
        data[RIM0 + r, 2] = unpack_rim(sent[2 * RIM0], sent[2 * RIM0 + 1], r * RIM0, RIM0)
    for r in range(RIM0):
        for t in range(2):
            data[r, t] = from_low[2 * r + t]
            data[RIM0 + rows + r, t] = from_high[2 * r + t]
        low_at = (rows - RIM0 + r) * RIM0
        data[r, 2] = unpack_rim(from_low[2 * RIM0], from_low[2 * RIM0 + 1], low_at, RIM0)
        data[RIM0 + rows + r, 2] = unpack_rim(from_high[2 * RIM0], from_high[2 * RIM0 + 1], r * RIM0, RIM0)

    make_coefs(data, coef, scaled, diag, 1, total - 1, 1.0, False, 1)
    copies = [pltpu.make_async_copy(coef, coef_out, sems.at[0]), pltpu.make_async_copy(scaled, scaled_out, sems.at[1])]
    for copy in copies:
        copy.start()
    sweep(scaled, wa, coef, scaled, slope, across, 2, total - 2, False, 1)
    copies.append(pltpu.make_async_copy(wa, w_out, sems.at[2]))
    copies[-1].start()

    def coefs_row(i):
        coarse[i, 32:56, :] = restrict_row(data, slice(32, 56), RIM0 + 2 * i)

    rows_loop(0, rows // 2, coefs_row, 2)
    remainders(wa, diag, data, diag, coef, slope, across, RIM0, RIM0 + rows, 1, 2)

    def target_row(i):
        coarse[i, 0:32, :] = restrict_row(diag, slice(0, 32), RIM0 + 2 * i)

    rows_loop(0, rows // 2, target_row, 2)
    group = LANES // STRIP1
    for side in range(2):
        for part in range(rows // 2 // group):
            for first in range(0, NP, 8):
                planes = slice(first, first + 8)
                strip = jnp.zeros((8, LANES), F32)
                for j in range(group):
                    at = j * STRIP1
                    shift = at if side == 0 else at + STRIP1
                    strip = put(strip, coarse[part * group + j, planes, :], shift, STRIP1, at)
                strips1[side, part, planes, :] = strip
    for copy in copies:
        copy.wait()


def down12_kernel(own, sent, from_low, from_high, piece, w1_out, coef1_out, scaled1_out, w2_out, coef2_out, scaled2_out,
                  data1, coef1, scaled1, diag1, wa1, slope1, across1,
                  data2, coef2, scaled2, diag2, wa2, slope2, across2, sems):
    rows = own.shape[0]
    total = rows + 2 * RIM1
    group = LANES // STRIP1
    parts = rows // group

    def rim(source, base, r):
        part, j = r // group, r % group
        return unpack_rim(source[base + part], source[base + parts + part], j * STRIP1, STRIP1)

    def copy_row(r):
        data1[RIM1 + r, 0] = own[r]

    rows_loop(0, rows, copy_row, 4)

    def copy_rim(r):
        data1[r, 0] = from_low[r]
        data1[RIM1 + rows + r, 0] = from_high[r]

    rows_loop(0, RIM1, copy_rim, 1)
    for r in range(rows):
        data1[RIM1 + r, 1] = rim(sent, RIM1, r)
    for r in range(RIM1):
        data1[r, 1] = rim(from_low, RIM1, rows - RIM1 + r)
        data1[RIM1 + rows + r, 1] = rim(from_high, RIM1, r)

    make_coefs(data1, coef1, scaled1, diag1, 1, total - 1, 0.25, False, 2)
    copies = [pltpu.make_async_copy(coef1, coef1_out, sems.at[0]), pltpu.make_async_copy(scaled1, scaled1_out, sems.at[1])]
    for copy in copies:
        copy.start()
    sweep(scaled1, wa1, coef1, scaled1, slope1, across1, 2, total - 2, False, 2)
    copies.append(pltpu.make_async_copy(wa1, w1_out, sems.at[2]))
    copies[-1].start()
    remainders(wa1, diag1, data1, diag1, coef1, slope1, across1, 3, total - 3, 2, 2)

    rows2 = rows // 2
    total2 = rows2 + 2 * RIM2

    def coefs_row(i):
        data2[i, 0, 32:56, :] = restrict_row(data1, slice(32, 56), 1 + 2 * i)

    rows_loop(0, total2, coefs_row, 2)

    def target_row(i):
        data2[i, 0, 0:32, :] = restrict_row(diag1, slice(0, 32), 1 + 2 * i)

    rows_loop(1, total2 - 1, target_row, 2)

    make_coefs(data2, coef2, scaled2, diag2, 1, total2 - 1, 0.0625, False, 2)
    sweep(scaled2, wa2, coef2, scaled2, slope2, across2, 2, total2 - 2, False, 2)
    late = [
        pltpu.make_async_copy(coef2, coef2_out, sems.at[3]),
        pltpu.make_async_copy(scaled2, scaled2_out, sems.at[4]),
        pltpu.make_async_copy(wa2, w2_out, sems.at[5]),
    ]
    for copy in late:
        copy.start()
    remainders(wa2, diag2, data2, diag2, coef2, slope2, across2, RIM2, RIM2 + rows2, 2, 1)

    rows3 = rows2 // 2
    width = LANES // rows3
    for first in range(0, NP, 8):
        planes = slice(first, first + 8)
        source = diag2 if first < 32 else data2
        strip = jnp.zeros((8, LANES), F32)
        for i in range(rows3):
            strip = put(strip, restrict_row(source, planes, RIM2 + 2 * i), i * width, width, i * width)
        piece[planes, :] = strip
    for copy in copies + late:
        copy.wait()


def up_kernel(place, pieces, w0_in, coef0_in, scaled0_in, w1_in, coef1_in, scaled1_in, w2_in, coef2_in, scaled2_in, result,
              data3, coef3, scaled3, wa3, wb3, slope3, across3,
              wa2, wb2, coef2, scaled2, slope2, across2,
              wa1, wb1, coef1, scaled1, slope1, across1,
              wa0, wb0, coef0, scaled0, slope0, across0, result_half, sems):
    copies = [
        pltpu.make_async_copy(source, target, sems.at[n])
        for n, (source, target) in enumerate(
            (
                (w2_in, wa2), (coef2_in, coef2), (scaled2_in, scaled2),
                (w1_in, wa1), (coef1_in, coef1), (scaled1_in, scaled1),
                (w0_in, wa0), (coef0_in, coef0), (scaled0_in, scaled0),
            )
        )
    ]
    for copy in copies:
        copy.start()

    devices_x, devices_y = pieces.shape[0], pieces.shape[1]
    rows3 = devices_y
    width = LANES // devices_y
    whole = devices_x * rows3
    zero = jnp.zeros((NP, LANES), F32)
    for r in range(RIM3):
        for end in (r, RIM3 + whole + r):
            data3[end, 0] = zero
            wa3[end, 0] = zero[:32]
            wb3[end, 0] = zero[:32]
            scaled3[end, 0] = zero[:32]
            slope3[end, 0] = zero[:32]
            coef3[end, 0, 0:16, :] = zero[:16]

    def assemble(d, carry):
        for i in range(rows3):
            line = jnp.zeros((NP, LANES), F32)
            for j in range(devices_y):
                line = put(line, pieces[d, j], (j - i) * width, width, j * width)
            data3[RIM3 + d * rows3 + i, 0] = line
        return carry

    lax.fori_loop(0, devices_x, assemble, 0)
    first, last = RIM3, RIM3 + whole
    make_coefs(data3, coef3, scaled3, None, first, last, 0.25 ** (LEVELS - 1), True, 2)

    def coarse_sweep(source, target):
        def look(r):
            norths, souths = shifted([source[r, 0]], True)
            slope3[r, 0] = norths[0] - souths[0]
            across3[r, 0] = twice(coef3[r, 0, 16:32, :]) * norths[0] + twice(coef3[r, 0, 32:48, :]) * souths[0]

        rows_loop(first, last, look, 4)

        def row(r):
            here, total = off_diagonal(source, coef3, slope3, across3, r, 0)
            target[r, 0] = (1.0 - OMEGA) * here + scaled3[r, 0] + coef3[r, 0, 88:120, :] * total

        rows_loop(first, last, row, 4)

    coarse_sweep(scaled3, wa3)

    def two_sweeps(i, carry):
        coarse_sweep(wa3, wb3)
        coarse_sweep(wb3, wa3)
        return carry

    lax.fori_loop(0, (COARSE_ITERS - 2) // 2, two_sweeps, 0)

    gx, gy, = place[0], place[1]
    lane = lane_ids(32)
    y = jnp.where(lane < 96, lane, lane - LANES)
    column = gy * width + (y + LANES) // 2 - LANES // 2
    inside = (column >= 0) & (column < LANES)
    pick = jnp.where(inside, column, 0)

    for copy in copies[:3]:
        copy.wait()
    rows2 = 2 * rows3
    for i in range(rows2 // 2 + 2 * RIM3):
        line = wa3[gx * rows3 + i, 0]
        add = jnp.where(inside, gather_lanes(line, pick), 0.0)
        for r in (2 * i + 2, 2 * i + 3):
            wa2[r, 0] = wa2[r, 0] + add
    total2 = rows2 + 2 * RIM2
    sweep(wa2, wb2, coef2, scaled2, slope2, across2, 3, total2 - 3, False, 2)
    sweep(wb2, wa2, coef2, scaled2, slope2, across2, 4, total2 - 4, False, 2)

    for copy in copies[3:6]:
        copy.wait()

    def add1(r):
        adds = prolong_row([wa2[r, 0]], 2)
        for t in range(2):
            for fine in (2 * r + 1, 2 * r + 2):
                wa1[fine, t] = wa1[fine, t] + adds[t]

    rows_loop(4, total2 - 4, add1, 2)
    total1 = 2 * rows2 + 2 * RIM1
    sweep(wa1, wb1, coef1, scaled1, slope1, across1, 11, total1 - 11, False, 2)
    sweep(wb1, wa1, coef1, scaled1, slope1, across1, 12, total1 - 12, False, 2)

    for copy in copies[6:]:
        copy.wait()

    def add0(r):
        adds = prolong_row([wa1[r, t] for t in range(2)], 3)
        for t in range(3):
            for fine in (2 * r - 22, 2 * r - 21):
                wa0[fine, t] = wa0[fine, t] + adds[t]

    rows_loop(12, total1 - 12, add0, 2)
    rows0 = 4 * rows2
    total0 = rows0 + 2 * RIM0
    sweep(wa0, wb0, coef0, scaled0, slope0, across0, 3, total0 - 3, False, 1)

    def emit(r, t, value):
        for c in range(2):
            for p in range(2):
                start = c * 16 * rows0 + p * rows0 + r - RIM0
                result_half[t, pl.ds(start, 8, stride=2 * rows0), :] = value[16 * c + 8 * p : 16 * c + 8 * p + 8]

    sweep(wb0, None, coef0, scaled0, slope0, across0, RIM0, RIM0 + rows0, False, 1, tiles=2, emit=emit)
    copies = [
        pltpu.make_async_copy(result_half.at[t], result.at[:, pl.ds(t * LANES, LANES)], sems.at[t]) for t in range(2)
    ]
    for copy in copies:
        copy.start()
    for copy in copies:
        copy.wait()


def shape(*dims):
    return jax.ShapeDtypeStruct(dims, F32)


VM = pl.BlockSpec(memory_space=pltpu.VMEM)
SM = pl.BlockSpec(memory_space=pltpu.SMEM)
HB = pl.BlockSpec(memory_space=pl.ANY)
PARAMS = pltpu.CompilerParams(vmem_limit_bytes=VMEM_LIMIT)


def buffers(rows, tiles, names):
    planes = {"data": NP, "coef": 8 * NC}
    return [pltpu.VMEM((rows, tiles, planes.get(name, 32), LANES), F32) for name in names]


def per_device(misfit, viscosity, friction, ice_mask, grounded):
    rows, columns = friction.shape
    gx, gy = lax.axis_index("gx"), lax.axis_index("gy")
    nx, ny = lax.axis_size("gx"), lax.axis_size("gy")
    upward = [(i, i + 1) for i in range(nx - 1)]
    downward = [(i + 1, i) for i in range(nx - 1)]

    def beside(strips):
        every = lax.all_gather(strips, "gy", axis=0)
        left = lax.dynamic_index_in_dim(every, jnp.maximum(gy - 1, 0), 0, keepdims=False)[1]
        right = lax.dynamic_index_in_dim(every, jnp.minimum(gy + 1, ny - 1), 0, keepdims=False)[0]
        return jnp.where(gy > 0, left, 0.0), jnp.where(gy < ny - 1, right, 0.0)

    data0, strips0 = pl.pallas_call(
        arrange_kernel,
        out_shape=(shape(rows, 2, NP, LANES), shape(2, NP, LANES)),
        in_specs=[HB, HB, VM, VM, VM],
        out_specs=(VM, VM),
        scratch_shapes=[
            pltpu.VMEM((2, 2 * 16 * rows, LANES), F32),
            pltpu.VMEM((2, 16 * rows, LANES), F32),
            pltpu.SemaphoreType.DMA((4,)),
        ],
        compiler_params=PARAMS,
        name="arrange",
    )(misfit.reshape(-1, columns), viscosity.reshape(-1, columns), friction, ice_mask, grounded)
    left, right = beside(strips0)
    rims = [left[None], right[None]]
    low_face = jnp.concatenate([data0[:RIM0].reshape(-1, NP, LANES)] + rims, 0)
    high_face = jnp.concatenate([data0[rows - RIM0 :].reshape(-1, NP, LANES)] + rims, 0)
    from_low = lax.ppermute(high_face, "gx", upward)
    from_high = lax.ppermute(low_face, "gx", downward)

    total0 = rows + 2 * RIM0
    rows1 = rows // 2
    group = LANES // STRIP1
    field0 = shape(total0, 3, 32, LANES)
    data1, strips1, w0, coef0, scaled0 = pl.pallas_call(
        down0_kernel,
        out_shape=(
            shape(rows1, NP, LANES),
            shape(2, rows1 // group, NP, LANES),
            field0,
            shape(total0, 3, 8 * NC, LANES),
            field0,
        ),
        in_specs=[VM] * 4,
        out_specs=(VM, VM, HB, HB, HB),
        scratch_shapes=buffers(total0, 3, ("data", "coef", "scaled", "diag", "w", "slope", "across"))
        + [pltpu.SemaphoreType.DMA((3,))],
        compiler_params=PARAMS,
        name="down0",
    )(data0, low_face, from_low, from_high)

    left, right = beside(strips1)
    low_face = jnp.concatenate([data1[:RIM1], left, right], 0)
    high_face = jnp.concatenate([data1[rows1 - RIM1 :], left, right], 0)
    from_low = lax.ppermute(high_face, "gx", upward)
    from_high = lax.ppermute(low_face, "gx", downward)

    total1 = rows1 + 2 * RIM1
    rows2 = rows1 // 2
    total2 = rows2 + 2 * RIM2
    field1 = shape(total1, 2, 32, LANES)
    field2 = shape(total2, 1, 32, LANES)
    names = ("data", "coef", "scaled", "diag", "w", "slope", "across")
    piece, w1, coef1, scaled1, w2, coef2, scaled2 = pl.pallas_call(
        down12_kernel,
        out_shape=(
            shape(NP, LANES),
            field1,
            shape(total1, 2, 8 * NC, LANES),
            field1,
            field2,
            shape(total2, 1, 8 * NC, LANES),
            field2,
        ),
        in_specs=[VM] * 4,
        out_specs=(VM,) + (HB,) * 6,
        scratch_shapes=buffers(total1, 2, names) + buffers(total2, 1, names) + [pltpu.SemaphoreType.DMA((6,))],
        compiler_params=PARAMS,
        name="down12",
    )(data1, low_face, from_low, from_high)

    pieces = lax.all_to_all(jnp.broadcast_to(piece, (nx * ny,) + piece.shape), ("gx", "gy"), 0, 0)
    pieces = pieces.reshape((nx, ny) + piece.shape)

    rows3 = rows2 // 2
    total3 = nx * rows3 + 2 * RIM3
    ups = ("w", "w", "coef", "scaled", "slope", "across")
    result = pl.pallas_call(
        up_kernel,
        out_shape=shape(2 * 16 * rows, columns),
        in_specs=[SM, VM] + [HB] * 9,
        out_specs=HB,
        scratch_shapes=buffers(total3, 1, ("data", "coef", "scaled", "w", "w", "slope", "across"))
        + buffers(total2, 1, ups)
        + buffers(total1, 2, ups)
        + buffers(total0, 3, ups)
        + [pltpu.VMEM((2, 2 * 16 * rows, LANES), F32), pltpu.SemaphoreType.DMA((9,))],
        compiler_params=PARAMS,
        name="up",
    )(jnp.stack([gx, gy]).astype(jnp.int32), pieces, w0, coef0, scaled0, w1, coef1, scaled1, w2, coef2, scaled2)
    return result.reshape(misfit.shape)


def solution(mesh):
    placed = (
        P(None, None, "gx", "gy"),
        P(None, "gx", "gy"),
        P("gx", "gy"),
        P("gx", "gy"),
        P("gx", "gy"),
    )
    return jax.shard_map(
        per_device, mesh=mesh, in_specs=placed, out_specs=P(None, None, "gx", "gy"), check_vma=False
    )
```

profile of v0, /device:TPU:0, one launch (start us, length us, event | category | flops | bytes accessed | tf_op | source)
XLA Modules:
  0.0 178.1 jit_solution(1422735994603140186)
XLA Ops:
  0.0 4.9 %arrange.1 = (f32[32,2,56,128]{3,2,1,0:T(8,128)}, f32[2,56,128]{2,1,0:T(8,128)}) custom-call(f32[1024,256]{1,0:T(8,128)} %bitcast.19, f32[512,256]{1,0:T(8,128)} %bitcast.23, f32[32,256]{1,0:T(8,128)} %friction.1, s32[32,256]{1,0:T(8,128)} %ice_mask.1, s32[32,256]{1,0:T(8,128)} %grounded.1), custom_call_target="tpu_custom_call" | custom-call | tf_op jit(solution)/shard_map/arrange/pallas_call | solution.py:549
  4.9 7.3 %all-gather = f32[8,56,128]{2,1,0:T(8,128)S(1)} all-gather(f32[2,56,128]{2,1,0:T(8,128)} %get-tuple-element.20), channel_id=2, replica_groups=mesh['gx'=8,'gy'=4] {'gy'}, dimensions={0}, use_global_device_ids=true | all-gather | bytes 286720 | tf_op jit(solution)/shard_map/all_gather | solution.py:544
  12.1 1.1 fusion.4
  13.3 0.0 copy-start.2
  13.3 3.5 %collective-permute-start = (f32[10,56,128]{2,1,0:T(8,128)S(1)}, f32[10,56,128]{2,1,0:T(8,128)S(1)}, u32[]{:S(2)}, u32[]{:S(2)}) collective-permute-start(f32[10,56,128]{2,1,0:T(8,128)S(1)} %get-tuple-element.43), channel_id=1, source_target_pairs={{0,4},{4,8},{8,12},{12,16},{16,20},{20,24},{24,28},{1,5},{5,9},{9,... | collective-permute-start | bytes 860168 | tf_op jit(solution)/shard_map/ppermute | solution.py:566
  16.8 1.3 collective-permute-start.1
  18.1 11.4 %collective-permute-done.from_low = f32[10,56,128]{2,1,0:T(8,128)S(1)} collective-permute-done((f32[10,56,128]{2,1,0:T(8,128)S(1)}, f32[10,56,128]{2,1,0:T(8,128)S(1)}, u32[]{:S(2)}, u32[]{:S(2)}) %collective-permute-start) | collective-permute-done | bytes 286752 | tf_op jit(solution)/shard_map/ppermute | solution.py:566
  29.5 0.0 copy-start.5
  29.5 0.0 collective-permute-done.1.from_high
  29.5 0.0 copy-done.2
  29.5 0.7 copy-done.5
  30.2 0.0 copy-start.6
  30.2 0.7 copy-done.6
  31.0 19.2 %down0.1 = (f32[16,56,128]{2,1,0:T(8,128)}, f32[2,2,56,128]{3,2,1,0:T(8,128)}, f32[40,3,32,128]{3,2,1,0:T(8,128)}, f32[40,3,120,128]{3,2,1,0:T(8,128)}, f32[40,3,32,128]{3,2,1,0:T(8,128)}) custom-call(f32[32,2,56,128]{3,2,1,0:T(8,128)} %get-tuple-element.19.own, f32[10,56,128]{2,1,0:T(8,128)} %copy-done.2, f32[10,56,128]{2,1,0:T(8,128)} %copy-done.5, ...), custom_call_target="tpu_custom_call" | custom-call | tf_op jit(solution)/shard_map/down0/pallas_call | solution.py:573
  50.2 7.1 %all-gather.1 = f32[8,2,56,128]{3,2,1,0:T(8,128)S(1)} all-gather(f32[2,2,56,128]{3,2,1,0:T(8,128)} %get-tuple-element.22), channel_id=3, replica_groups=mesh['gx'=8,'gy'=4] {'gy'}, dimensions={0}, use_global_device_ids=true | all-gather | bytes 573440 | tf_op jit(solution)/shard_map/all_gather | solution.py:544
  57.3 1.2 fusion.5
  58.4 0.1 pad_maximum_fusion
  58.5 0.0 copy-start.1
  58.5 4.4 %collective-permute-start.2 = (f32[17,56,128]{2,1,0:T(8,128)S(1)}, f32[17,56,128]{2,1,0:T(8,128)S(1)}, u32[]{:S(2)}, u32[]{:S(2)}) collective-permute-start(f32[17,56,128]{2,1,0:T(8,128)S(1)} %get-tuple-element.41), channel_id=1, source_target_pairs={{0,4},{4,8},{8,12},{12,16},{16,20},{20,24},{24,28},{1,5},{5,9},{9,... | collective-permute-start | bytes 1462280 | tf_op jit(solution)/shard_map/ppermute | solution.py:593
  63.0 1.3 collective-permute-start.3
  64.3 20.0 %collective-permute-done.2.from_low = f32[17,56,128]{2,1,0:T(8,128)S(1)} collective-permute-done((f32[17,56,128]{2,1,0:T(8,128)S(1)}, f32[17,56,128]{2,1,0:T(8,128)S(1)}, u32[]{:S(2)}, u32[]{:S(2)}) %collective-permute-start.2) | collective-permute-done | bytes 487456 | tf_op jit(solution)/shard_map/ppermute | solution.py:593
  84.3 0.0 collective-permute-done.3.from_high
  84.3 0.0 copy-done.1
  84.3 0.8 copy-done.3
  85.0 0.8 copy-done.4
  85.8 16.7 %down12.1 = (f32[56,128]{1,0:T(8,128)}, f32[42,2,32,128]{3,2,1,0:T(8,128)}, f32[42,2,120,128]{3,2,1,0:T(8,128)}, f32[42,2,32,128]{3,2,1,0:T(8,128)}, f32[20,1,32...) custom-call(f32[16,56,128]{2,1,0:T(8,128)} %get-tuple-element.21.own, ...), custom_call_target="tpu_custom_call" | custom-call | tf_op jit(solution)/shard_map/down12/pallas_call | solution.py:602
  102.6 1.7 broadcast_in_dim.17
  104.3 6.0 %all-to-all-start = ((f32[32,56,128]{2,1,0:T(8,128)}), f32[32,56,128]{2,1,0:T(8,128)S(1)}, u32[]{:S(2)}, u32[]{:S(2)}) async-start(f32[32,56,128]{2,1,0:T(8,128)} %broadcast_in_dim.17), calls=%async_computation | async-start | bytes 1835008 | tf_op jit(solution)/shard_map/all_to_all | solution.py:620
  110.3 0.6 pad_add_fusion.place
  110.9 22.8 %all-to-all-done = f32[32,56,128]{2,1,0:T(8,128)S(1)} async-done(((f32[32,56,128]{2,1,0:T(8,128)}), f32[32,56,128]{2,1,0:T(8,128)S(1)}, u32[]{:S(2)}, u32[]{:S(2)}) %all-to-all-start) | async-done | bytes 917536 | tf_op jit(solution)/shard_map/all_to_all | solution.py:620
  133.7 0.9 copy-done
  134.7 43.4 %up.1 = f32[1024,256]{1,0:T(8,128)} custom-call(s32[2]{0:T(128)} %pad_add_fusion.place, f32[8,4,56,128]{3,2,1,0:T(8,128)} %bitcast.18, f32[40,3,32,128]{3,2,1,0:T(8,128)} %get-tuple-element.24.w0_in, f32[40,3,120,128]{3,2,1,0:T(8,128)} %get-tuple-element.25.coef0_in, f32[40,3,32,128]{3,2,1,0:T(8,128)} %get-tuple-element.26.scaled0_in, ...), custom_call_target="tpu_custom_call" | custom-call | tf_op jit(solution)/shard_map/up/pallas_call | solution.py:626
  (6 shorter events, 0.1 us)
Async XLA Ops:
  13.3 16.3 %copy-start.2 = (f32[10,56,128]{2,1,0:T(8,128)}, f32[10,56,128]{2,1,0:T(8,128)S(1)}, u32[]{:S(2)}) copy-start(f32[10,56,128]{2,1,0:T(8,128)S(1)} %get-tuple-element.44.sent) | copy-start | bytes 860164
  13.3 16.2 %collective-permute-start = (f32[10,56,128]{2,1,0:T(8,128)S(1)}, f32[10,56,128]{2,1,0:T(8,128)S(1)}, u32[]{:S(2)}, u32[]{:S(2)}) collective-permute-start(f32[10,56,128]{2,1,0:T(8,128)S(1)} %get-tuple-element.43), channel_id=1, source_target_pairs={{0,4},{4,8},{8,12},{12,16},{16,20},{20,24},{24,28},{1,5},{5,9},{9,... | collective-permute-start | bytes 860168 | tf_op jit(solution)/shard_map/ppermute | solution.py:566
  16.8 12.7 %collective-permute-start.1 = (f32[10,56,128]{2,1,0:T(8,128)S(1)}, f32[10,56,128]{2,1,0:T(8,128)S(1)}, u32[]{:S(2)}, u32[]{:S(2)}) collective-permute-start(f32[10,56,128]{2,1,0:T(8,128)S(1)} %get-tuple-element.44.sent), channel_id=1, source_target_pairs={{4,0},{8,4},{12,8},{16,12},{20,16},{24,20},{28,24},{5,1},{9,5},{13... | collective-permute-start | bytes 860168 | tf_op jit(solution)/shard_map/ppermute | solution.py:567
  29.5 0.7 copy-start.5
  30.2 0.7 copy-start.6
  58.5 25.7 %copy-start.1 = (f32[17,56,128]{2,1,0:T(8,128)}, f32[17,56,128]{2,1,0:T(8,128)S(1)}, u32[]{:S(2)}) copy-start(f32[17,56,128]{2,1,0:T(8,128)S(1)} %get-tuple-element.42.sent) | copy-start | bytes 1462276
  58.5 25.7 %collective-permute-start.2 = (f32[17,56,128]{2,1,0:T(8,128)S(1)}, f32[17,56,128]{2,1,0:T(8,128)S(1)}, u32[]{:S(2)}, u32[]{:S(2)}) collective-permute-start(f32[17,56,128]{2,1,0:T(8,128)S(1)} %get-tuple-element.41), channel_id=1, source_target_pairs={{0,4},{4,8},{8,12},{12,16},{16,20},{20,24},{24,28},{1,5},{5,9},{9,... | collective-permute-start | bytes 1462280 | tf_op jit(solution)/shard_map/ppermute | solution.py:593
  63.0 21.3 %collective-permute-start.3 = (f32[17,56,128]{2,1,0:T(8,128)S(1)}, f32[17,56,128]{2,1,0:T(8,128)S(1)}, u32[]{:S(2)}, u32[]{:S(2)}) collective-permute-start(f32[17,56,128]{2,1,0:T(8,128)S(1)} %get-tuple-element.42.sent), channel_id=1, source_target_pairs={{4,0},{8,4},{12,8},{16,12},{20,16},{24,20},{28,24},{5,1},{9,5},{13... | collective-permute-start | bytes 1462280 | tf_op jit(solution)/shard_map/ppermute | solution.py:594
  84.3 0.8 copy-start.3
  85.0 0.8 copy-start.4
  104.3 29.4 %all-to-all-start = ((f32[32,56,128]{2,1,0:T(8,128)}), f32[32,56,128]{2,1,0:T(8,128)S(1)}, u32[]{:S(2)}, u32[]{:S(2)}) async-start(f32[32,56,128]{2,1,0:T(8,128)} %broadcast_in_dim.17), calls=%async_computation | async-start | bytes 1835008 | tf_op jit(solution)/shard_map/all_to_all | solution.py:620
  133.7 0.9 copy-start
where the time goes:
time: 179 us; the launch traced here: 178 us
  Pallas kernels  84.3 us (47%)
  waiting for transfers between devices  54.3 us (30%)
  starting transfers between devices  16.5 us (9%)
  blocking collectives  14.3 us (8%)
  local copies, waits for them, and re-layouts  7.87 us (4%)
    pallas_call x1, Pallas kernels, per_device(): pl.pallas_call(up_kernel, out_shape=shape(2 * 16 * rows, columns), in_spe...  43.4 us
    ppermute x2, waiting for transfers between devices, per_device(): from_low = lax.ppermute(high_face, 'gx', upward)  31.4 us
    all_to_all x1, waiting for transfers between devices, per_device(): lax.all_to_all(jnp.broadcast_to(piece, (nx * ny,) + piece.shape), ('gx',...  22.8 us
    pallas_call x1, Pallas kernels, per_device(): pl.pallas_call(down0_kernel, out_shape=(shape(rows1, NP, LANES), shape(2,...  19.2 us
    pallas_call x1, Pallas kernels, per_device(): pl.pallas_call(down12_kernel, out_shape=(shape(NP, LANES), field1, shape(...  16.7 us
    all_gather x2, blocking collectives, beside(): every = lax.all_gather(strips, 'gy', axis=0)  14.3 us
    ppermute x2, starting transfers between devices, per_device(): from_low = lax.ppermute(high_face, 'gx', upward)  7.93 us
    all_to_all x1, starting transfers between devices, per_device(): lax.all_to_all(jnp.broadcast_to(piece, (nx * ny,) + piece.shape), ('gx',...  6.01 us
  transfers between devices with their start and end apart: 5, of which 3 were waited for; matrix products, arithmetic and copies ran while one was open for 0% of the time, Pallas kernels for 0%

commit v1 on v0

--- a/solution.py
+++ b/solution.py
@@ -19,8 +19,14 @@
 RIM3 = 2
 STRIP1 = 16
 NC = 15
-VMEM_LIMIT = 60 * 1024 * 1024
+VMEM_DOWN = 20 * 1024 * 1024
+VMEM_UP = 39 * 1024 * 1024
 F32 = jnp.float32
+UNROLL0 = (18, 6, 4)
+UNROLL1 = (18, 6, 4)
+UNROLL2 = (18, 6, 4)
+UNROLL3 = (32, 32, 2)
+UNROLL_MOVE = 8
 
 
 def rows_loop(first, last, body, unroll):
@@ -144,8 +150,9 @@
 
 
 def sweep(w, new, coef, scaled, slope, across, first, last, closed, unroll, tiles=None, emit=None):
+    look, unroll, _ = unroll
     nt = w.shape[1]
-    prepare(w, coef, slope, across, first - 1, last + 1, closed, unroll)
+    prepare(w, coef, slope, across, first - 1, last + 1, closed, look)
 
     def row(r):
         for t in range(nt if tiles is None else tiles):
@@ -160,7 +167,8 @@
 
 
 def remainders(w, out, data, diag, coef, slope, across, first, last, unroll, tiles):
-    prepare(w, coef, slope, across, first - 1, last + 1, False, unroll)
+    look, unroll, _ = unroll
+    prepare(w, coef, slope, across, first - 1, last + 1, False, look)
 
     def row(r):
         for t in range(tiles):
@@ -261,8 +269,8 @@
             strips[side, planes, :] = strip
 
 
-def down0_kernel(own, sent, from_low, from_high, coarse, strips1, w_out, coef_out, scaled_out,
-                 data, coef, scaled, diag, wa, slope, across, sems):
+def down0_kernel(own, sent, from_low, from_high, coarse, strips1, wa, coef, scaled,
+                 data, diag, slope, across):
     rows = own.shape[0]
     total = rows + 2 * RIM0
 
@@ -281,24 +289,19 @@
         data[r, 2] = unpack_rim(from_low[2 * RIM0], from_low[2 * RIM0 + 1], low_at, RIM0)
         data[RIM0 + rows + r, 2] = unpack_rim(from_high[2 * RIM0], from_high[2 * RIM0 + 1], r * RIM0, RIM0)
 
-    make_coefs(data, coef, scaled, diag, 1, total - 1, 1.0, False, 1)
-    copies = [pltpu.make_async_copy(coef, coef_out, sems.at[0]), pltpu.make_async_copy(scaled, scaled_out, sems.at[1])]
-    for copy in copies:
-        copy.start()
-    sweep(scaled, wa, coef, scaled, slope, across, 2, total - 2, False, 1)
-    copies.append(pltpu.make_async_copy(wa, w_out, sems.at[2]))
-    copies[-1].start()
+    make_coefs(data, coef, scaled, diag, 1, total - 1, 1.0, False, UNROLL0[2])
+    sweep(scaled, wa, coef, scaled, slope, across, 2, total - 2, False, UNROLL0)
 
     def coefs_row(i):
         coarse[i, 32:56, :] = restrict_row(data, slice(32, 56), RIM0 + 2 * i)
 
-    rows_loop(0, rows // 2, coefs_row, 2)
-    remainders(wa, diag, data, diag, coef, slope, across, RIM0, RIM0 + rows, 1, 2)
+    rows_loop(0, rows // 2, coefs_row, UNROLL_MOVE)
+    remainders(wa, diag, data, diag, coef, slope, across, RIM0, RIM0 + rows, UNROLL0, 2)
 
     def target_row(i):
         coarse[i, 0:32, :] = restrict_row(diag, slice(0, 32), RIM0 + 2 * i)
 
-    rows_loop(0, rows // 2, target_row, 2)
+    rows_loop(0, rows // 2, target_row, UNROLL_MOVE)
     group = LANES // STRIP1
     for side in range(2):
         for part in range(rows // 2 // group):
@@ -310,13 +313,10 @@
                     shift = at if side == 0 else at + STRIP1
                     strip = put(strip, coarse[part * group + j, planes, :], shift, STRIP1, at)
                 strips1[side, part, planes, :] = strip
-    for copy in copies:
-        copy.wait()
-
-
-def down12_kernel(own, sent, from_low, from_high, piece, w1_out, coef1_out, scaled1_out, w2_out, coef2_out, scaled2_out,
-                  data1, coef1, scaled1, diag1, wa1, slope1, across1,
-                  data2, coef2, scaled2, diag2, wa2, slope2, across2, sems):
+
+
+def down12_kernel(own, sent, from_low, from_high, piece, wa1, coef1, scaled1, wa2, coef2, scaled2,
+                  data1, diag1, slope1, across1, data2, diag2, slope2, across2):
     rows = own.shape[0]
     total = rows + 2 * RIM1
     group = LANES // STRIP1
@@ -342,14 +342,9 @@
         data1[r, 1] = rim(from_low, RIM1, rows - RIM1 + r)
         data1[RIM1 + rows + r, 1] = rim(from_high, RIM1, r)
 
-    make_coefs(data1, coef1, scaled1, diag1, 1, total - 1, 0.25, False, 2)
-    copies = [pltpu.make_async_copy(coef1, coef1_out, sems.at[0]), pltpu.make_async_copy(scaled1, scaled1_out, sems.at[1])]
-    for copy in copies:
-        copy.start()
-    sweep(scaled1, wa1, coef1, scaled1, slope1, across1, 2, total - 2, False, 2)
-    copies.append(pltpu.make_async_copy(wa1, w1_out, sems.at[2]))
-    copies[-1].start()
-    remainders(wa1, diag1, data1, diag1, coef1, slope1, across1, 3, total - 3, 2, 2)
+    make_coefs(data1, coef1, scaled1, diag1, 1, total - 1, 0.25, False, UNROLL1[2])
+    sweep(scaled1, wa1, coef1, scaled1, slope1, across1, 2, total - 2, False, UNROLL1)
+    remainders(wa1, diag1, data1, diag1, coef1, slope1, across1, 3, total - 3, UNROLL1, 2)
 
     rows2 = rows // 2
     total2 = rows2 + 2 * RIM2
@@ -357,23 +352,16 @@
     def coefs_row(i):
         data2[i, 0, 32:56, :] = restrict_row(data1, slice(32, 56), 1 + 2 * i)
 
-    rows_loop(0, total2, coefs_row, 2)
+    rows_loop(0, total2, coefs_row, UNROLL_MOVE)
 
     def target_row(i):
         data2[i, 0, 0:32, :] = restrict_row(diag1, slice(0, 32), 1 + 2 * i)
 
-    rows_loop(1, total2 - 1, target_row, 2)
-
-    make_coefs(data2, coef2, scaled2, diag2, 1, total2 - 1, 0.0625, False, 2)
-    sweep(scaled2, wa2, coef2, scaled2, slope2, across2, 2, total2 - 2, False, 2)
-    late = [
-        pltpu.make_async_copy(coef2, coef2_out, sems.at[3]),
-        pltpu.make_async_copy(scaled2, scaled2_out, sems.at[4]),
-        pltpu.make_async_copy(wa2, w2_out, sems.at[5]),
-    ]
-    for copy in late:
-        copy.start()
-    remainders(wa2, diag2, data2, diag2, coef2, slope2, across2, RIM2, RIM2 + rows2, 2, 1)
+    rows_loop(1, total2 - 1, target_row, UNROLL_MOVE)
+
+    make_coefs(data2, coef2, scaled2, diag2, 1, total2 - 1, 0.0625, False, UNROLL2[2])
+    sweep(scaled2, wa2, coef2, scaled2, slope2, across2, 2, total2 - 2, False, UNROLL2)
+    remainders(wa2, diag2, data2, diag2, coef2, slope2, across2, RIM2, RIM2 + rows2, UNROLL2, 1)
 
     rows3 = rows2 // 2
     width = LANES // rows3
@@ -384,28 +372,13 @@
         for i in range(rows3):
             strip = put(strip, restrict_row(source, planes, RIM2 + 2 * i), i * width, width, i * width)
         piece[planes, :] = strip
-    for copy in copies + late:
-        copy.wait()
-
-
-def up_kernel(place, pieces, w0_in, coef0_in, scaled0_in, w1_in, coef1_in, scaled1_in, w2_in, coef2_in, scaled2_in, result,
+
+
+def up_kernel(place, pieces, w0, coef0, scaled0, w1, coef1, scaled1, w2, coef2, scaled2, result,
               data3, coef3, scaled3, wa3, wb3, slope3, across3,
-              wa2, wb2, coef2, scaled2, slope2, across2,
-              wa1, wb1, coef1, scaled1, slope1, across1,
-              wa0, wb0, coef0, scaled0, slope0, across0, result_half, sems):
-    copies = [
-        pltpu.make_async_copy(source, target, sems.at[n])
-        for n, (source, target) in enumerate(
-            (
-                (w2_in, wa2), (coef2_in, coef2), (scaled2_in, scaled2),
-                (w1_in, wa1), (coef1_in, coef1), (scaled1_in, scaled1),
-                (w0_in, wa0), (coef0_in, coef0), (scaled0_in, scaled0),
-            )
-        )
-    ]
-    for copy in copies:
-        copy.start()
-
+              wa2, wb2, wa1, wb1, wa0, wb0, slope0, across0, result_half, sems):
+    slope1, across1 = (v.at[pl.ds(0, wa1.shape[0]), pl.ds(0, 2)] for v in (slope0, across0))
+    slope2, across2 = (v.at[pl.ds(0, wa2.shape[0]), pl.ds(0, 1)] for v in (slope0, across0))
     devices_x, devices_y = pieces.shape[0], pieces.shape[1]
     rows3 = devices_y
     width = LANES // devices_y
@@ -430,7 +403,7 @@
 
     lax.fori_loop(0, devices_x, assemble, 0)
     first, last = RIM3, RIM3 + whole
-    make_coefs(data3, coef3, scaled3, None, first, last, 0.25 ** (LEVELS - 1), True, 2)
+    make_coefs(data3, coef3, scaled3, None, first, last, 0.25 ** (LEVELS - 1), True, UNROLL3[2])
 
     def coarse_sweep(source, target):
         def look(r):
@@ -438,13 +411,13 @@
             slope3[r, 0] = norths[0] - souths[0]
             across3[r, 0] = twice(coef3[r, 0, 16:32, :]) * norths[0] + twice(coef3[r, 0, 32:48, :]) * souths[0]
 
-        rows_loop(first, last, look, 4)
+        rows_loop(first, last, look, UNROLL3[0])
 
         def row(r):
             here, total = off_diagonal(source, coef3, slope3, across3, r, 0)
             target[r, 0] = (1.0 - OMEGA) * here + scaled3[r, 0] + coef3[r, 0, 88:120, :] * total
 
-        rows_loop(first, last, row, 4)
+        rows_loop(first, last, row, UNROLL3[1])
 
     coarse_sweep(scaled3, wa3)
 
@@ -462,45 +435,39 @@
     inside = (column >= 0) & (column < LANES)
     pick = jnp.where(inside, column, 0)
 
-    for copy in copies[:3]:
-        copy.wait()
     rows2 = 2 * rows3
     for i in range(rows2 // 2 + 2 * RIM3):
         line = wa3[gx * rows3 + i, 0]
         add = jnp.where(inside, gather_lanes(line, pick), 0.0)
         for r in (2 * i + 2, 2 * i + 3):
-            wa2[r, 0] = wa2[r, 0] + add
+            wa2[r, 0] = w2[r, 0] + add
     total2 = rows2 + 2 * RIM2
-    sweep(wa2, wb2, coef2, scaled2, slope2, across2, 3, total2 - 3, False, 2)
-    sweep(wb2, wa2, coef2, scaled2, slope2, across2, 4, total2 - 4, False, 2)
-
-    for copy in copies[3:6]:
-        copy.wait()
+    sweep(wa2, wb2, coef2, scaled2, slope2, across2, 3, total2 - 3, False, UNROLL2)
+    sweep(wb2, wa2, coef2, scaled2, slope2, across2, 4, total2 - 4, False, UNROLL2)
+
 
     def add1(r):
         adds = prolong_row([wa2[r, 0]], 2)
         for t in range(2):
             for fine in (2 * r + 1, 2 * r + 2):
-                wa1[fine, t] = wa1[fine, t] + adds[t]
-
-    rows_loop(4, total2 - 4, add1, 2)
+                wa1[fine, t] = w1[fine, t] + adds[t]
+
+    rows_loop(4, total2 - 4, add1, UNROLL_MOVE)
     total1 = 2 * rows2 + 2 * RIM1
-    sweep(wa1, wb1, coef1, scaled1, slope1, across1, 11, total1 - 11, False, 2)
-    sweep(wb1, wa1, coef1, scaled1, slope1, across1, 12, total1 - 12, False, 2)
-
-    for copy in copies[6:]:
-        copy.wait()
+    sweep(wa1, wb1, coef1, scaled1, slope1, across1, 11, total1 - 11, False, UNROLL1)
+    sweep(wb1, wa1, coef1, scaled1, slope1, across1, 12, total1 - 12, False, UNROLL1)
+
 
     def add0(r):
         adds = prolong_row([wa1[r, t] for t in range(2)], 3)
         for t in range(3):
             for fine in (2 * r - 22, 2 * r - 21):
-                wa0[fine, t] = wa0[fine, t] + adds[t]
-
-    rows_loop(12, total1 - 12, add0, 2)
+                wa0[fine, t] = w0[fine, t] + adds[t]
+
+    rows_loop(12, total1 - 12, add0, UNROLL_MOVE)
     rows0 = 4 * rows2
     total0 = rows0 + 2 * RIM0
-    sweep(wa0, wb0, coef0, scaled0, slope0, across0, 3, total0 - 3, False, 1)
+    sweep(wa0, wb0, coef0, scaled0, slope0, across0, 3, total0 - 3, False, UNROLL0)
 
     def emit(r, t, value):
         for c in range(2):
@@ -508,7 +475,7 @@
                 start = c * 16 * rows0 + p * rows0 + r - RIM0
                 result_half[t, pl.ds(start, 8, stride=2 * rows0), :] = value[16 * c + 8 * p : 16 * c + 8 * p + 8]
 
-    sweep(wb0, None, coef0, scaled0, slope0, across0, RIM0, RIM0 + rows0, False, 1, tiles=2, emit=emit)
+    sweep(wb0, None, coef0, scaled0, slope0, across0, RIM0, RIM0 + rows0, False, UNROLL0, tiles=2, emit=emit)
     copies = [
         pltpu.make_async_copy(result_half.at[t], result.at[:, pl.ds(t * LANES, LANES)], sems.at[t]) for t in range(2)
     ]
@@ -522,10 +489,19 @@
     return jax.ShapeDtypeStruct(dims, F32)
 
 
+def kept(*dims):
+    return pltpu.VMEM(dims, F32)
+
+
+def keep(arrays):
+    return [pltpu.with_memory_space_constraint(v, pltpu.VMEM) for v in arrays]
+
+
 VM = pl.BlockSpec(memory_space=pltpu.VMEM)
 SM = pl.BlockSpec(memory_space=pltpu.SMEM)
 HB = pl.BlockSpec(memory_space=pl.ANY)
-PARAMS = pltpu.CompilerParams(vmem_limit_bytes=VMEM_LIMIT)
+PARAMS = pltpu.CompilerParams(vmem_limit_bytes=VMEM_DOWN)
+UP_PARAMS = pltpu.CompilerParams(vmem_limit_bytes=VMEM_UP)
 
 
 def buffers(rows, tiles, names):
@@ -558,7 +534,12 @@
         ],
         compiler_params=PARAMS,
         name="arrange",
-    )(misfit.reshape(-1, columns), viscosity.reshape(-1, columns), friction, ice_mask, grounded)
+    )(
+        *(pltpu.with_memory_space_constraint(v.reshape(-1, columns), pltpu.HBM) for v in (misfit, viscosity)),
+        friction,
+        ice_mask,
+        grounded,
+    )
     left, right = beside(strips0)
     rims = [left[None], right[None]]
     low_face = jnp.concatenate([data0[:RIM0].reshape(-1, NP, LANES)] + rims, 0)
@@ -567,22 +548,22 @@
     from_high = lax.ppermute(low_face, "gx", downward)
 
     total0 = rows + 2 * RIM0
+    names = ("data", "diag", "slope", "across")
     rows1 = rows // 2
     group = LANES // STRIP1
-    field0 = shape(total0, 3, 32, LANES)
+    field0 = kept(total0, 3, 32, LANES)
     data1, strips1, w0, coef0, scaled0 = pl.pallas_call(
         down0_kernel,
         out_shape=(
             shape(rows1, NP, LANES),
             shape(2, rows1 // group, NP, LANES),
             field0,
-            shape(total0, 3, 8 * NC, LANES),
+            kept(total0, 3, 8 * NC, LANES),
             field0,
         ),
         in_specs=[VM] * 4,
-        out_specs=(VM, VM, HB, HB, HB),
-        scratch_shapes=buffers(total0, 3, ("data", "coef", "scaled", "diag", "w", "slope", "across"))
-        + [pltpu.SemaphoreType.DMA((3,))],
+        out_specs=(VM,) * 5,
+        scratch_shapes=buffers(total0, 3, names),
         compiler_params=PARAMS,
         name="down0",
     )(data0, low_face, from_low, from_high)
@@ -596,23 +577,22 @@
     total1 = rows1 + 2 * RIM1
     rows2 = rows1 // 2
     total2 = rows2 + 2 * RIM2
-    field1 = shape(total1, 2, 32, LANES)
-    field2 = shape(total2, 1, 32, LANES)
-    names = ("data", "coef", "scaled", "diag", "w", "slope", "across")
+    field1 = kept(total1, 2, 32, LANES)
+    field2 = kept(total2, 1, 32, LANES)
     piece, w1, coef1, scaled1, w2, coef2, scaled2 = pl.pallas_call(
         down12_kernel,
         out_shape=(
             shape(NP, LANES),
             field1,
-            shape(total1, 2, 8 * NC, LANES),
+            kept(total1, 2, 8 * NC, LANES),
             field1,
             field2,
-            shape(total2, 1, 8 * NC, LANES),
+            kept(total2, 1, 8 * NC, LANES),
             field2,
         ),
         in_specs=[VM] * 4,
-        out_specs=(VM,) + (HB,) * 6,
-        scratch_shapes=buffers(total1, 2, names) + buffers(total2, 1, names) + [pltpu.SemaphoreType.DMA((6,))],
+        out_specs=(VM,) * 7,
+        scratch_shapes=buffers(total1, 2, names) + buffers(total2, 1, names),
         compiler_params=PARAMS,
         name="down12",
     )(data1, low_face, from_low, from_high)
@@ -622,20 +602,25 @@
 
     rows3 = rows2 // 2
     total3 = nx * rows3 + 2 * RIM3
-    ups = ("w", "w", "coef", "scaled", "slope", "across")
+    ups = ("w", "w")
     result = pl.pallas_call(
         up_kernel,
         out_shape=shape(2 * 16 * rows, columns),
-        in_specs=[SM, VM] + [HB] * 9,
+        in_specs=[SM] + [VM] * 10,
         out_specs=HB,
         scratch_shapes=buffers(total3, 1, ("data", "coef", "scaled", "w", "w", "slope", "across"))
         + buffers(total2, 1, ups)
         + buffers(total1, 2, ups)
         + buffers(total0, 3, ups)
-        + [pltpu.VMEM((2, 2 * 16 * rows, LANES), F32), pltpu.SemaphoreType.DMA((9,))],
-        compiler_params=PARAMS,
+        + buffers(max(total0, total1), 3, ("slope", "across"))
+        + [pltpu.VMEM((2, 2 * 16 * rows, LANES), F32), pltpu.SemaphoreType.DMA((2,))],
+        compiler_params=UP_PARAMS,
         name="up",
-    )(jnp.stack([gx, gy]).astype(jnp.int32), pieces, w0, coef0, scaled0, w1, coef1, scaled1, w2, coef2, scaled2)
+    )(
+        jnp.stack([gx, gy]).astype(jnp.int32),
+        pieces,
+        *keep([w0, coef0, scaled0, w1, coef1, scaled1, w2, coef2, scaled2]),
+    )
     return result.reshape(misfit.shape)
 
 

time: 179 us -> 151 us (0.84)
  Pallas kernels: 84.3 us -> 39.1 us
  local copies, waits for them, and re-layouts: 7.87 us -> 23.8 us
  starting transfers between devices: 16.5 us -> 18.3 us
    pallas_call x1, Pallas kernels: 43.4 us -> 20.1 us  [per_device(): pl.pallas_call(up_kernel, out_shape=shape(2 * 16 * rows, columns), in_spe...]
    unnamed x14 -> x38, local copies, waits for them, and re-layouts: 3.91 us -> 22.7 us
    pallas_call x1, Pallas kernels: 19.2 us -> 7.84 us  [per_device(): pl.pallas_call(down0_kernel, out_shape=(shape(rows1, NP, LANES), shape(2,...]
    pallas_call x1, Pallas kernels: 16.7 us -> 8.23 us  [per_device(): pl.pallas_call(down12_kernel, out_shape=(shape(NP, LANES), field1, kept(t...]
    pallas_call x1, Pallas kernels: 4.87 us -> 2.89 us  [per_device(): pl.pallas_call(arrange_kernel, out_shape=(shape(rows, 2, NP, LANES), shap...]
where the time goes in v1:
time: 151 us; the launch traced here: 150 us
  waiting for transfers between devices  54 us (36%)
  Pallas kernels  39.1 us (26%)
  local copies, waits for them, and re-layouts  23.8 us (16%)
  starting transfers between devices  18.3 us (12%)
  blocking collectives  13.9 us (9%)
    ppermute x2, waiting for transfers between devices, per_device(): from_low = lax.ppermute(high_face, 'gx', upward)  31.4 us
    unnamed x38, local copies, waits for them, and re-layouts  22.7 us
    all_to_all x1, waiting for transfers between devices, per_device(): lax.all_to_all(jnp.broadcast_to(piece, (nx * ny,) + piece.shape), ('gx',...  22.6 us
    pallas_call x1, Pallas kernels, per_device(): pl.pallas_call(up_kernel, out_shape=shape(2 * 16 * rows, columns), in_spe...  20.1 us
    all_gather x2, blocking collectives, beside(): every = lax.all_gather(strips, 'gy', axis=0)  13.9 us
    pallas_call x1, Pallas kernels, per_device(): pl.pallas_call(down12_kernel, out_shape=(shape(NP, LANES), field1, kept(t...  8.23 us
    ppermute x2, starting transfers between devices, per_device(): from_low = lax.ppermute(high_face, 'gx', upward)  7.93 us
    pallas_call x1, Pallas kernels, per_device(): pl.pallas_call(down0_kernel, out_shape=(shape(rows1, NP, LANES), shape(2,...  7.84 us
  transfers between devices with their start and end apart: 5, of which 3 were waited for; matrix products, arithmetic and copies ran while one was open for 0% of the time, Pallas kernels for 0%

profile of v1, /device:TPU:0, one launch (start us, length us, event | category | flops | bytes accessed | tf_op | source)
XLA Modules:
  0.0 150.2 jit_solution(4995171875852024119)
XLA Ops:
  0.0 0.8 copy-done.16
  0.8 0.8 copy-done.17
  1.5 0.8 copy-done.18
  2.3 2.9 %arrange.1 = (f32[32,2,56,128]{3,2,1,0:T(8,128)S(1)}, f32[2,56,128]{2,1,0:T(8,128)S(1)}) custom-call(f32[1024,256]{1,0:T(8,128)} %bitcast.18, f32[512,256]{1,0:T(8,128)} %bitcast.22, f32[32,256]{1,0:T(8,128)S(1)} %copy-done.16, s32[32,256]{1,0:T(8,128)S(1)} %copy-done.17, s32[32,256]{1,0:T(8,128)S(1)} %copy-done.18), custom_call_target="tpu_custom_call" | custom-call | tf_op jit(solution)/shard_map/arrange/pallas_call | solution.py:525
  5.2 7.0 %all-gather = f32[8,56,128]{2,1,0:T(8,128)S(1)} all-gather(f32[2,56,128]{2,1,0:T(8,128)S(1)} %get-tuple-element.20), channel_id=2, replica_groups=mesh['gx'=8,'gy'=4] {'gy'}, dimensions={0}, use_global_device_ids=true | all-gather | bytes 286720 | tf_op jit(solution)/shard_map/all_gather | solution.py:520
  12.3 3.5 %collective-permute-start = (f32[10,56,128]{2,1,0:T(8,128)S(1)}, f32[10,56,128]{2,1,0:T(8,128)S(1)}, u32[]{:S(2)}, u32[]{:S(2)}) collective-permute-start(f32[10,56,128]{2,1,0:T(8,128)S(1)} %get-tuple-element.43), channel_id=1, source_target_pairs={{0,4},{4,8},{8,12},{12,16},{16,20},{20,24},{24,28},{1,5},{5,9},{9,... | collective-permute-start | bytes 860168 | tf_op jit(solution)/shard_map/ppermute | solution.py:547
  15.8 1.3 collective-permute-start.1
  17.1 11.4 %collective-permute-done.from_low = f32[10,56,128]{2,1,0:T(8,128)S(1)} collective-permute-done((f32[10,56,128]{2,1,0:T(8,128)S(1)}, f32[10,56,128]{2,1,0:T(8,128)S(1)}, u32[]{:S(2)}, u32[]{:S(2)}) %collective-permute-start) | collective-permute-done | bytes 286752 | tf_op jit(solution)/shard_map/ppermute | solution.py:547
  28.6 7.8 %down0.1 = (f32[16,56,128]{2,1,0:T(8,128)S(1)}, f32[2,2,56,128]{3,2,1,0:T(8,128)S(1)}, f32[40,3,32,128]{3,2,1,0:T(8,128)S(1)}, f32[40,3,120,128]{3,2,1,0:T(8,128)S(1)}, f32[40,3,32,128]{3,2,1,0:T(8,128)S(1)}) custom-call(f32[32,2,56,128]{3,2,1,0:T(8,128)S(1)} %get-tuple-element.19.own, f32[10,56,128]{2,1,0:T(8,128)S(1)} %get-tuple-element.44.sent, ...), custom_call_target="tpu_custom_call" | custom-call | tf_op jit(solution)/shard_map/down0/pallas_call | solution.py:555
  36.4 2.9 %copy-done = f32[40,3,120,128]{3,2,1,0:T(8,128)} copy-done((f32[40,3,120,128]{3,2,1,0:T(8,128)}, f32[40,3,120,128]{3,2,1,0:T(8,128)S(1)}, u32[]{:S(2)}) %copy-start) | copy-done | bytes 7372824
  39.3 6.8 %all-gather.1 = f32[8,2,56,128]{3,2,1,0:T(8,128)S(1)} all-gather(f32[2,2,56,128]{3,2,1,0:T(8,128)S(1)} %get-tuple-element.22), channel_id=3, replica_groups=mesh['gx'=8,'gy'=4] {'gy'}, dimensions={0}, use_global_device_ids=true | all-gather | bytes 573440 | tf_op jit(solution)/shard_map/all_gather | solution.py:520
  46.4 4.4 %collective-permute-start.2 = (f32[17,56,128]{2,1,0:T(8,128)S(1)}, f32[17,56,128]{2,1,0:T(8,128)S(1)}, u32[]{:S(2)}, u32[]{:S(2)}) collective-permute-start(f32[17,56,128]{2,1,0:T(8,128)S(1)} %get-tuple-element.41), channel_id=1, source_target_pairs={{0,4},{4,8},{8,12},{12,16},{16,20},{20,24},{24,28},{1,5},{5,9},{9,... | collective-permute-start | bytes 1462280 | tf_op jit(solution)/shard_map/ppermute | solution.py:574
  50.8 1.3 collective-permute-start.3
  52.1 20.0 %collective-permute-done.2.from_low = f32[17,56,128]{2,1,0:T(8,128)S(1)} collective-permute-done((f32[17,56,128]{2,1,0:T(8,128)S(1)}, f32[17,56,128]{2,1,0:T(8,128)S(1)}, u32[]{:S(2)}, u32[]{:S(2)}) %collective-permute-start.2) | collective-permute-done | bytes 487456 | tf_op jit(solution)/shard_map/ppermute | solution.py:574
  72.1 8.2 %down12.1 = (f32[56,128]{1,0:T(8,128)S(1)}, f32[42,2,32,128]{3,2,1,0:T(8,128)S(1)}, f32[42,2,120,128]{3,2,1,0:T(8,128)S(1)}, f32[42,2,32,128]{3,2,1,0:T(8,128)S(...) custom-call(f32[16,56,128]{2,1,0:T(8,128)S(1)} %get-tuple-element.21.own, ...), custom_call_target="tpu_custom_call" | custom-call | tf_op jit(solution)/shard_map/down12/pallas_call | solution.py:582
  80.3 2.3 %copy-done.2 = f32[42,2,120,128]{3,2,1,0:T(8,128)} copy-done((f32[42,2,120,128]{3,2,1,0:T(8,128)}, f32[42,2,120,128]{3,2,1,0:T(8,128)S(1)}, u32[]{:S(2)}) %copy-start.2) | copy-done | bytes 5160984
  82.6 1.1 copy-done.8
  83.7 1.0 copy-done.10
  84.8 0.7 copy-done.12
  85.5 0.7 copy-done.14
  86.2 1.0 broadcast_in_dim.17
  87.2 7.8 %all-to-all-start = ((f32[32,56,128]{2,1,0:T(8,128)}), f32[32,56,128]{2,1,0:T(8,128)}, u32[]{:S(2)}, u32[]{:S(2)}) async-start(f32[32,56,128]{2,1,0:T(8,128)} %broadcast_in_dim.17), calls=%async_computation | async-start | bytes 1835008 | tf_op jit(solution)/shard_map/all_to_all | solution.py:600
  95.0 0.6 pad_add_fusion.place
  95.6 22.6 %all-to-all-done = f32[32,56,128]{2,1,0:T(8,128)} async-done(((f32[32,56,128]{2,1,0:T(8,128)}), f32[32,56,128]{2,1,0:T(8,128)}, u32[]{:S(2)}, u32[]{:S(2)}) %all-to-all-start) | async-done | bytes 917536 | tf_op jit(solution)/shard_map/all_to_all | solution.py:600
  118.2 3.1 %copy-done.1 = f32[40,3,120,128]{3,2,1,0:T(8,128)S(1)} copy-done((f32[40,3,120,128]{3,2,1,0:T(8,128)S(1)}, f32[40,3,120,128]{3,2,1,0:T(8,128)}, u32[]{:S(2)}) %copy-start.1) | copy-done | bytes 7372824
  121.3 2.5 %copy-done.3 = f32[42,2,120,128]{3,2,1,0:T(8,128)S(1)} copy-done((f32[42,2,120,128]{3,2,1,0:T(8,128)S(1)}, f32[42,2,120,128]{3,2,1,0:T(8,128)}, u32[]{:S(2)}) %copy-start.3) | copy-done | bytes 5160984
  123.8 1.5 %copy-done.7 = f32[40,3,32,128]{3,2,1,0:T(8,128)S(1)} copy-done((f32[40,3,32,128]{3,2,1,0:T(8,128)S(1)}, f32[40,3,32,128]{3,2,1,0:T(8,128)}, u32[]{:S(2)}) %copy-start.7) | copy-done | bytes 1966104
  125.3 1.3 copy-done.9
  126.7 1.3 copy-done.11
  127.9 1.0 copy-done.13
  128.9 1.0 copy-done.15
  129.9 20.1 %up.1 = f32[1024,256]{1,0:T(8,128)} custom-call(s32[2]{0:T(128)} %pad_add_fusion.place, f32[8,4,56,128]{3,2,1,0:T(8,128)} %bitcast.12.pieces, f32[40,3,32,128]{3,2,1,0:T(8,128)S(1)} %copy-done.5, f32[40,3,120,128]{3,2,1,0:T(8,128)S(1)} %copy-done.1, f32[40,3,32,128]{3,2,1,0:T(8,128)S(1)} %copy-done.7, f32[42,2,32,128]{3,2,1,0:T(8,128)S(1)} %get-tuple-element.27.w1, ...), custom_call_target="tpu_custom_call" | custom-call | tf_op jit(solution)/shard_map/up/pallas_call | solution.py:606
  (30 shorter events, 0.3 us)
Async XLA Ops:
  0.0 0.8 copy-start.16
  0.8 0.8 copy-start.17
  1.5 0.8 copy-start.18
  12.3 16.2 %collective-permute-start = (f32[10,56,128]{2,1,0:T(8,128)S(1)}, f32[10,56,128]{2,1,0:T(8,128)S(1)}, u32[]{:S(2)}, u32[]{:S(2)}) collective-permute-start(f32[10,56,128]{2,1,0:T(8,128)S(1)} %get-tuple-element.43), channel_id=1, source_target_pairs={{0,4},{4,8},{8,12},{12,16},{16,20},{20,24},{24,28},{1,5},{5,9},{9,... | collective-permute-start | bytes 860168 | tf_op jit(solution)/shard_map/ppermute | solution.py:547
  15.8 12.7 %collective-permute-start.1 = (f32[10,56,128]{2,1,0:T(8,128)S(1)}, f32[10,56,128]{2,1,0:T(8,128)S(1)}, u32[]{:S(2)}, u32[]{:S(2)}) collective-permute-start(f32[10,56,128]{2,1,0:T(8,128)S(1)} %get-tuple-element.44.sent), channel_id=1, source_target_pairs={{4,0},{8,4},{12,8},{16,12},{20,16},{24,20},{28,24},{5,1},{9,5},{13... | collective-permute-start | bytes 860168 | tf_op jit(solution)/shard_map/ppermute | solution.py:548
  36.4 2.9 %copy-start = (f32[40,3,120,128]{3,2,1,0:T(8,128)}, f32[40,3,120,128]{3,2,1,0:T(8,128)S(1)}, u32[]{:S(2)}) copy-start(f32[40,3,120,128]{3,2,1,0:T(8,128)S(1)} %get-tuple-element.25.coef0) | copy-start | bytes 22118404
  39.3 7.0 %copy-start.4 = (f32[40,3,32,128]{3,2,1,0:T(8,128)}, f32[40,3,32,128]{3,2,1,0:T(8,128)S(1)}, u32[]{:S(2)}) copy-start(f32[40,3,32,128]{3,2,1,0:T(8,128)S(1)} %get-tuple-element.24.w0) | copy-start | bytes 5898244
  39.3 7.0 %copy-start.6 = (f32[40,3,32,128]{3,2,1,0:T(8,128)}, f32[40,3,32,128]{3,2,1,0:T(8,128)S(1)}, u32[]{:S(2)}) copy-start(f32[40,3,32,128]{3,2,1,0:T(8,128)S(1)} %get-tuple-element.26.scaled0) | copy-start | bytes 5898244
  46.4 25.7 %collective-permute-start.2 = (f32[17,56,128]{2,1,0:T(8,128)S(1)}, f32[17,56,128]{2,1,0:T(8,128)S(1)}, u32[]{:S(2)}, u32[]{:S(2)}) collective-permute-start(f32[17,56,128]{2,1,0:T(8,128)S(1)} %get-tuple-element.41), channel_id=1, source_target_pairs={{0,4},{4,8},{8,12},{12,16},{16,20},{20,24},{24,28},{1,5},{5,9},{9,... | collective-permute-start | bytes 1462280 | tf_op jit(solution)/shard_map/ppermute | solution.py:574
  50.8 21.3 %collective-permute-start.3 = (f32[17,56,128]{2,1,0:T(8,128)S(1)}, f32[17,56,128]{2,1,0:T(8,128)S(1)}, u32[]{:S(2)}, u32[]{:S(2)}) collective-permute-start(f32[17,56,128]{2,1,0:T(8,128)S(1)} %get-tuple-element.42.sent), channel_id=1, source_target_pairs={{4,0},{8,4},{12,8},{16,12},{20,16},{24,20},{28,24},{5,1},{9,5},{13... | collective-permute-start | bytes 1462280 | tf_op jit(solution)/shard_map/ppermute | solution.py:575
  80.3 2.3 %copy-start.2 = (f32[42,2,120,128]{3,2,1,0:T(8,128)}, f32[42,2,120,128]{3,2,1,0:T(8,128)S(1)}, u32[]{:S(2)}) copy-start(f32[42,2,120,128]{3,2,1,0:T(8,128)S(1)} %get-tuple-element.28.coef1) | copy-start | bytes 15482884
  82.6 1.1 copy-start.8
  83.7 1.0 copy-start.10
  84.8 0.7 copy-start.12
  85.5 0.7 copy-start.14
  86.2 32.0 %copy-start.5 = (f32[40,3,32,128]{3,2,1,0:T(8,128)S(1)}, f32[40,3,32,128]{3,2,1,0:T(8,128)}, u32[]{:S(2)}) copy-start(f32[40,3,32,128]{3,2,1,0:T(8,128)} %copy-done.4) | copy-start | bytes 5898244
  87.2 31.0 %all-to-all-start = ((f32[32,56,128]{2,1,0:T(8,128)}), f32[32,56,128]{2,1,0:T(8,128)}, u32[]{:S(2)}, u32[]{:S(2)}) async-start(f32[32,56,128]{2,1,0:T(8,128)} %broadcast_in_dim.17), calls=%async_computation | async-start | bytes 1835008 | tf_op jit(solution)/shard_map/all_to_all | solution.py:600
  118.2 3.1 %copy-start.1 = (f32[40,3,120,128]{3,2,1,0:T(8,128)S(1)}, f32[40,3,120,128]{3,2,1,0:T(8,128)}, u32[]{:S(2)}) copy-start(f32[40,3,120,128]{3,2,1,0:T(8,128)} %copy-done) | copy-start | bytes 22118404
  121.3 2.5 %copy-start.3 = (f32[42,2,120,128]{3,2,1,0:T(8,128)S(1)}, f32[42,2,120,128]{3,2,1,0:T(8,128)}, u32[]{:S(2)}) copy-start(f32[42,2,120,128]{3,2,1,0:T(8,128)} %copy-done.2) | copy-start | bytes 15482884
  123.8 1.5 %copy-start.7 = (f32[40,3,32,128]{3,2,1,0:T(8,128)S(1)}, f32[40,3,32,128]{3,2,1,0:T(8,128)}, u32[]{:S(2)}) copy-start(f32[40,3,32,128]{3,2,1,0:T(8,128)} %copy-done.6) | copy-start | bytes 5898244
  125.3 1.3 copy-start.9
  126.6 1.3 copy-start.11
  127.9 1.0 copy-start.13
  128.9 1.0 copy-start.15

commit v2 on v1

--- a/solution.py
+++ b/solution.py
@@ -19,8 +19,10 @@
 RIM3 = 2
 STRIP1 = 16
 NC = 15
-VMEM_DOWN = 20 * 1024 * 1024
-VMEM_UP = 39 * 1024 * 1024
+VMEM_DOWN = 14 * 1024 * 1024
+VMEM_UP = 17 * 1024 * 1024
+VMEM_COARSE = 3 * 1024 * 1024
+VMEM_COARSE_ROW = 200 * 1024
 F32 = jnp.float32
 UNROLL0 = (18, 6, 4)
 UNROLL1 = (18, 6, 4)
@@ -226,9 +228,13 @@
     return jnp.where(lane < LANES // 2, to_low, to_high)
 
 
-def arrange_kernel(misfit, viscosity, friction, ice_mask, grounded, data, strips, misfit_half, viscosity_half, sems):
+def arrange_kernel(misfit, viscosity, friction_in, ice_mask_in, grounded_in, data, strips,
+                   misfit_half, viscosity_half, friction, ice_mask, grounded, sems):
     rows = friction.shape[0]
-    copies = []
+    copies = [
+        pltpu.make_async_copy(source, target, sems.at[4 + n])
+        for n, (source, target) in enumerate(((friction_in, friction), (ice_mask_in, ice_mask), (grounded_in, grounded)))
+    ]
     for t in range(2):
         lanes = pl.ds(t * LANES, LANES)
         copies.append(pltpu.make_async_copy(misfit.at[:, lanes], misfit_half.at[t], sems.at[t]))
@@ -371,15 +377,12 @@
         strip = jnp.zeros((8, LANES), F32)
         for i in range(rows3):
             strip = put(strip, restrict_row(source, planes, RIM2 + 2 * i), i * width, width, i * width)
-        piece[planes, :] = strip
-
-
-def up_kernel(place, pieces, w0, coef0, scaled0, w1, coef1, scaled1, w2, coef2, scaled2, result,
-              data3, coef3, scaled3, wa3, wb3, slope3, across3,
-              wa2, wb2, wa1, wb1, wa0, wb0, slope0, across0, result_half, sems):
-    slope1, across1 = (v.at[pl.ds(0, wa1.shape[0]), pl.ds(0, 2)] for v in (slope0, across0))
-    slope2, across2 = (v.at[pl.ds(0, wa2.shape[0]), pl.ds(0, 1)] for v in (slope0, across0))
-    devices_x, devices_y = pieces.shape[0], pieces.shape[1]
+        for d in range(piece.shape[0]):
+            piece[d, planes, :] = strip
+
+
+def coarse_kernel(place, pieces, correction, data3, coef3, scaled3, wa3, wb3, slope3, across3):
+    devices_y, devices_x = pieces.shape[0], pieces.shape[1]
     rows3 = devices_y
     width = LANES // devices_y
     whole = devices_x * rows3
@@ -397,7 +400,7 @@
         for i in range(rows3):
             line = jnp.zeros((NP, LANES), F32)
             for j in range(devices_y):
-                line = put(line, pieces[d, j], (j - i) * width, width, j * width)
+                line = put(line, pieces[j, d], (j - i) * width, width, j * width)
             data3[RIM3 + d * rows3 + i, 0] = line
         return carry
 
@@ -435,12 +438,19 @@
     inside = (column >= 0) & (column < LANES)
     pick = jnp.where(inside, column, 0)
 
-    rows2 = 2 * rows3
-    for i in range(rows2 // 2 + 2 * RIM3):
+    for i in range(rows3 + 2 * RIM3):
         line = wa3[gx * rows3 + i, 0]
-        add = jnp.where(inside, gather_lanes(line, pick), 0.0)
+        correction[i] = jnp.where(inside, gather_lanes(line, pick), 0.0)
+
+
+def up_kernel(correction, w0, coef0, scaled0, w1, coef1, scaled1, w2, coef2, scaled2, result,
+              wa2, wb2, wa1, wb1, wa0, wb0, slope0, across0, result_half, sems):
+    slope1, across1 = (v.at[pl.ds(0, wa1.shape[0]), pl.ds(0, 2)] for v in (slope0, across0))
+    slope2, across2 = (v.at[pl.ds(0, wa2.shape[0]), pl.ds(0, 1)] for v in (slope0, across0))
+    rows2 = w2.shape[0] - 2 * RIM2
+    for i in range(correction.shape[0]):
         for r in (2 * i + 2, 2 * i + 3):
-            wa2[r, 0] = w2[r, 0] + add
+            wa2[r, 0] = w2[r, 0] + correction[i]
     total2 = rows2 + 2 * RIM2
     sweep(wa2, wb2, coef2, scaled2, slope2, across2, 3, total2 - 3, False, UNROLL2)
     sweep(wb2, wa2, coef2, scaled2, slope2, across2, 4, total2 - 4, False, UNROLL2)
@@ -525,20 +535,23 @@
     data0, strips0 = pl.pallas_call(
         arrange_kernel,
         out_shape=(shape(rows, 2, NP, LANES), shape(2, NP, LANES)),
-        in_specs=[HB, HB, VM, VM, VM],
+        in_specs=[HB] * 5,
         out_specs=(VM, VM),
         scratch_shapes=[
             pltpu.VMEM((2, 2 * 16 * rows, LANES), F32),
             pltpu.VMEM((2, 16 * rows, LANES), F32),
-            pltpu.SemaphoreType.DMA((4,)),
+            pltpu.VMEM((rows, columns), F32),
+            pltpu.VMEM((rows, columns), jnp.int32),
+            pltpu.VMEM((rows, columns), jnp.int32),
+            pltpu.SemaphoreType.DMA((7,)),
         ],
         compiler_params=PARAMS,
         name="arrange",
     )(
-        *(pltpu.with_memory_space_constraint(v.reshape(-1, columns), pltpu.HBM) for v in (misfit, viscosity)),
-        friction,
-        ice_mask,
-        grounded,
+        *(
+            pltpu.with_memory_space_constraint(v.reshape(-1, columns), pltpu.HBM)
+            for v in (misfit, viscosity, friction, ice_mask, grounded)
+        )
     )
     left, right = beside(strips0)
     rims = [left[None], right[None]]
@@ -582,7 +595,7 @@
     piece, w1, coef1, scaled1, w2, coef2, scaled2 = pl.pallas_call(
         down12_kernel,
         out_shape=(
-            shape(NP, LANES),
+            shape(nx, NP, LANES),
             field1,
             kept(total1, 2, 8 * NC, LANES),
             field1,
@@ -597,19 +610,26 @@
         name="down12",
     )(data1, low_face, from_low, from_high)
 
-    pieces = lax.all_to_all(jnp.broadcast_to(piece, (nx * ny,) + piece.shape), ("gx", "gy"), 0, 0)
-    pieces = pieces.reshape((nx, ny) + piece.shape)
+    pieces = lax.all_gather(lax.all_to_all(piece, "gx", 0, 0), "gy", axis=0)
 
     rows3 = rows2 // 2
     total3 = nx * rows3 + 2 * RIM3
     ups = ("w", "w")
+    correction = pl.pallas_call(
+        coarse_kernel,
+        out_shape=shape(rows3 + 2 * RIM3, 32, LANES),
+        in_specs=[SM, VM],
+        out_specs=VM,
+        scratch_shapes=buffers(total3, 1, ("data", "coef", "scaled", "w", "w", "slope", "across")),
+        compiler_params=pltpu.CompilerParams(vmem_limit_bytes=VMEM_COARSE + VMEM_COARSE_ROW * total3),
+        name="coarse",
+    )(jnp.stack([gx, gy]).astype(jnp.int32), pieces)
     result = pl.pallas_call(
         up_kernel,
         out_shape=shape(2 * 16 * rows, columns),
-        in_specs=[SM] + [VM] * 10,
+        in_specs=[VM] * 10,
         out_specs=HB,
-        scratch_shapes=buffers(total3, 1, ("data", "coef", "scaled", "w", "w", "slope", "across"))
-        + buffers(total2, 1, ups)
+        scratch_shapes=buffers(total2, 1, ups)
         + buffers(total1, 2, ups)
         + buffers(total0, 3, ups)
         + buffers(max(total0, total1), 3, ("slope", "across"))
@@ -617,8 +637,7 @@
         compiler_params=UP_PARAMS,
         name="up",
     )(
-        jnp.stack([gx, gy]).astype(jnp.int32),
-        pieces,
+        correction,
         *keep([w0, coef0, scaled0, w1, coef1, scaled1, w2, coef2, scaled2]),
     )
     return result.reshape(misfit.shape)

time: 151 us -> 141 us (0.934)
  waiting for transfers between devices: 54 us -> 40 us
  blocking collectives: 13.9 us -> 23.5 us
  local copies, waits for them, and re-layouts: 23.8 us -> 19.7 us
    all_to_all x1, waiting for transfers between devices: 22.6 us -> 8.69 us  [per_device(): pieces = lax.all_gather(lax.all_to_all(piece, 'gx', 0, 0), 'gy', axis=0)]
    pallas_call x1, Pallas kernels: 20.1 us -> 8.15 us  [per_device(): pl.pallas_call(up_kernel, out_shape=shape(2 * 16 * rows, columns), in_spe...]
    pallas_call x1 -> x2, Pallas kernels: 8.23 us -> 19.6 us  [the longest x1 11.4 us: per_device(): pl.pallas_call(coarse_kernel, out_shape=shape(rows3 + 2 * RIM3, 32, LANES...]
    all_gather x0 -> x1, blocking collectives: none -> 9.62 us  [per_device(): pieces = lax.all_gather(lax.all_to_all(piece, 'gx', 0, 0), 'gy', axis=0)]
    unnamed x38 -> x34, local copies, waits for them, and re-layouts: 22.7 us -> 19.6 us
where the time goes in v2:
time: 141 us
  waiting for transfers between devices  40 us (28%)
  Pallas kernels  38.5 us (27%)
  blocking collectives  23.5 us (17%)
  local copies, waits for them, and re-layouts  19.7 us (14%)
  starting transfers between devices  18.3 us (13%)
    ppermute x2, waiting for transfers between devices, per_device(): from_low = lax.ppermute(high_face, 'gx', upward)  31.3 us
    unnamed x34, local copies, waits for them, and re-layouts  19.6 us
    all_gather x2, blocking collectives, beside(): every = lax.all_gather(strips, 'gy', axis=0)  13.9 us
    pallas_call x1, Pallas kernels, per_device(): pl.pallas_call(coarse_kernel, out_shape=shape(rows3 + 2 * RIM3, 32, LANES...  11.4 us
    all_gather x1, blocking collectives, per_device(): pieces = lax.all_gather(lax.all_to_all(piece, 'gx', 0, 0), 'gy', axis=0)  9.62 us
    all_to_all x1, waiting for transfers between devices, per_device(): pieces = lax.all_gather(lax.all_to_all(piece, 'gx', 0, 0), 'gy', axis=0)  8.69 us
    pallas_call x1, Pallas kernels, per_device(): pl.pallas_call(down12_kernel, out_shape=(shape(nx, NP, LANES), field1, ke...  8.2 us
    pallas_call x1, Pallas kernels, per_device(): pl.pallas_call(up_kernel, out_shape=shape(2 * 16 * rows, columns), in_spe...  8.15 us
  transfers between devices with their start and end apart: 5, of which 3 were waited for; matrix products, arithmetic and copies ran while one was open for 0% of the time, Pallas kernels for 0%

profile of v2, /device:TPU:0, one launch (start us, length us, event | category | flops | bytes accessed | tf_op | source)
XLA Modules:
  0.0 140.5 jit_solution(14726790193834743813)
XLA Ops:
  0.0 3.0 %arrange.1 = (f32[32,2,56,128]{3,2,1,0:T(8,128)S(1)}, f32[2,56,128]{2,1,0:T(8,128)S(1)}) custom-call(f32[1024,256]{1,0:T(8,128)} %bitcast.19, f32[512,256]{1,0:T(8,128)} %bitcast.23, f32[32,256]{1,0:T(8,128)} %friction_in.1, s32[32,256]{1,0:T(8,128)} %ice_mask_in.1, s32[32,256]{1,0:T(8,128)} %grounded_in.1), custom_call_target="tpu_custom_call" | custom-call | tf_op jit(solution)/shard_map/arrange/pallas_call | solution.py:535
  3.0 7.0 %all-gather = f32[8,56,128]{2,1,0:T(8,128)S(1)} all-gather(f32[2,56,128]{2,1,0:T(8,128)S(1)} %get-tuple-element.20), channel_id=2, replica_groups=mesh['gx'=8,'gy'=4] {'gy'}, dimensions={0}, use_global_device_ids=true | all-gather | bytes 286720 | tf_op jit(solution)/shard_map/all_gather | solution.py:530
  10.1 3.5 %collective-permute-start = (f32[10,56,128]{2,1,0:T(8,128)S(1)}, f32[10,56,128]{2,1,0:T(8,128)S(1)}, u32[]{:S(2)}, u32[]{:S(2)}) collective-permute-start(f32[10,56,128]{2,1,0:T(8,128)S(1)} %get-tuple-element.43), channel_id=1, source_target_pairs={{0,4},{4,8},{8,12},{12,16},{16,20},{20,24},{24,28},{1,5},{5,9},{9,... | collective-permute-start | bytes 860168 | tf_op jit(solution)/shard_map/ppermute | solution.py:560
  13.7 1.3 collective-permute-start.1
  15.0 11.4 %collective-permute-done.from_low = f32[10,56,128]{2,1,0:T(8,128)S(1)} collective-permute-done((f32[10,56,128]{2,1,0:T(8,128)S(1)}, f32[10,56,128]{2,1,0:T(8,128)S(1)}, u32[]{:S(2)}, u32[]{:S(2)}) %collective-permute-start) | collective-permute-done | bytes 286752 | tf_op jit(solution)/shard_map/ppermute | solution.py:560
  26.4 7.8 %down0.1 = (f32[16,56,128]{2,1,0:T(8,128)S(1)}, f32[2,2,56,128]{3,2,1,0:T(8,128)S(1)}, f32[40,3,32,128]{3,2,1,0:T(8,128)S(1)}, f32[40,3,120,128]{3,2,1,0:T(8,128)S(1)}, f32[40,3,32,128]{3,2,1,0:T(8,128)S(1)}) custom-call(f32[32,2,56,128]{3,2,1,0:T(8,128)S(1)} %get-tuple-element.19.own, f32[10,56,128]{2,1,0:T(8,128)S(1)} %get-tuple-element.44.sent, ...), custom_call_target="tpu_custom_call" | custom-call | tf_op jit(solution)/shard_map/down0/pallas_call | solution.py:568
  34.2 2.9 %copy-done = f32[40,3,120,128]{3,2,1,0:T(8,128)} copy-done((f32[40,3,120,128]{3,2,1,0:T(8,128)}, f32[40,3,120,128]{3,2,1,0:T(8,128)S(1)}, u32[]{:S(2)}) %copy-start) | copy-done | bytes 7372824
  37.1 6.8 %all-gather.1 = f32[8,2,56,128]{3,2,1,0:T(8,128)S(1)} all-gather(f32[2,2,56,128]{3,2,1,0:T(8,128)S(1)} %get-tuple-element.22), channel_id=3, replica_groups=mesh['gx'=8,'gy'=4] {'gy'}, dimensions={0}, use_global_device_ids=true | all-gather | bytes 573440 | tf_op jit(solution)/shard_map/all_gather | solution.py:530
  43.9 0.1 fusion.5
  44.0 0.1 pad_maximum_fusion
  44.1 4.4 %collective-permute-start.2 = (f32[17,56,128]{2,1,0:T(8,128)S(1)}, f32[17,56,128]{2,1,0:T(8,128)S(1)}, u32[]{:S(2)}, u32[]{:S(2)}) collective-permute-start(f32[17,56,128]{2,1,0:T(8,128)S(1)} %get-tuple-element.41), channel_id=1, source_target_pairs={{0,4},{4,8},{8,12},{12,16},{16,20},{20,24},{24,28},{1,5},{5,9},{9,... | collective-permute-start | bytes 1462280 | tf_op jit(solution)/shard_map/ppermute | solution.py:587
  48.6 1.4 %collective-permute-start.3 = (f32[17,56,128]{2,1,0:T(8,128)S(1)}, f32[17,56,128]{2,1,0:T(8,128)S(1)}, u32[]{:S(2)}, u32[]{:S(2)}) collective-permute-start(f32[17,56,128]{2,1,0:T(8,128)S(1)} %get-tuple-element.42.sent), channel_id=1, source_target_pairs={{4,0},{8,4},{12,8},{16,12},{20,16},{24,20},{28,24},{5,1},{9,5},{13... | collective-permute-start | bytes 1462280 | tf_op jit(solution)/shard_map/ppermute | solution.py:588
  50.0 19.9 %collective-permute-done.2.from_low = f32[17,56,128]{2,1,0:T(8,128)S(1)} collective-permute-done((f32[17,56,128]{2,1,0:T(8,128)S(1)}, f32[17,56,128]{2,1,0:T(8,128)S(1)}, u32[]{:S(2)}, u32[]{:S(2)}) %collective-permute-start.2) | collective-permute-done | bytes 487456 | tf_op jit(solution)/shard_map/ppermute | solution.py:587
  69.8 8.2 %down12.1 = (f32[8,56,128]{2,1,0:T(8,128)S(1)}, f32[42,2,32,128]{3,2,1,0:T(8,128)S(1)}, f32[42,2,120,128]{3,2,1,0:T(8,128)S(1)}, f32[42,2,32,128]{3,2,1,0:T(8,12...) custom-call(f32[16,56,128]{2,1,0:T(8,128)S(1)} %get-tuple-element.21.own, ...), custom_call_target="tpu_custom_call" | custom-call | tf_op jit(solution)/shard_map/down12/pallas_call | solution.py:595
  78.1 2.3 %copy-done.2 = f32[42,2,120,128]{3,2,1,0:T(8,128)} copy-done((f32[42,2,120,128]{3,2,1,0:T(8,128)}, f32[42,2,120,128]{3,2,1,0:T(8,128)S(1)}, u32[]{:S(2)}) %copy-start.2) | copy-done | bytes 5160984
  80.3 1.1 copy-done.8
  81.4 1.0 copy-done.10
  82.5 0.7 copy-done.12
  83.2 0.7 copy-done.14
  83.9 0.7 copy-done.16
  84.6 7.7 %all-to-all-start = ((f32[8,56,128]{2,1,0:T(8,128)}), f32[8,56,128]{2,1,0:T(8,128)}, u32[]{:S(2)}, u32[]{:S(2)}) async-start(f32[8,56,128]{2,1,0:T(8,128)} %copy-done.16), calls=%async_computation | async-start | bytes 458752 | tf_op jit(solution)/shard_map/all_to_all | solution.py:613
  92.3 0.1 pad_add_fusion.place
  92.4 8.7 %all-to-all-done = f32[8,56,128]{2,1,0:T(8,128)} async-done(((f32[8,56,128]{2,1,0:T(8,128)}), f32[8,56,128]{2,1,0:T(8,128)}, u32[]{:S(2)}, u32[]{:S(2)}) %all-to-all-start) | async-done | bytes 229408 | tf_op jit(solution)/shard_map/all_to_all | solution.py:613
  101.0 9.6 %all-gather.2 = f32[32,56,128]{2,1,0:T(8,128)S(1)} all-gather(f32[8,56,128]{2,1,0:T(8,128)} %all-to-all-done), channel_id=4, replica_groups=mesh['gx'=8,'gy'=4] {'gy'}, dimensions={0}, use_global_device_ids=true | all-gather | bytes 1146880 | tf_op jit(solution)/shard_map/all_gather | solution.py:613
  110.7 11.4 %coarse.1.correction = f32[8,32,128]{2,1,0:T(8,128)S(1)} custom-call(s32[2]{0:T(128)S(1)} %pad_add_fusion.place, f32[4,8,56,128]{3,2,1,0:T(8,128)S(1)} %bitcast.18), custom_call_target="tpu_custom_call" | custom-call | tf_op jit(solution)/shard_map/coarse/pallas_call | solution.py:618
  122.1 3.1 %copy-done.1 = f32[40,3,120,128]{3,2,1,0:T(8,128)S(1)} copy-done((f32[40,3,120,128]{3,2,1,0:T(8,128)S(1)}, f32[40,3,120,128]{3,2,1,0:T(8,128)}, u32[]{:S(2)}) %copy-start.1) | copy-done | bytes 7372824
  125.2 2.5 %copy-done.3 = f32[42,2,120,128]{3,2,1,0:T(8,128)S(1)} copy-done((f32[42,2,120,128]{3,2,1,0:T(8,128)S(1)}, f32[42,2,120,128]{3,2,1,0:T(8,128)}, u32[]{:S(2)}) %copy-start.3) | copy-done | bytes 5160984
  127.6 1.3 copy-done.9
  129.0 1.3 copy-done.11
  130.3 1.0 copy-done.13
  131.2 1.0 copy-done.15
  132.2 8.2 %up.1 = f32[1024,256]{1,0:T(8,128)} custom-call(f32[8,32,128]{2,1,0:T(8,128)S(1)} %coarse.1.correction, f32[40,3,32,128]{3,2,1,0:T(8,128)S(1)} %copy-done.5, f32[40,3,120,128]{3,2,1,0:T(8,128)S(1)} %copy-done.1, f32[40,3,32,128]{3,2,1,0:T(8,128)S(1)} %copy-done.7, f32[42,2,32,128]{3,2,1,0:T(8,128)S(1)} %get-tuple-element.27.w1, ...), custom_call_target="tpu_custom_call" | custom-call | tf_op jit(solution)/shard_map/up/pallas_call | solution.py:627
  (27 shorter events, 0.1 us)
Async XLA Ops:
  10.1 16.2 %collective-permute-start = (f32[10,56,128]{2,1,0:T(8,128)S(1)}, f32[10,56,128]{2,1,0:T(8,128)S(1)}, u32[]{:S(2)}, u32[]{:S(2)}) collective-permute-start(f32[10,56,128]{2,1,0:T(8,128)S(1)} %get-tuple-element.43), channel_id=1, source_target_pairs={{0,4},{4,8},{8,12},{12,16},{16,20},{20,24},{24,28},{1,5},{5,9},{9,... | collective-permute-start | bytes 860168 | tf_op jit(solution)/shard_map/ppermute | solution.py:560
  13.7 12.7 %collective-permute-start.1 = (f32[10,56,128]{2,1,0:T(8,128)S(1)}, f32[10,56,128]{2,1,0:T(8,128)S(1)}, u32[]{:S(2)}, u32[]{:S(2)}) collective-permute-start(f32[10,56,128]{2,1,0:T(8,128)S(1)} %get-tuple-element.44.sent), channel_id=1, source_target_pairs={{4,0},{8,4},{12,8},{16,12},{20,16},{24,20},{28,24},{5,1},{9,5},{13... | collective-permute-start | bytes 860168 | tf_op jit(solution)/shard_map/ppermute | solution.py:561
  34.1 2.9 %copy-start = (f32[40,3,120,128]{3,2,1,0:T(8,128)}, f32[40,3,120,128]{3,2,1,0:T(8,128)S(1)}, u32[]{:S(2)}) copy-start(f32[40,3,120,128]{3,2,1,0:T(8,128)S(1)} %get-tuple-element.25.coef0) | copy-start | bytes 22118404
  37.1 7.0 %copy-start.4 = (f32[40,3,32,128]{3,2,1,0:T(8,128)}, f32[40,3,32,128]{3,2,1,0:T(8,128)S(1)}, u32[]{:S(2)}) copy-start(f32[40,3,32,128]{3,2,1,0:T(8,128)S(1)} %get-tuple-element.24.w0) | copy-start | bytes 5898244
  37.1 7.0 %copy-start.6 = (f32[40,3,32,128]{3,2,1,0:T(8,128)}, f32[40,3,32,128]{3,2,1,0:T(8,128)S(1)}, u32[]{:S(2)}) copy-start(f32[40,3,32,128]{3,2,1,0:T(8,128)S(1)} %get-tuple-element.26.scaled0) | copy-start | bytes 5898244
  44.1 25.7 %collective-permute-start.2 = (f32[17,56,128]{2,1,0:T(8,128)S(1)}, f32[17,56,128]{2,1,0:T(8,128)S(1)}, u32[]{:S(2)}, u32[]{:S(2)}) collective-permute-start(f32[17,56,128]{2,1,0:T(8,128)S(1)} %get-tuple-element.41), channel_id=1, source_target_pairs={{0,4},{4,8},{8,12},{12,16},{16,20},{20,24},{24,28},{1,5},{5,9},{9,... | collective-permute-start | bytes 1462280 | tf_op jit(solution)/shard_map/ppermute | solution.py:587
  48.5 73.5 %copy-start.5 = (f32[40,3,32,128]{3,2,1,0:T(8,128)S(1)}, f32[40,3,32,128]{3,2,1,0:T(8,128)}, u32[]{:S(2)}) copy-start(f32[40,3,32,128]{3,2,1,0:T(8,128)} %copy-done.4) | copy-start | bytes 5898244
  48.6 21.3 %collective-permute-start.3 = (f32[17,56,128]{2,1,0:T(8,128)S(1)}, f32[17,56,128]{2,1,0:T(8,128)S(1)}, u32[]{:S(2)}, u32[]{:S(2)}) collective-permute-start(f32[17,56,128]{2,1,0:T(8,128)S(1)} %get-tuple-element.42.sent), channel_id=1, source_target_pairs={{4,0},{8,4},{12,8},{16,12},{20,16},{24,20},{28,24},{5,1},{9,5},{13... | collective-permute-start | bytes 1462280 | tf_op jit(solution)/shard_map/ppermute | solution.py:588
  78.1 2.3 %copy-start.2 = (f32[42,2,120,128]{3,2,1,0:T(8,128)}, f32[42,2,120,128]{3,2,1,0:T(8,128)S(1)}, u32[]{:S(2)}) copy-start(f32[42,2,120,128]{3,2,1,0:T(8,128)S(1)} %get-tuple-element.28.coef1) | copy-start | bytes 15482884
  80.3 1.1 copy-start.8
  81.4 1.0 copy-start.10
  82.5 0.7 copy-start.12
  83.2 0.7 copy-start.14
  83.9 0.7 copy-start.16
  84.6 16.4 %all-to-all-start = ((f32[8,56,128]{2,1,0:T(8,128)}), f32[8,56,128]{2,1,0:T(8,128)}, u32[]{:S(2)}, u32[]{:S(2)}) async-start(f32[8,56,128]{2,1,0:T(8,128)} %copy-done.16), calls=%async_computation | async-start | bytes 458752 | tf_op jit(solution)/shard_map/all_to_all | solution.py:613
  101.0 21.0 %copy-start.7 = (f32[40,3,32,128]{3,2,1,0:T(8,128)S(1)}, f32[40,3,32,128]{3,2,1,0:T(8,128)}, u32[]{:S(2)}) copy-start(f32[40,3,32,128]{3,2,1,0:T(8,128)} %copy-done.6) | copy-start | bytes 5898244
  122.1 3.1 %copy-start.1 = (f32[40,3,120,128]{3,2,1,0:T(8,128)S(1)}, f32[40,3,120,128]{3,2,1,0:T(8,128)}, u32[]{:S(2)}) copy-start(f32[40,3,120,128]{3,2,1,0:T(8,128)} %copy-done) | copy-start | bytes 22118404
  125.2 2.5 %copy-start.3 = (f32[42,2,120,128]{3,2,1,0:T(8,128)S(1)}, f32[42,2,120,128]{3,2,1,0:T(8,128)}, u32[]{:S(2)}) copy-start(f32[42,2,120,128]{3,2,1,0:T(8,128)} %copy-done.2) | copy-start | bytes 15482884
  127.6 1.3 copy-start.9
  129.0 1.3 copy-start.11
  130.2 1.0 copy-start.13
  131.2 1.0 copy-start.15

commit v3 on v2

--- a/solution.py
+++ b/solution.py
@@ -19,10 +19,8 @@
 RIM3 = 2
 STRIP1 = 16
 NC = 15
-VMEM_DOWN = 14 * 1024 * 1024
-VMEM_UP = 17 * 1024 * 1024
-VMEM_COARSE = 3 * 1024 * 1024
-VMEM_COARSE_ROW = 200 * 1024
+VMEM_DOWN = 28 * 1024 * 1024
+VMEM_UP = 60 * 1024 * 1024
 F32 = jnp.float32
 UNROLL0 = (18, 6, 4)
 UNROLL1 = (18, 6, 4)
@@ -228,6 +226,13 @@
     return jnp.where(lane < LANES // 2, to_low, to_high)
 
 
+def copy_rows(source, target, sem, first, last):
+    rows = pl.ds(first, last - first)
+    copy = pltpu.make_async_copy(source.at[rows], target.at[rows], sem)
+    copy.start()
+    return copy
+
+
 def arrange_kernel(misfit, viscosity, friction_in, ice_mask_in, grounded_in, data, strips,
                    misfit_half, viscosity_half, friction, ice_mask, grounded, sems):
     rows = friction.shape[0]
@@ -275,8 +280,8 @@
             strips[side, planes, :] = strip
 
 
-def down0_kernel(own, sent, from_low, from_high, coarse, strips1, wa, coef, scaled,
-                 data, diag, slope, across):
+def down0_kernel(own, sent, from_low, from_high, coarse, strips1, w_out, coef_out, scaled_out,
+                 data, diag, slope, across, wa, coef, scaled, sems):
     rows = own.shape[0]
     total = rows + 2 * RIM0
 
@@ -295,8 +300,14 @@
         data[r, 2] = unpack_rim(from_low[2 * RIM0], from_low[2 * RIM0 + 1], low_at, RIM0)
         data[RIM0 + rows + r, 2] = unpack_rim(from_high[2 * RIM0], from_high[2 * RIM0 + 1], r * RIM0, RIM0)
 
-    make_coefs(data, coef, scaled, diag, 1, total - 1, 1.0, False, UNROLL0[2])
+    half = total // 2 + 1
+    make_coefs(data, coef, scaled, diag, 1, half, 1.0, False, UNROLL0[2])
+    copies = [copy_rows(coef, coef_out, sems.at[0], 2, half)]
+    make_coefs(data, coef, scaled, diag, half, total - 1, 1.0, False, UNROLL0[2])
+    copies.append(copy_rows(coef, coef_out, sems.at[1], half, total - 2))
+    copies.append(copy_rows(scaled, scaled_out, sems.at[2], 3, total - 3))
     sweep(scaled, wa, coef, scaled, slope, across, 2, total - 2, False, UNROLL0)
+    copies.append(copy_rows(wa, w_out, sems.at[3], 2, total - 2))
 
     def coefs_row(i):
         coarse[i, 32:56, :] = restrict_row(data, slice(32, 56), RIM0 + 2 * i)
@@ -319,10 +330,12 @@
                     shift = at if side == 0 else at + STRIP1
                     strip = put(strip, coarse[part * group + j, planes, :], shift, STRIP1, at)
                 strips1[side, part, planes, :] = strip
-
-
-def down12_kernel(own, sent, from_low, from_high, piece, wa1, coef1, scaled1, wa2, coef2, scaled2,
-                  data1, diag1, slope1, across1, data2, diag2, slope2, across2):
+    for copy in copies:
+        copy.wait()
+
+
+def down12_kernel(own, sent, from_low, from_high, piece, w1_out, coef1_out, scaled1_out, w2_out, coef2_out, scaled2_out,
+                  data1, diag1, slope1, across1, wa1, coef1, scaled1, data2, diag2, slope2, across2, wa2, coef2, scaled2, sems):
     rows = own.shape[0]
     total = rows + 2 * RIM1
     group = LANES // STRIP1
@@ -349,7 +362,10 @@
         data1[RIM1 + rows + r, 1] = rim(from_high, RIM1, r)
 
     make_coefs(data1, coef1, scaled1, diag1, 1, total - 1, 0.25, False, UNROLL1[2])
+    copies = [copy_rows(coef1, coef1_out, sems.at[0], 10, total - 10)]
+    copies.append(copy_rows(scaled1, scaled1_out, sems.at[1], 11, total - 11))
     sweep(scaled1, wa1, coef1, scaled1, slope1, across1, 2, total - 2, False, UNROLL1)
+    copies.append(copy_rows(wa1, w1_out, sems.at[2], 9, total - 9))
     remainders(wa1, diag1, data1, diag1, coef1, slope1, across1, 3, total - 3, UNROLL1, 2)
 
     rows2 = rows // 2
@@ -366,7 +382,10 @@
     rows_loop(1, total2 - 1, target_row, UNROLL_MOVE)
 
     make_coefs(data2, coef2, scaled2, diag2, 1, total2 - 1, 0.0625, False, UNROLL2[2])
+    copies.append(copy_rows(coef2, coef2_out, sems.at[3], 2, total2 - 2))
+    copies.append(copy_rows(scaled2, scaled2_out, sems.at[4], 3, total2 - 3))
     sweep(scaled2, wa2, coef2, scaled2, slope2, across2, 2, total2 - 2, False, UNROLL2)
+    copies.append(copy_rows(wa2, w2_out, sems.at[5], 2, total2 - 2))
     remainders(wa2, diag2, data2, diag2, coef2, slope2, across2, RIM2, RIM2 + rows2, UNROLL2, 1)
 
     rows3 = rows2 // 2
@@ -379,9 +398,22 @@
             strip = put(strip, restrict_row(source, planes, RIM2 + 2 * i), i * width, width, i * width)
         for d in range(piece.shape[0]):
             piece[d, planes, :] = strip
-
-
-def coarse_kernel(place, pieces, correction, data3, coef3, scaled3, wa3, wb3, slope3, across3):
+    for copy in copies:
+        copy.wait()
+
+
+def up_kernel(place, pieces, w0_in, coef0_in, scaled0_in, w1_in, coef1_in, scaled1_in, w2_in, coef2_in, scaled2_in, result,
+              data3, coef3, scaled3, wa3, wb3, slope3, across3, w2, coef2, scaled2, wa2, wb2, w1, coef1, scaled1, wa1, wb1,
+              w0, coef0, scaled0, wa0, wb0, slope0, across0, result_half, sems):
+    slope1, across1 = (v.at[pl.ds(0, wa1.shape[0]), pl.ds(0, 2)] for v in (slope0, across0))
+    slope2, across2 = (v.at[pl.ds(0, wa2.shape[0]), pl.ds(0, 1)] for v in (slope0, across0))
+    copies = []
+    for source, target, first in (
+        (w2_in, w2, 2), (coef2_in, coef2, 2), (scaled2_in, scaled2, 3),
+        (w1_in, w1, 9), (coef1_in, coef1, 10), (scaled1_in, scaled1, 11),
+        (w0_in, w0, 2), (coef0_in, coef0, 2), (scaled0_in, scaled0, 3),
+    ):
+        copies.append(copy_rows(source, target, sems.at[len(copies)], first, source.shape[0] - first))
     devices_y, devices_x = pieces.shape[0], pieces.shape[1]
     rows3 = devices_y
     width = LANES // devices_y
@@ -438,23 +470,20 @@
     inside = (column >= 0) & (column < LANES)
     pick = jnp.where(inside, column, 0)
 
+    for copy in copies[:3]:
+        copy.wait()
+    rows2 = 2 * rows3
     for i in range(rows3 + 2 * RIM3):
-        line = wa3[gx * rows3 + i, 0]
-        correction[i] = jnp.where(inside, gather_lanes(line, pick), 0.0)
-
-
-def up_kernel(correction, w0, coef0, scaled0, w1, coef1, scaled1, w2, coef2, scaled2, result,
-              wa2, wb2, wa1, wb1, wa0, wb0, slope0, across0, result_half, sems):
-    slope1, across1 = (v.at[pl.ds(0, wa1.shape[0]), pl.ds(0, 2)] for v in (slope0, across0))
-    slope2, across2 = (v.at[pl.ds(0, wa2.shape[0]), pl.ds(0, 1)] for v in (slope0, across0))
-    rows2 = w2.shape[0] - 2 * RIM2
-    for i in range(correction.shape[0]):
+        add = jnp.where(inside, gather_lanes(wa3[gx * rows3 + i, 0], pick), 0.0)
         for r in (2 * i + 2, 2 * i + 3):
-            wa2[r, 0] = w2[r, 0] + correction[i]
+            wa2[r, 0] = w2[r, 0] + add
     total2 = rows2 + 2 * RIM2
     sweep(wa2, wb2, coef2, scaled2, slope2, across2, 3, total2 - 3, False, UNROLL2)
     sweep(wb2, wa2, coef2, scaled2, slope2, across2, 4, total2 - 4, False, UNROLL2)
 
+
+    for copy in copies[3:6]:
+        copy.wait()
 
     def add1(r):
         adds = prolong_row([wa2[r, 0]], 2)
@@ -467,6 +496,9 @@
     sweep(wa1, wb1, coef1, scaled1, slope1, across1, 11, total1 - 11, False, UNROLL1)
     sweep(wb1, wa1, coef1, scaled1, slope1, across1, 12, total1 - 12, False, UNROLL1)
 
+
+    for copy in copies[6:]:
+        copy.wait()
 
     def add0(r):
         adds = prolong_row([wa1[r, t] for t in range(2)], 3)
@@ -499,19 +531,18 @@
     return jax.ShapeDtypeStruct(dims, F32)
 
 
-def kept(*dims):
-    return pltpu.VMEM(dims, F32)
-
-
-def keep(arrays):
-    return [pltpu.with_memory_space_constraint(v, pltpu.VMEM) for v in arrays]
+def stored(*dims):
+    return pltpu.HBM(dims, F32)
+
+
+def in_hbm(arrays):
+    return [pltpu.with_memory_space_constraint(v, pltpu.HBM) for v in arrays]
 
 
 VM = pl.BlockSpec(memory_space=pltpu.VMEM)
 SM = pl.BlockSpec(memory_space=pltpu.SMEM)
 HB = pl.BlockSpec(memory_space=pl.ANY)
 PARAMS = pltpu.CompilerParams(vmem_limit_bytes=VMEM_DOWN)
-UP_PARAMS = pltpu.CompilerParams(vmem_limit_bytes=VMEM_UP)
 
 
 def buffers(rows, tiles, names):
@@ -548,10 +579,7 @@
         compiler_params=PARAMS,
         name="arrange",
     )(
-        *(
-            pltpu.with_memory_space_constraint(v.reshape(-1, columns), pltpu.HBM)
-            for v in (misfit, viscosity, friction, ice_mask, grounded)
-        )
+        *in_hbm(v.reshape(-1, columns) for v in (misfit, viscosity, friction, ice_mask, grounded))
     )
     left, right = beside(strips0)
     rims = [left[None], right[None]]
@@ -561,22 +589,22 @@
     from_high = lax.ppermute(low_face, "gx", downward)
 
     total0 = rows + 2 * RIM0
-    names = ("data", "diag", "slope", "across")
+    names = ("data", "diag", "slope", "across", "w", "coef", "scaled")
     rows1 = rows // 2
     group = LANES // STRIP1
-    field0 = kept(total0, 3, 32, LANES)
+    field0 = stored(total0, 3, 32, LANES)
     data1, strips1, w0, coef0, scaled0 = pl.pallas_call(
         down0_kernel,
         out_shape=(
             shape(rows1, NP, LANES),
             shape(2, rows1 // group, NP, LANES),
             field0,
-            kept(total0, 3, 8 * NC, LANES),
+            stored(total0, 3, 8 * NC, LANES),
             field0,
         ),
         in_specs=[VM] * 4,
-        out_specs=(VM,) * 5,
-        scratch_shapes=buffers(total0, 3, names),
+        out_specs=(VM, VM, HB, HB, HB),
+        scratch_shapes=buffers(total0, 3, names) + [pltpu.SemaphoreType.DMA((4,))],
         compiler_params=PARAMS,
         name="down0",
     )(data0, low_face, from_low, from_high)
@@ -590,22 +618,22 @@
     total1 = rows1 + 2 * RIM1
     rows2 = rows1 // 2
     total2 = rows2 + 2 * RIM2
-    field1 = kept(total1, 2, 32, LANES)
-    field2 = kept(total2, 1, 32, LANES)
+    field1 = stored(total1, 2, 32, LANES)
+    field2 = stored(total2, 1, 32, LANES)
     piece, w1, coef1, scaled1, w2, coef2, scaled2 = pl.pallas_call(
         down12_kernel,
         out_shape=(
             shape(nx, NP, LANES),
             field1,
-            kept(total1, 2, 8 * NC, LANES),
+            stored(total1, 2, 8 * NC, LANES),
             field1,
             field2,
-            kept(total2, 1, 8 * NC, LANES),
+            stored(total2, 1, 8 * NC, LANES),
             field2,
         ),
         in_specs=[VM] * 4,
-        out_specs=(VM,) * 7,
-        scratch_shapes=buffers(total1, 2, names) + buffers(total2, 1, names),
+        out_specs=(VM,) + (HB,) * 6,
+        scratch_shapes=buffers(total1, 2, names) + buffers(total2, 1, names) + [pltpu.SemaphoreType.DMA((6,))],
         compiler_params=PARAMS,
         name="down12",
     )(data1, low_face, from_low, from_high)
@@ -614,31 +642,24 @@
 
     rows3 = rows2 // 2
     total3 = nx * rows3 + 2 * RIM3
-    ups = ("w", "w")
-    correction = pl.pallas_call(
-        coarse_kernel,
-        out_shape=shape(rows3 + 2 * RIM3, 32, LANES),
-        in_specs=[SM, VM],
-        out_specs=VM,
-        scratch_shapes=buffers(total3, 1, ("data", "coef", "scaled", "w", "w", "slope", "across")),
-        compiler_params=pltpu.CompilerParams(vmem_limit_bytes=VMEM_COARSE + VMEM_COARSE_ROW * total3),
-        name="coarse",
-    )(jnp.stack([gx, gy]).astype(jnp.int32), pieces)
+    ups = ("w", "coef", "scaled", "w", "w")
     result = pl.pallas_call(
         up_kernel,
         out_shape=shape(2 * 16 * rows, columns),
-        in_specs=[VM] * 10,
+        in_specs=[SM, VM] + [HB] * 9,
         out_specs=HB,
-        scratch_shapes=buffers(total2, 1, ups)
+        scratch_shapes=buffers(total3, 1, ("data", "coef", "scaled", "w", "w", "slope", "across"))
+        + buffers(total2, 1, ups)
         + buffers(total1, 2, ups)
         + buffers(total0, 3, ups)
         + buffers(max(total0, total1), 3, ("slope", "across"))
-        + [pltpu.VMEM((2, 2 * 16 * rows, LANES), F32), pltpu.SemaphoreType.DMA((2,))],
-        compiler_params=UP_PARAMS,
+        + [pltpu.VMEM((2, 2 * 16 * rows, LANES), F32), pltpu.SemaphoreType.DMA((9,))],
+        compiler_params=pltpu.CompilerParams(vmem_limit_bytes=VMEM_UP),
         name="up",
     )(
-        correction,
-        *keep([w0, coef0, scaled0, w1, coef1, scaled1, w2, coef2, scaled2]),
+        jnp.stack([gx, gy]).astype(jnp.int32),
+        pieces,
+        *in_hbm([w0, coef0, scaled0, w1, coef1, scaled1, w2, coef2, scaled2]),
     )
     return result.reshape(misfit.shape)
 

time: 141 us -> 123 us (0.87)
  local copies, waits for them, and re-layouts: 19.7 us -> 0.08 us
  Pallas kernels: 38.5 us -> 40.4 us
    unnamed x34 -> x0, local copies, waits for them, and re-layouts: 19.6 us -> none
    pallas_call x1, Pallas kernels: 8.15 us -> 20.2 us  [per_device(): pl.pallas_call(up_kernel, out_shape=shape(2 * 16 * rows, columns), in_spe...]
    pallas_call x2 -> x1, Pallas kernels: 19.6 us -> 9.41 us  [per_device(): pl.pallas_call(down12_kernel, out_shape=(shape(nx, NP, LANES), field1, st...]
  transfers between devices with their start and end apart: 5 -> 5, of which waited for: 3 -> 3; matrix products, arithmetic and copies ran while one was open for 0% -> 1% of each run, Pallas kernels for 0% -> 0%
where the time goes in v3:
time: 123 us
  Pallas kernels  40.4 us (33%)
  waiting for transfers between devices  39.4 us (32%)
  blocking collectives  23.6 us (19%)
  starting transfers between devices  18.2 us (15%)
    ppermute x2, waiting for transfers between devices, per_device(): from_low = lax.ppermute(high_face, 'gx', upward)  31.4 us
    pallas_call x1, Pallas kernels, per_device(): pl.pallas_call(up_kernel, out_shape=shape(2 * 16 * rows, columns), in_spe...  20.2 us
    all_gather x2, blocking collectives, beside(): every = lax.all_gather(strips, 'gy', axis=0)  13.9 us
    all_gather x1, blocking collectives, per_device(): pieces = lax.all_gather(lax.all_to_all(piece, 'gx', 0, 0), 'gy', axis=0)  9.72 us
    pallas_call x1, Pallas kernels, per_device(): pl.pallas_call(down12_kernel, out_shape=(shape(nx, NP, LANES), field1, st...  9.41 us
    all_to_all x1, waiting for transfers between devices, per_device(): pieces = lax.all_gather(lax.all_to_all(piece, 'gx', 0, 0), 'gy', axis=0)  8.01 us
    ppermute x2, starting transfers between devices, per_device(): from_low = lax.ppermute(high_face, 'gx', upward)  7.93 us
    pallas_call x1, Pallas kernels, per_device(): pl.pallas_call(down0_kernel, out_shape=(shape(rows1, NP, LANES), shape(2,...  7.82 us
  transfers between devices with their start and end apart: 5, of which 3 were waited for; matrix products, arithmetic and copies ran while one was open for 1% of the time, Pallas kernels for 0%

profile of v3, /device:TPU:0, one launch (start us, length us, event | category | flops | bytes accessed | tf_op | source)
XLA Modules:
  0.0 122.8 jit_solution(11526654940528202283)
XLA Ops:
  0.0 3.0 %arrange.1 = (f32[32,2,56,128]{3,2,1,0:T(8,128)S(1)}, f32[2,56,128]{2,1,0:T(8,128)S(1)}) custom-call(f32[1024,256]{1,0:T(8,128)} %bitcast.19, f32[512,256]{1,0:T(8,128)} %bitcast.23, f32[32,256]{1,0:T(8,128)} %friction_in.1, s32[32,256]{1,0:T(8,128)} %ice_mask_in.1, s32[32,256]{1,0:T(8,128)} %grounded_in.1), custom_call_target="tpu_custom_call" | custom-call | tf_op jit(solution)/shard_map/arrange/pallas_call | solution.py:566
  3.0 7.0 %all-gather = f32[8,56,128]{2,1,0:T(8,128)S(1)} all-gather(f32[2,56,128]{2,1,0:T(8,128)S(1)} %get-tuple-element.20), channel_id=2, replica_groups=mesh['gx'=8,'gy'=4] {'gy'}, dimensions={0}, use_global_device_ids=true | all-gather | bytes 286720 | tf_op jit(solution)/shard_map/all_gather | solution.py:561
  10.1 3.5 %collective-permute-start = (f32[10,56,128]{2,1,0:T(8,128)S(1)}, f32[10,56,128]{2,1,0:T(8,128)S(1)}, u32[]{:S(2)}, u32[]{:S(2)}) collective-permute-start(f32[10,56,128]{2,1,0:T(8,128)S(1)} %get-tuple-element.43), channel_id=1, source_target_pairs={{0,4},{4,8},{8,12},{12,16},{16,20},{20,24},{24,28},{1,5},{5,9},{9,... | collective-permute-start | bytes 860168 | tf_op jit(solution)/shard_map/ppermute | solution.py:588
  13.7 1.3 %collective-permute-start.1 = (f32[10,56,128]{2,1,0:T(8,128)S(1)}, f32[10,56,128]{2,1,0:T(8,128)S(1)}, u32[]{:S(2)}, u32[]{:S(2)}) collective-permute-start(f32[10,56,128]{2,1,0:T(8,128)S(1)} %get-tuple-element.44.sent), channel_id=1, source_target_pairs={{4,0},{8,4},{12,8},{16,12},{20,16},{24,20},{28,24},{5,1},{9,5},{13... | collective-permute-start | bytes 860168 | tf_op jit(solution)/shard_map/ppermute | solution.py:589
  15.0 11.4 %collective-permute-done.from_low = f32[10,56,128]{2,1,0:T(8,128)S(1)} collective-permute-done((f32[10,56,128]{2,1,0:T(8,128)S(1)}, f32[10,56,128]{2,1,0:T(8,128)S(1)}, u32[]{:S(2)}, u32[]{:S(2)}) %collective-permute-start) | collective-permute-done | bytes 286752 | tf_op jit(solution)/shard_map/ppermute | solution.py:588
  26.4 0.0 collective-permute-done.1.from_high
  26.4 7.8 %down0.1 = (f32[16,56,128]{2,1,0:T(8,128)S(1)}, f32[2,2,56,128]{3,2,1,0:T(8,128)S(1)}, f32[40,3,32,128]{3,2,1,0:T(8,128)}, f32[40,3,120,128]{3,2,1,0:T(8,128)}, f32[40,3,32,128]{3,2,1,0:T(8,128)}) custom-call(f32[32,2,56,128]{3,2,1,0:T(8,128)S(1)} %get-tuple-element.19.own, f32[10,56,128]{2,1,0:T(8,128)S(1)} %get-tuple-element.44.sent, ...), custom_call_target="tpu_custom_call" | custom-call | tf_op jit(solution)/shard_map/down0/pallas_call | solution.py:596
  34.2 6.8 %all-gather.1 = f32[8,2,56,128]{3,2,1,0:T(8,128)S(1)} all-gather(f32[2,2,56,128]{3,2,1,0:T(8,128)S(1)} %get-tuple-element.22), channel_id=3, replica_groups=mesh['gx'=8,'gy'=4] {'gy'}, dimensions={0}, use_global_device_ids=true | all-gather | bytes 573440 | tf_op jit(solution)/shard_map/all_gather | solution.py:561
  41.0 0.1 fusion.5
  41.1 0.1 pad_maximum_fusion
  41.2 4.4 %collective-permute-start.2 = (f32[17,56,128]{2,1,0:T(8,128)S(1)}, f32[17,56,128]{2,1,0:T(8,128)S(1)}, u32[]{:S(2)}, u32[]{:S(2)}) collective-permute-start(f32[17,56,128]{2,1,0:T(8,128)S(1)} %get-tuple-element.41), channel_id=1, source_target_pairs={{0,4},{4,8},{8,12},{12,16},{16,20},{20,24},{24,28},{1,5},{5,9},{9,... | collective-permute-start | bytes 1462280 | tf_op jit(solution)/shard_map/ppermute | solution.py:615
  45.7 1.3 %collective-permute-start.3 = (f32[17,56,128]{2,1,0:T(8,128)S(1)}, f32[17,56,128]{2,1,0:T(8,128)S(1)}, u32[]{:S(2)}, u32[]{:S(2)}) collective-permute-start(f32[17,56,128]{2,1,0:T(8,128)S(1)} %get-tuple-element.42.sent), channel_id=1, source_target_pairs={{4,0},{8,4},{12,8},{16,12},{20,16},{24,20},{28,24},{5,1},{9,5},{13... | collective-permute-start | bytes 1462280 | tf_op jit(solution)/shard_map/ppermute | solution.py:616
  47.0 20.0 %collective-permute-done.2.from_low = f32[17,56,128]{2,1,0:T(8,128)S(1)} collective-permute-done((f32[17,56,128]{2,1,0:T(8,128)S(1)}, f32[17,56,128]{2,1,0:T(8,128)S(1)}, u32[]{:S(2)}, u32[]{:S(2)}) %collective-permute-start.2) | collective-permute-done | bytes 487456 | tf_op jit(solution)/shard_map/ppermute | solution.py:615
  67.0 0.0 collective-permute-done.3.from_high
  67.0 9.4 %down12.1 = (f32[8,56,128]{2,1,0:T(8,128)}, f32[42,2,32,128]{3,2,1,0:T(8,128)}, f32[42,2,120,128]{3,2,1,0:T(8,128)}, f32[42,2,32,128]{3,2,1,0:T(8,128)}, f32[20,...) custom-call(f32[16,56,128]{2,1,0:T(8,128)S(1)} %get-tuple-element.21.own, ...), custom_call_target="tpu_custom_call" | custom-call | tf_op jit(solution)/shard_map/down12/pallas_call | solution.py:623
  76.4 7.7 %all-to-all-start = ((f32[8,56,128]{2,1,0:T(8,128)}), f32[8,56,128]{2,1,0:T(8,128)S(1)}, u32[]{:S(2)}, u32[]{:S(2)}) async-start(f32[8,56,128]{2,1,0:T(8,128)} %get-tuple-element.23), calls=%async_computation | async-start | bytes 458752 | tf_op jit(solution)/shard_map/all_to_all | solution.py:641
  84.0 0.6 pad_add_fusion.place
  84.7 8.0 %all-to-all-done = f32[8,56,128]{2,1,0:T(8,128)S(1)} async-done(((f32[8,56,128]{2,1,0:T(8,128)}), f32[8,56,128]{2,1,0:T(8,128)S(1)}, u32[]{:S(2)}, u32[]{:S(2)}) %all-to-all-start) | async-done | bytes 229408 | tf_op jit(solution)/shard_map/all_to_all | solution.py:641
  92.7 9.7 %all-gather.2 = f32[32,56,128]{2,1,0:T(8,128)} all-gather(f32[8,56,128]{2,1,0:T(8,128)S(1)} %all-to-all-done), channel_id=4, replica_groups=mesh['gx'=8,'gy'=4] {'gy'}, dimensions={0}, use_global_device_ids=true | all-gather | bytes 1146880 | tf_op jit(solution)/shard_map/all_gather | solution.py:641
  102.4 20.2 %up.1 = f32[1024,256]{1,0:T(8,128)} custom-call(s32[2]{0:T(128)} %pad_add_fusion.place, f32[4,8,56,128]{3,2,1,0:T(8,128)} %bitcast.18, f32[40,3,32,128]{3,2,1,0:T(8,128)} %get-tuple-element.24.w0_in, f32[40,3,120,128]{3,2,1,0:T(8,128)} %get-tuple-element.25.coef0_in, f32[40,3,32,128]{3,2,1,0:T(8,128)} %get-tuple-element.26.scaled0_in, ...), custom_call_target="tpu_custom_call" | custom-call | tf_op jit(solution)/shard_map/up/pallas_call | solution.py:646
  (4 shorter events, 0.1 us)
Async XLA Ops:
  10.1 16.2 %collective-permute-start = (f32[10,56,128]{2,1,0:T(8,128)S(1)}, f32[10,56,128]{2,1,0:T(8,128)S(1)}, u32[]{:S(2)}, u32[]{:S(2)}) collective-permute-start(f32[10,56,128]{2,1,0:T(8,128)S(1)} %get-tuple-element.43), channel_id=1, source_target_pairs={{0,4},{4,8},{8,12},{12,16},{16,20},{20,24},{24,28},{1,5},{5,9},{9,... | collective-permute-start | bytes 860168 | tf_op jit(solution)/shard_map/ppermute | solution.py:588
  13.7 12.7 %collective-permute-start.1 = (f32[10,56,128]{2,1,0:T(8,128)S(1)}, f32[10,56,128]{2,1,0:T(8,128)S(1)}, u32[]{:S(2)}, u32[]{:S(2)}) collective-permute-start(f32[10,56,128]{2,1,0:T(8,128)S(1)} %get-tuple-element.44.sent), channel_id=1, source_target_pairs={{4,0},{8,4},{12,8},{16,12},{20,16},{24,20},{28,24},{5,1},{9,5},{13... | collective-permute-start | bytes 860168 | tf_op jit(solution)/shard_map/ppermute | solution.py:589
  41.2 25.7 %collective-permute-start.2 = (f32[17,56,128]{2,1,0:T(8,128)S(1)}, f32[17,56,128]{2,1,0:T(8,128)S(1)}, u32[]{:S(2)}, u32[]{:S(2)}) collective-permute-start(f32[17,56,128]{2,1,0:T(8,128)S(1)} %get-tuple-element.41), channel_id=1, source_target_pairs={{0,4},{4,8},{8,12},{12,16},{16,20},{20,24},{24,28},{1,5},{5,9},{9,... | collective-permute-start | bytes 1462280 | tf_op jit(solution)/shard_map/ppermute | solution.py:615
  45.7 21.3 %collective-permute-start.3 = (f32[17,56,128]{2,1,0:T(8,128)S(1)}, f32[17,56,128]{2,1,0:T(8,128)S(1)}, u32[]{:S(2)}, u32[]{:S(2)}) collective-permute-start(f32[17,56,128]{2,1,0:T(8,128)S(1)} %get-tuple-element.42.sent), channel_id=1, source_target_pairs={{4,0},{8,4},{12,8},{16,12},{20,16},{24,20},{28,24},{5,1},{9,5},{13... | collective-permute-start | bytes 1462280 | tf_op jit(solution)/shard_map/ppermute | solution.py:616
  76.4 16.3 %all-to-all-start = ((f32[8,56,128]{2,1,0:T(8,128)}), f32[8,56,128]{2,1,0:T(8,128)S(1)}, u32[]{:S(2)}, u32[]{:S(2)}) async-start(f32[8,56,128]{2,1,0:T(8,128)} %get-tuple-element.23), calls=%async_computation | async-start | bytes 458752 | tf_op jit(solution)/shard_map/all_to_all | solution.py:641

commit v4 on v3

--- a/solution.py
+++ b/solution.py
@@ -226,6 +226,18 @@
     return jnp.where(lane < LANES // 2, to_low, to_high)
 
 
+def pair_rows(tiles):
+    sub = lax.broadcasted_iota(jnp.int32, (8, LANES), 0)
+    out = tiles[0]
+    for j in range(1, len(tiles)):
+        out = jnp.where(sub >= 2 * j, pltpu.roll(tiles[j], 2 * j, 0), out)
+    return out
+
+
+def pair_row(tile, j):
+    return pltpu.roll(tile, 8 - 2 * j, 0) if j else tile
+
+
 def copy_rows(source, target, sem, first, last):
     rows = pl.ds(first, last - first)
     copy = pltpu.make_async_copy(source.at[rows], target.at[rows], sem)
@@ -233,7 +245,7 @@
     return copy
 
 
-def arrange_kernel(misfit, viscosity, friction_in, ice_mask_in, grounded_in, data, strips,
+def arrange_kernel(misfit, viscosity, friction_in, ice_mask_in, grounded_in, data, strips, edges,
                    misfit_half, viscosity_half, friction, ice_mask, grounded, sems):
     rows = friction.shape[0]
     copies = [
@@ -270,7 +282,10 @@
         return carry
 
     lax.fori_loop(0, rows // 8, eight, 0)
+    corner = RIM0 * RIM0
     for side in range(2):
+        low = jnp.zeros((8, LANES), F32)
+        high = low
         for first in range(0, NP, 8):
             planes = slice(first, first + 8)
             strip = jnp.zeros((8, LANES), F32)
@@ -278,9 +293,17 @@
                 at = r * RIM0
                 strip = put(strip, data[r, side, planes, :], at if side == 0 else at + RIM0, RIM0, at)
             strips[side, planes, :] = strip
-
-
-def down0_kernel(own, sent, from_low, from_high, coarse, strips1, w_out, coef_out, scaled_out,
+            at = first // 8 * corner
+            low = put(low, strip, at, corner, at)
+            high = put(high, strip, at + corner, corner, at)
+        strips[side, NP : NP + 8, :] = low
+        strips[side, NP + 8 : NP + 16, :] = high
+    for t in range(2):
+        edges[0, 8 * t : 8 * t + 8, :] = pair_rows([data[r, t, 48:56, :] for r in range(RIM0 - 1)])
+        edges[1, 8 * t : 8 * t + 8, :] = pair_rows([data[rows - RIM0 + 1 + r, t, 48:56, :] for r in range(RIM0 - 1)])
+
+
+def down0_kernel(own, left, right, from_low, from_high, coarse, strips1, edges1, w_out, coef_out, scaled_out,
                  data, diag, slope, across, wa, coef, scaled, sems):
     rows = own.shape[0]
     total = rows + 2 * RIM0
@@ -291,14 +314,26 @@
 
     rows_loop(0, rows, copy_row, 4)
     for r in range(rows):
-        data[RIM0 + r, 2] = unpack_rim(sent[2 * RIM0], sent[2 * RIM0 + 1], r * RIM0, RIM0)
-    for r in range(RIM0):
+        data[RIM0 + r, 2] = unpack_rim(left[0:NP, :], right[0:NP, :], r * RIM0, RIM0)
+    inner = RIM0 - 1
+    thick = 64 * inner
+    thin = thick + 32 * RIM0
+    corner = thin + 16
+    for face, base, skip in ((from_low, 0, 1), (from_high, RIM0 + rows, 0)):
         for t in range(2):
-            data[r, t] = from_low[2 * r + t]
-            data[RIM0 + rows + r, t] = from_high[2 * r + t]
-        low_at = (rows - RIM0 + r) * RIM0
-        data[r, 2] = unpack_rim(from_low[2 * RIM0], from_low[2 * RIM0 + 1], low_at, RIM0)
-        data[RIM0 + rows + r, 2] = unpack_rim(from_high[2 * RIM0], from_high[2 * RIM0 + 1], r * RIM0, RIM0)
+            for r in range(inner):
+                at = 32 * (2 * r + t)
+                data[base + skip + r, t, 0:32, :] = face[at : at + 32, :]
+                data[base + skip + r, t, 48:56, :] = pair_row(face[thin + 8 * t : thin + 8 * t + 8, :], r)
+            for r in range(RIM0):
+                at = thick + 16 * (2 * r + t)
+                data[base + r, t, 32:48, :] = face[at : at + 16, :]
+        for q in range(NP // 8):
+            for r in range(RIM0):
+                at = RIM0 * (RIM0 * q + r)
+                data[base + r, 2, 8 * q : 8 * q + 8, :] = unpack_rim(
+                    face[corner : corner + 8, :], face[corner + 8 : corner + 16, :], at, RIM0
+                )
 
     half = total // 2 + 1
     make_coefs(data, coef, scaled, diag, 1, half, 1.0, False, UNROLL0[2])
@@ -330,36 +365,45 @@
                     shift = at if side == 0 else at + STRIP1
                     strip = put(strip, coarse[part * group + j, planes, :], shift, STRIP1, at)
                 strips1[side, part, planes, :] = strip
+    inner1 = RIM1 - 1
+    for face, base in enumerate((0, rows // 2 - inner1)):
+        for j in range(0, inner1, 4):
+            edges1[face, 2 * j : 2 * j + 8, :] = pair_rows([coarse[base + j + n, 48:56, :] for n in range(4)])
     for copy in copies:
         copy.wait()
 
 
-def down12_kernel(own, sent, from_low, from_high, piece, w1_out, coef1_out, scaled1_out, w2_out, coef2_out, scaled2_out,
+def down12_kernel(own, left, right, from_low, from_high, piece, w1_out, coef1_out, scaled1_out, w2_out, coef2_out, scaled2_out,
                   data1, diag1, slope1, across1, wa1, coef1, scaled1, data2, diag2, slope2, across2, wa2, coef2, scaled2, sems):
     rows = own.shape[0]
     total = rows + 2 * RIM1
     group = LANES // STRIP1
     parts = rows // group
 
-    def rim(source, base, r):
+    def rim(low, high, base, r):
         part, j = r // group, r % group
-        return unpack_rim(source[base + part], source[base + parts + part], j * STRIP1, STRIP1)
+        at = base + part * NP
+        return unpack_rim(low[at : at + NP, :], high[at : at + NP, :], j * STRIP1, STRIP1)
 
     def copy_row(r):
         data1[RIM1 + r, 0] = own[r]
 
     rows_loop(0, rows, copy_row, 4)
-
-    def copy_rim(r):
-        data1[r, 0] = from_low[r]
-        data1[RIM1 + rows + r, 0] = from_high[r]
-
-    rows_loop(0, RIM1, copy_rim, 1)
     for r in range(rows):
-        data1[RIM1 + r, 1] = rim(sent, RIM1, r)
-    for r in range(RIM1):
-        data1[r, 1] = rim(from_low, RIM1, rows - RIM1 + r)
-        data1[RIM1 + rows + r, 1] = rim(from_high, RIM1, r)
+        data1[RIM1 + r, 1] = rim(left, right, 0, r)
+    inner = RIM1 - 1
+    thick = 32 * inner
+    thin = thick + 16 * RIM1
+    corner = thin + 2 * inner
+    for face, base, skip, first in ((from_low, 0, 1, rows - RIM1), (from_high, RIM1 + rows, 0, 0)):
+        for r in range(inner):
+            data1[base + skip + r, 0, 0:32, :] = face[32 * r : 32 * r + 32, :]
+            at = thin + 8 * (r // 4)
+            data1[base + skip + r, 0, 48:56, :] = pair_row(face[at : at + 8, :], r % 4)
+        for r in range(RIM1):
+            at = thick + 16 * r
+            data1[base + r, 0, 32:48, :] = face[at : at + 16, :]
+            data1[base + r, 1] = rim(face, face.at[pl.ds(parts * NP, face.shape[0] - parts * NP)], corner, first + r)
 
     make_coefs(data1, coef1, scaled1, diag1, 1, total - 1, 0.25, False, UNROLL1[2])
     copies = [copy_rows(coef1, coef1_out, sems.at[0], 10, total - 10)]
@@ -563,11 +607,11 @@
         right = lax.dynamic_index_in_dim(every, jnp.minimum(gy + 1, ny - 1), 0, keepdims=False)[0]
         return jnp.where(gy > 0, left, 0.0), jnp.where(gy < ny - 1, right, 0.0)
 
-    data0, strips0 = pl.pallas_call(
+    data0, strips0, edges0 = pl.pallas_call(
         arrange_kernel,
-        out_shape=(shape(rows, 2, NP, LANES), shape(2, NP, LANES)),
+        out_shape=(shape(rows, 2, NP, LANES), shape(2, NP + 16, LANES), shape(2, 16, LANES)),
         in_specs=[HB] * 5,
-        out_specs=(VM, VM),
+        out_specs=(VM, VM, VM),
         scratch_shapes=[
             pltpu.VMEM((2, 2 * 16 * rows, LANES), F32),
             pltpu.VMEM((2, 16 * rows, LANES), F32),
@@ -582,9 +626,21 @@
         *in_hbm(v.reshape(-1, columns) for v in (misfit, viscosity, friction, ice_mask, grounded))
     )
     left, right = beside(strips0)
-    rims = [left[None], right[None]]
-    low_face = jnp.concatenate([data0[:RIM0].reshape(-1, NP, LANES)] + rims, 0)
-    high_face = jnp.concatenate([data0[rows - RIM0 :].reshape(-1, NP, LANES)] + rims, 0)
+    inner = RIM0 - 1
+
+    def face0(which, first, first_inner):
+        corner = slice(NP + 8 * which, NP + 8 * which + 8)
+        parts = (
+            data0[first_inner : first_inner + inner, :, 0:32],
+            data0[first : first + RIM0, :, 32:48],
+            edges0[which],
+            left[corner],
+            right[corner],
+        )
+        return jnp.concatenate([v.reshape(-1, LANES) for v in parts], 0)
+
+    low_face = face0(0, 0, 0)
+    high_face = face0(1, rows - RIM0, rows - inner)
     from_low = lax.ppermute(high_face, "gx", upward)
     from_high = lax.ppermute(low_face, "gx", downward)
 
@@ -593,25 +649,39 @@
     rows1 = rows // 2
     group = LANES // STRIP1
     field0 = stored(total0, 3, 32, LANES)
-    data1, strips1, w0, coef0, scaled0 = pl.pallas_call(
+    inner1 = RIM1 - 1
+    data1, strips1, edges1, w0, coef0, scaled0 = pl.pallas_call(
         down0_kernel,
         out_shape=(
             shape(rows1, NP, LANES),
             shape(2, rows1 // group, NP, LANES),
+            shape(2, 2 * inner1, LANES),
             field0,
             stored(total0, 3, 8 * NC, LANES),
             field0,
         ),
-        in_specs=[VM] * 4,
-        out_specs=(VM, VM, HB, HB, HB),
+        in_specs=[VM] * 5,
+        out_specs=(VM, VM, VM, HB, HB, HB),
         scratch_shapes=buffers(total0, 3, names) + [pltpu.SemaphoreType.DMA((4,))],
         compiler_params=PARAMS,
         name="down0",
-    )(data0, low_face, from_low, from_high)
+    )(data0, left, right, from_low, from_high)
 
     left, right = beside(strips1)
-    low_face = jnp.concatenate([data1[:RIM1], left, right], 0)
-    high_face = jnp.concatenate([data1[rows1 - RIM1 :], left, right], 0)
+    left, right = left.reshape(-1, LANES), right.reshape(-1, LANES)
+
+    def face1(which, first, first_inner):
+        parts = (
+            data1[first_inner : first_inner + inner1, 0:32],
+            data1[first : first + RIM1, 32:48],
+            edges1[which],
+            left,
+            right,
+        )
+        return jnp.concatenate([v.reshape(-1, LANES) for v in parts], 0)
+
+    low_face = face1(0, 0, 0)
+    high_face = face1(1, rows1 - RIM1, rows1 - inner1)
     from_low = lax.ppermute(high_face, "gx", upward)
     from_high = lax.ppermute(low_face, "gx", downward)
 
@@ -631,12 +701,12 @@
             stored(total2, 1, 8 * NC, LANES),
             field2,
         ),
-        in_specs=[VM] * 4,
+        in_specs=[VM] * 5,
         out_specs=(VM,) + (HB,) * 6,
         scratch_shapes=buffers(total1, 2, names) + buffers(total2, 1, names) + [pltpu.SemaphoreType.DMA((6,))],
         compiler_params=PARAMS,
         name="down12",
-    )(data1, low_face, from_low, from_high)
+    )(data1, left, right, from_low, from_high)
 
     pieces = lax.all_gather(lax.all_to_all(piece, "gx", 0, 0), "gy", axis=0)
 

time: 123 us -> 117 us (0.951)
  waiting for transfers between devices: 39.4 us -> 32.5 us
    ppermute x2, waiting for transfers between devices: 31.4 us -> 13.2 us  [per_device(): from_low = lax.ppermute(high_face, 'gx', upward)]
    ppermute x2, waiting for transfers between devices: 0.01 us -> 11.3 us  [per_device(): from_high = lax.ppermute(low_face, 'gx', downward)]
    all_to_all x1, starting transfers between devices: 7.67 us -> 5.77 us  [per_device(): pieces = lax.all_gather(lax.all_to_all(piece, 'gx', 0, 0), 'gy', axis=0)]
    ppermute x2, starting transfers between devices: 7.93 us -> 9.6 us  [per_device(): from_low = lax.ppermute(high_face, 'gx', upward)]
  transfers between devices with their start and end apart: 5 -> 5, of which waited for: 3 -> 5; matrix products, arithmetic and copies ran while one was open for 1% -> 1% of each run, Pallas kernels for 0% -> 0%
where the time goes in v4:
time: 117 us
  Pallas kernels  41.1 us (35%)
  waiting for transfers between devices  32.5 us (28%)
  blocking collectives  23.9 us (20%)
  starting transfers between devices  18 us (15%)
    pallas_call x1, Pallas kernels, per_device(): pl.pallas_call(up_kernel, out_shape=shape(2 * 16 * rows, columns), in_spe...  20.2 us
    all_gather x2, blocking collectives, beside(): every = lax.all_gather(strips, 'gy', axis=0)  14.2 us
    ppermute x2, waiting for transfers between devices, per_device(): from_low = lax.ppermute(high_face, 'gx', upward)  13.2 us
    ppermute x2, waiting for transfers between devices, per_device(): from_high = lax.ppermute(low_face, 'gx', downward)  11.3 us
    all_gather x1, blocking collectives, per_device(): pieces = lax.all_gather(lax.all_to_all(piece, 'gx', 0, 0), 'gy', axis=0)  9.72 us
    ppermute x2, starting transfers between devices, per_device(): from_low = lax.ppermute(high_face, 'gx', upward)  9.6 us
    pallas_call x1, Pallas kernels, per_device(): pl.pallas_call(down12_kernel, out_shape=(shape(nx, NP, LANES), field1, st...  9.31 us
    all_to_all x1, waiting for transfers between devices, per_device(): pieces = lax.all_gather(lax.all_to_all(piece, 'gx', 0, 0), 'gy', axis=0)  8.05 us
  transfers between devices with their start and end apart: 5, of which 5 were waited for; matrix products, arithmetic and copies ran while one was open for 1% of the time, Pallas kernels for 0%

profile of v4, /device:TPU:0, one launch (start us, length us, event | category | flops | bytes accessed | tf_op | source)
XLA Modules:
  0.0 116.6 jit_solution(575222815059531522)
XLA Ops:
  0.0 3.7 %arrange.1 = (f32[32,2,56,128]{3,2,1,0:T(8,128)S(1)}, f32[2,72,128]{2,1,0:T(8,128)S(1)}, f32[2,16,128]{2,1,0:T(8,128)S(1)}) custom-call(f32[1024,256]{1,0:T(8,128)} %bitcast.51, f32[512,256]{1,0:T(8,128)} %bitcast.55, f32[32,256]{1,0:T(8,128)} %friction_in.1, s32[32,256]{1,0:T(8,128)} %ice_mask_in.1, s32[32,256]{1,0:T(8,128)} %grounded_in.1), custom_call_target="tpu_custom_call" | custom-call | tf_op jit(solution)/shard_map/arrange/pallas_call | solution.py:610
  3.8 7.4 %all-gather = f32[8,72,128]{2,1,0:T(8,128)S(1)} all-gather(f32[2,72,128]{2,1,0:T(8,128)S(1)} %get-tuple-element.22), channel_id=2, replica_groups=mesh['gx'=8,'gy'=4] {'gy'}, dimensions={0}, use_global_device_ids=true | all-gather | bytes 368640 | tf_op jit(solution)/shard_map/all_gather | solution.py:605
  11.3 1.3 %collective-permute-start.1 = (f32[352,128]{1,0:T(8,128)S(1)}, f32[352,128]{1,0:T(8,128)S(1)}, u32[]{:S(2)}, u32[]{:S(2)}) collective-permute-start(f32[352,128]{1,0:T(8,128)S(1)} %get-tuple-element.53), channel_id=1, source_target_pairs={{4,0},{8,4},{12,8},{16,12},{20,16},{24,20},{28,24},{5,1},{9,5},{13... | collective-permute-start | bytes 540680 | tf_op jit(solution)/shard_map/ppermute | solution.py:645
  12.6 4.6 %collective-permute-start = (f32[352,128]{1,0:T(8,128)S(1)}, f32[352,128]{1,0:T(8,128)S(1)}, u32[]{:S(2)}, u32[]{:S(2)}) collective-permute-start(f32[352,128]{1,0:T(8,128)S(1)} %get-tuple-element.54), channel_id=1, source_target_pairs={{0,4},{4,8},{8,12},{12,16},{16,20},{20,24},{24,28},{1,5},{5,9},{9,... | collective-permute-start | bytes 540680 | tf_op jit(solution)/shard_map/ppermute | solution.py:644
  17.1 2.8 %collective-permute-done.1.from_high = f32[352,128]{1,0:T(8,128)S(1)} collective-permute-done((f32[352,128]{1,0:T(8,128)S(1)}, f32[352,128]{1,0:T(8,128)S(1)}, u32[]{:S(2)}, u32[]{:S(2)}) %collective-permute-start.1) | collective-permute-done | bytes 180256 | tf_op jit(solution)/shard_map/ppermute | solution.py:645
  20.0 3.8 %collective-permute-done.from_low = f32[352,128]{1,0:T(8,128)S(1)} collective-permute-done((f32[352,128]{1,0:T(8,128)S(1)}, f32[352,128]{1,0:T(8,128)S(1)}, u32[]{:S(2)}, u32[]{:S(2)}) %collective-permute-start) | collective-permute-done | bytes 180256 | tf_op jit(solution)/shard_map/ppermute | solution.py:644
  23.8 7.9 %down0.1 = (f32[16,56,128]{2,1,0:T(8,128)S(1)}, f32[2,2,56,128]{3,2,1,0:T(8,128)S(1)}, f32[2,24,128]{2,1,0:T(8,128)S(1)}, f32[40,3,32,128]{3,2,1,0:T(8,128)}, f3...) custom-call(f32[32,2,56,128]{3,2,1,0:T(8,128)S(1)} %get-tuple-element.21.own, f32[72,128]{1,0:T(8,128)S(1)} %bitcast.49, ...), custom_call_target="tpu_custom_call" | custom-call | tf_op jit(solution)/shard_map/down0/pallas_call | solution.py:653
  31.7 6.8 %all-gather.1 = f32[8,2,56,128]{3,2,1,0:T(8,128)S(1)} all-gather(f32[2,2,56,128]{3,2,1,0:T(8,128)S(1)} %get-tuple-element.25), channel_id=3, replica_groups=mesh['gx'=8,'gy'=4] {'gy'}, dimensions={0}, use_global_device_ids=true | all-gather | bytes 573440 | tf_op jit(solution)/shard_map/all_gather | solution.py:605
  38.6 1.3 %collective-permute-start.3 = (f32[840,128]{1,0:T(8,128)S(1)}, f32[840,128]{1,0:T(8,128)S(1)}, u32[]{:S(2)}, u32[]{:S(2)}) collective-permute-start(f32[840,128]{1,0:T(8,128)S(1)} %get-tuple-element.49), channel_id=1, source_target_pairs={{4,0},{8,4},{12,8},{16,12},{20,16},{24,20},{28,24},{5,1},{9,5},{13... | collective-permute-start | bytes 1290248 | tf_op jit(solution)/shard_map/ppermute | solution.py:686
  39.9 5.0 %collective-permute-start.2 = (f32[840,128]{1,0:T(8,128)S(1)}, f32[840,128]{1,0:T(8,128)S(1)}, u32[]{:S(2)}, u32[]{:S(2)}) collective-permute-start(f32[840,128]{1,0:T(8,128)S(1)} %get-tuple-element.50), channel_id=1, source_target_pairs={{0,4},{4,8},{8,12},{12,16},{16,20},{20,24},{24,28},{1,5},{5,9},{9,... | collective-permute-start | bytes 1290248 | tf_op jit(solution)/shard_map/ppermute | solution.py:685
  44.9 8.4 %collective-permute-done.3.from_high = f32[840,128]{1,0:T(8,128)S(1)} collective-permute-done((f32[840,128]{1,0:T(8,128)S(1)}, f32[840,128]{1,0:T(8,128)S(1)}, u32[]{:S(2)}, u32[]{:S(2)}) %collective-permute-start.3) | collective-permute-done | bytes 430112 | tf_op jit(solution)/shard_map/ppermute | solution.py:686
  53.4 9.4 %collective-permute-done.2.from_low = f32[840,128]{1,0:T(8,128)S(1)} collective-permute-done((f32[840,128]{1,0:T(8,128)S(1)}, f32[840,128]{1,0:T(8,128)S(1)}, u32[]{:S(2)}, u32[]{:S(2)}) %collective-permute-start.2) | collective-permute-done | bytes 430112 | tf_op jit(solution)/shard_map/ppermute | solution.py:685
  62.8 9.3 %down12.1 = (f32[8,56,128]{2,1,0:T(8,128)}, f32[42,2,32,128]{3,2,1,0:T(8,128)}, f32[42,2,120,128]{3,2,1,0:T(8,128)}, f32[42,2,32,128]{3,2,1,0:T(8,128)}, f32[20,...) custom-call(f32[16,56,128]{2,1,0:T(8,128)S(1)} %get-tuple-element.24.own, ...), custom_call_target="tpu_custom_call" | custom-call | tf_op jit(solution)/shard_map/down12/pallas_call | solution.py:693
  72.1 5.8 %all-to-all-start = ((f32[8,56,128]{2,1,0:T(8,128)}), f32[8,56,128]{2,1,0:T(8,128)S(1)}, u32[]{:S(2)}, u32[]{:S(2)}) async-start(f32[8,56,128]{2,1,0:T(8,128)} %get-tuple-element.27), calls=%async_computation | async-start | bytes 458752 | tf_op jit(solution)/shard_map/all_to_all | solution.py:711
  77.9 0.6 pad_add_fusion.place
  78.5 8.0 %all-to-all-done = f32[8,56,128]{2,1,0:T(8,128)S(1)} async-done(((f32[8,56,128]{2,1,0:T(8,128)}), f32[8,56,128]{2,1,0:T(8,128)S(1)}, u32[]{:S(2)}, u32[]{:S(2)}) %all-to-all-start) | async-done | bytes 229408 | tf_op jit(solution)/shard_map/all_to_all | solution.py:711
  86.5 9.7 %all-gather.2 = f32[32,56,128]{2,1,0:T(8,128)} all-gather(f32[8,56,128]{2,1,0:T(8,128)S(1)} %all-to-all-done), channel_id=4, replica_groups=mesh['gx'=8,'gy'=4] {'gy'}, dimensions={0}, use_global_device_ids=true | all-gather | bytes 1146880 | tf_op jit(solution)/shard_map/all_gather | solution.py:711
  96.2 20.2 %up.1 = f32[1024,256]{1,0:T(8,128)} custom-call(s32[2]{0:T(128)} %pad_add_fusion.place, f32[4,8,56,128]{3,2,1,0:T(8,128)} %bitcast.50, f32[40,3,32,128]{3,2,1,0:T(8,128)} %get-tuple-element.28.w0_in, f32[40,3,120,128]{3,2,1,0:T(8,128)} %get-tuple-element.29.coef0_in, f32[40,3,32,128]{3,2,1,0:T(8,128)} %get-tuple-element.30.scaled0_in, ...), custom_call_target="tpu_custom_call" | custom-call | tf_op jit(solution)/shard_map/up/pallas_call | solution.py:716
  (19 shorter events, 0.2 us)
Async XLA Ops:
  11.3 8.7 %collective-permute-start.1 = (f32[352,128]{1,0:T(8,128)S(1)}, f32[352,128]{1,0:T(8,128)S(1)}, u32[]{:S(2)}, u32[]{:S(2)}) collective-permute-start(f32[352,128]{1,0:T(8,128)S(1)} %get-tuple-element.53), channel_id=1, source_target_pairs={{4,0},{8,4},{12,8},{16,12},{20,16},{24,20},{28,24},{5,1},{9,5},{13... | collective-permute-start | bytes 540680 | tf_op jit(solution)/shard_map/ppermute | solution.py:645
  12.6 11.2 %collective-permute-start = (f32[352,128]{1,0:T(8,128)S(1)}, f32[352,128]{1,0:T(8,128)S(1)}, u32[]{:S(2)}, u32[]{:S(2)}) collective-permute-start(f32[352,128]{1,0:T(8,128)S(1)} %get-tuple-element.54), channel_id=1, source_target_pairs={{0,4},{4,8},{8,12},{12,16},{16,20},{20,24},{24,28},{1,5},{5,9},{9,... | collective-permute-start | bytes 540680 | tf_op jit(solution)/shard_map/ppermute | solution.py:644
  38.6 14.8 %collective-permute-start.3 = (f32[840,128]{1,0:T(8,128)S(1)}, f32[840,128]{1,0:T(8,128)S(1)}, u32[]{:S(2)}, u32[]{:S(2)}) collective-permute-start(f32[840,128]{1,0:T(8,128)S(1)} %get-tuple-element.49), channel_id=1, source_target_pairs={{4,0},{8,4},{12,8},{16,12},{20,16},{24,20},{28,24},{5,1},{9,5},{13... | collective-permute-start | bytes 1290248 | tf_op jit(solution)/shard_map/ppermute | solution.py:686
  39.9 22.9 %collective-permute-start.2 = (f32[840,128]{1,0:T(8,128)S(1)}, f32[840,128]{1,0:T(8,128)S(1)}, u32[]{:S(2)}, u32[]{:S(2)}) collective-permute-start(f32[840,128]{1,0:T(8,128)S(1)} %get-tuple-element.50), channel_id=1, source_target_pairs={{0,4},{4,8},{8,12},{12,16},{16,20},{20,24},{24,28},{1,5},{5,9},{9,... | collective-permute-start | bytes 1290248 | tf_op jit(solution)/shard_map/ppermute | solution.py:685
  72.1 14.4 %all-to-all-start = ((f32[8,56,128]{2,1,0:T(8,128)}), f32[8,56,128]{2,1,0:T(8,128)S(1)}, u32[]{:S(2)}, u32[]{:S(2)}) async-start(f32[8,56,128]{2,1,0:T(8,128)} %get-tuple-element.27), calls=%async_computation | async-start | bytes 458752 | tf_op jit(solution)/shard_map/all_to_all | solution.py:711

commit v5 on v4

--- a/solution.py
+++ b/solution.py
@@ -19,13 +19,16 @@
 RIM3 = 2
 STRIP1 = 16
 NC = 15
+PITCH = 40
 VMEM_DOWN = 28 * 1024 * 1024
 VMEM_UP = 60 * 1024 * 1024
 F32 = jnp.float32
 UNROLL0 = (18, 6, 4)
-UNROLL1 = (18, 6, 4)
+UNROLL1 = (38, 12, 8)
 UNROLL2 = (18, 6, 4)
-UNROLL3 = (32, 32, 2)
+UNROLL3 = (32, 32, 8)
+UNROLL0_UP = (18, 17)
+UNROLL1_UP = (22, 20)
 UNROLL_MOVE = 8
 
 
@@ -150,7 +153,7 @@
 
 
 def sweep(w, new, coef, scaled, slope, across, first, last, closed, unroll, tiles=None, emit=None):
-    look, unroll, _ = unroll
+    look, unroll = unroll[:2]
     nt = w.shape[1]
     prepare(w, coef, slope, across, first - 1, last + 1, closed, look)
 
@@ -167,7 +170,7 @@
 
 
 def remainders(w, out, data, diag, coef, slope, across, first, last, unroll, tiles):
-    look, unroll, _ = unroll
+    look, unroll = unroll[:2]
     prepare(w, coef, slope, across, first - 1, last + 1, False, look)
 
     def row(r):
@@ -249,19 +252,24 @@
                    misfit_half, viscosity_half, friction, ice_mask, grounded, sems):
     rows = friction.shape[0]
     copies = [
-        pltpu.make_async_copy(source, target, sems.at[4 + n])
+        pltpu.make_async_copy(source, target, sems.at[n])
         for n, (source, target) in enumerate(((friction_in, friction), (ice_mask_in, ice_mask), (grounded_in, grounded)))
     ]
     for t in range(2):
         lanes = pl.ds(t * LANES, LANES)
-        copies.append(pltpu.make_async_copy(misfit.at[:, lanes], misfit_half.at[t], sems.at[t]))
-        copies.append(pltpu.make_async_copy(viscosity.at[:, lanes], viscosity_half.at[t], sems.at[2 + t]))
+        for p in range(2):
+            n = 2 * t + p
+            for source, target, sem in ((misfit, misfit_half, 3 + n), (viscosity, viscosity_half, 7 + n)):
+                copies.append(
+                    pltpu.make_async_copy(source.at[:, p, :, lanes], target.at[n, :, pl.ds(0, rows)], sems.at[sem])
+                )
     for copy in copies:
         copy.start()
     for copy in copies:
         copy.wait()
     sub = lax.broadcasted_iota(jnp.int32, (8, LANES), 0)
-    stride = 2 * rows
+    misfit_rows = misfit_half.reshape(4, -1, LANES)
+    viscosity_rows = viscosity_half.reshape(4, -1, LANES)
 
     def eight(i, carry):
         block = pl.ds(pl.multiple_of(8 * i, 8), 8)
@@ -274,10 +282,10 @@
                 ice, drag = ices[j : j + 1], drags[j : j + 1]
                 for c in range(2):
                     for p in range(2):
-                        v = misfit_half[t, pl.ds(c * 16 * rows + p * rows + r, 8, stride=stride), :]
+                        v = misfit_rows[2 * t + p, pl.ds(8 * c * PITCH + r, 8, stride=PITCH), :]
                         data[r, t, 16 * c + 8 * p : 16 * c + 8 * p + 8, :] = v * ice
                 for p in range(2):
-                    data[r, t, 32 + 8 * p : 40 + 8 * p, :] = viscosity_half[t, pl.ds(p * rows + r, 8, stride=stride), :]
+                    data[r, t, 32 + 8 * p : 40 + 8 * p, :] = viscosity_rows[2 * t + p, pl.ds(r, 8, stride=PITCH), :]
                 data[r, t, 48:56, :] = jnp.where(sub == 0, ice, jnp.where(sub == 1, drag, 0.0))
         return carry
 
@@ -470,7 +478,7 @@
             wb3[end, 0] = zero[:32]
             scaled3[end, 0] = zero[:32]
             slope3[end, 0] = zero[:32]
-            coef3[end, 0, 0:16, :] = zero[:16]
+            coef3[end, 0] = jnp.zeros((8 * NC, LANES), F32)
 
     def assemble(d, carry):
         for i in range(rows3):
@@ -484,30 +492,49 @@
     first, last = RIM3, RIM3 + whole
     make_coefs(data3, coef3, scaled3, None, first, last, 0.25 ** (LEVELS - 1), True, UNROLL3[2])
 
-    def coarse_sweep(source, target):
+    gx, gy = place[0], place[1]
+
+    def coarse_sweep(source, target, extent):
+        begin, end = (first, last) if extent is None else (0, extent)
+        start = 0 if extent is None else first + jnp.clip(gx * rows3 - (extent - rows3) // 2, 0, whole - extent)
+        around = 0 if extent is None else 1
+
         def look(r):
+            r = start + r
             norths, souths = shifted([source[r, 0]], True)
             slope3[r, 0] = norths[0] - souths[0]
             across3[r, 0] = twice(coef3[r, 0, 16:32, :]) * norths[0] + twice(coef3[r, 0, 32:48, :]) * souths[0]
 
-        rows_loop(first, last, look, UNROLL3[0])
+        rows_loop(begin - around, end + around, look, UNROLL3[0] if extent is None else extent + 2)
 
         def row(r):
+            r = start + r
             here, total = off_diagonal(source, coef3, slope3, across3, r, 0)
             target[r, 0] = (1.0 - OMEGA) * here + scaled3[r, 0] + coef3[r, 0, 88:120, :] * total
 
-        rows_loop(first, last, row, UNROLL3[1])
-
-    coarse_sweep(scaled3, wa3)
-
-    def two_sweeps(i, carry):
-        coarse_sweep(wa3, wb3)
-        coarse_sweep(wb3, wa3)
-        return carry
-
-    lax.fori_loop(0, (COARSE_ITERS - 2) // 2, two_sweeps, 0)
-
-    gx, gy, = place[0], place[1]
+        rows_loop(begin, end, row, UNROLL3[1])
+
+    coarse_sweep(scaled3, wa3, None)
+    done = 2
+    narrow = [(None, COARSE_ITERS - 9), (rows3 + 20, COARSE_ITERS - 5), (rows3 + 12, COARSE_ITERS)]
+    buffers = (wa3, wb3)
+    for extent, until in narrow:
+        if extent is not None and extent > whole:
+            extent = None
+
+        def two_sweeps(i, carry, extent=extent, pair=buffers):
+            coarse_sweep(pair[0], pair[1], extent)
+            coarse_sweep(pair[1], pair[0], extent)
+            return carry
+
+        if (until - done) // 2:
+            lax.fori_loop(0, (until - done) // 2, two_sweeps, 0)
+        if (until - done) % 2:
+            coarse_sweep(buffers[0], buffers[1], extent)
+            buffers = buffers[::-1]
+        done = until
+    solved = buffers[0]
+
     lane = lane_ids(32)
     y = jnp.where(lane < 96, lane, lane - LANES)
     column = gy * width + (y + LANES) // 2 - LANES // 2
@@ -518,7 +545,7 @@
         copy.wait()
     rows2 = 2 * rows3
     for i in range(rows3 + 2 * RIM3):
-        add = jnp.where(inside, gather_lanes(wa3[gx * rows3 + i, 0], pick), 0.0)
+        add = jnp.where(inside, gather_lanes(solved[gx * rows3 + i, 0], pick), 0.0)
         for r in (2 * i + 2, 2 * i + 3):
             wa2[r, 0] = w2[r, 0] + add
     total2 = rows2 + 2 * RIM2
@@ -537,8 +564,8 @@
 
     rows_loop(4, total2 - 4, add1, UNROLL_MOVE)
     total1 = 2 * rows2 + 2 * RIM1
-    sweep(wa1, wb1, coef1, scaled1, slope1, across1, 11, total1 - 11, False, UNROLL1)
-    sweep(wb1, wa1, coef1, scaled1, slope1, across1, 12, total1 - 12, False, UNROLL1)
+    sweep(wa1, wb1, coef1, scaled1, slope1, across1, 11, total1 - 11, False, UNROLL1_UP)
+    sweep(wb1, wa1, coef1, scaled1, slope1, across1, 12, total1 - 12, False, UNROLL1_UP)
 
 
     for copy in copies[6:]:
@@ -553,17 +580,23 @@
     rows_loop(12, total1 - 12, add0, UNROLL_MOVE)
     rows0 = 4 * rows2
     total0 = rows0 + 2 * RIM0
-    sweep(wa0, wb0, coef0, scaled0, slope0, across0, 3, total0 - 3, False, UNROLL0)
+    sweep(wa0, wb0, coef0, scaled0, slope0, across0, 3, total0 - 3, False, UNROLL0_UP)
+
+    result_rows = result_half.reshape(4, -1, LANES)
 
     def emit(r, t, value):
         for c in range(2):
             for p in range(2):
-                start = c * 16 * rows0 + p * rows0 + r - RIM0
-                result_half[t, pl.ds(start, 8, stride=2 * rows0), :] = value[16 * c + 8 * p : 16 * c + 8 * p + 8]
-
-    sweep(wb0, None, coef0, scaled0, slope0, across0, RIM0, RIM0 + rows0, False, UNROLL0, tiles=2, emit=emit)
+                start = 8 * c * PITCH + r - RIM0
+                result_rows[2 * t + p, pl.ds(start, 8, stride=PITCH), :] = value[16 * c + 8 * p : 16 * c + 8 * p + 8]
+
+    sweep(wb0, None, coef0, scaled0, slope0, across0, RIM0, RIM0 + rows0, False, UNROLL0_UP, tiles=2, emit=emit)
     copies = [
-        pltpu.make_async_copy(result_half.at[t], result.at[:, pl.ds(t * LANES, LANES)], sems.at[t]) for t in range(2)
+        pltpu.make_async_copy(
+            result_half.at[2 * t + p, :, pl.ds(0, rows0)], result.at[:, p, :, pl.ds(t * LANES, LANES)], sems.at[2 * t + p]
+        )
+        for t in range(2)
+        for p in range(2)
     ]
     for copy in copies:
         copy.start()
@@ -613,17 +646,19 @@
         in_specs=[HB] * 5,
         out_specs=(VM, VM, VM),
         scratch_shapes=[
-            pltpu.VMEM((2, 2 * 16 * rows, LANES), F32),
-            pltpu.VMEM((2, 16 * rows, LANES), F32),
+            pltpu.VMEM((4, 16, PITCH, LANES), F32),
+            pltpu.VMEM((4, 8, PITCH, LANES), F32),
             pltpu.VMEM((rows, columns), F32),
             pltpu.VMEM((rows, columns), jnp.int32),
             pltpu.VMEM((rows, columns), jnp.int32),
-            pltpu.SemaphoreType.DMA((7,)),
+            pltpu.SemaphoreType.DMA((11,)),
         ],
         compiler_params=PARAMS,
         name="arrange",
     )(
-        *in_hbm(v.reshape(-1, columns) for v in (misfit, viscosity, friction, ice_mask, grounded))
+        *in_hbm(
+            [v.reshape(-1, 2, rows, columns) for v in (misfit, viscosity)] + [friction, ice_mask, grounded]
+        )
     )
     left, right = beside(strips0)
     inner = RIM0 - 1
@@ -715,7 +750,7 @@
     ups = ("w", "coef", "scaled", "w", "w")
     result = pl.pallas_call(
         up_kernel,
-        out_shape=shape(2 * 16 * rows, columns),
+        out_shape=shape(16, 2, rows, columns),
         in_specs=[SM, VM] + [HB] * 9,
         out_specs=HB,
         scratch_shapes=buffers(total3, 1, ("data", "coef", "scaled", "w", "w", "slope", "across"))
@@ -723,7 +758,7 @@
         + buffers(total1, 2, ups)
         + buffers(total0, 3, ups)
         + buffers(max(total0, total1), 3, ("slope", "across"))
-        + [pltpu.VMEM((2, 2 * 16 * rows, LANES), F32), pltpu.SemaphoreType.DMA((9,))],
+        + [pltpu.VMEM((4, 16, PITCH, LANES), F32), pltpu.SemaphoreType.DMA((9,))],
         compiler_params=pltpu.CompilerParams(vmem_limit_bytes=VMEM_UP),
         name="up",
     )(

time: 117 us -> 112 us (0.957)
  Pallas kernels: 41.1 us -> 36.1 us
    pallas_call x1, Pallas kernels: 20.2 us -> 16.5 us  [per_device(): pl.pallas_call(up_kernel, out_shape=shape(16, 2, rows, columns), in_specs...]
where the time goes in v5:
time: 112 us
  Pallas kernels  36.1 us (32%)
  waiting for transfers between devices  32.5 us (29%)
  blocking collectives  23.9 us (21%)
  starting transfers between devices  18 us (16%)
    pallas_call x1, Pallas kernels, per_device(): pl.pallas_call(up_kernel, out_shape=shape(16, 2, rows, columns), in_specs...  16.5 us
    all_gather x2, blocking collectives, beside(): every = lax.all_gather(strips, 'gy', axis=0)  14.2 us
    ppermute x2, waiting for transfers between devices, per_device(): from_low = lax.ppermute(high_face, 'gx', upward)  13.2 us
    ppermute x2, waiting for transfers between devices, per_device(): from_high = lax.ppermute(low_face, 'gx', downward)  11.3 us
    all_gather x1, blocking collectives, per_device(): pieces = lax.all_gather(lax.all_to_all(piece, 'gx', 0, 0), 'gy', axis=0)  9.72 us
    ppermute x2, starting transfers between devices, per_device(): from_low = lax.ppermute(high_face, 'gx', upward)  9.6 us
    pallas_call x1, Pallas kernels, per_device(): pl.pallas_call(down12_kernel, out_shape=(shape(nx, NP, LANES), field1, st...  8.62 us
    all_to_all x1, waiting for transfers between devices, per_device(): pieces = lax.all_gather(lax.all_to_all(piece, 'gx', 0, 0), 'gy', axis=0)  8.05 us
  transfers between devices with their start and end apart: 5, of which 5 were waited for; matrix products, arithmetic and copies ran while one was open for 1% of the time, Pallas kernels for 0%

profile of v5, /device:TPU:0, one launch (start us, length us, event | category | flops | bytes accessed | tf_op | source)
XLA Modules:
  0.0 111.6 jit_solution(12470009436816882267)
XLA Ops:
  0.0 3.1 %arrange.1 = (f32[32,2,56,128]{3,2,1,0:T(8,128)S(1)}, f32[2,72,128]{2,1,0:T(8,128)S(1)}, f32[2,16,128]{2,1,0:T(8,128)S(1)}) custom-call(f32[16,2,32,256]{3,2,1,0:T(8,128)} %bitcast.51, f32[8,2,32,256]{3,2,1,0:T(8,128)} %bitcast.55, f32[32,256]{1,0:T(8,128)} %friction_in.1, s32[32,256]{1,0:T(8,128)} %ice_mask_in.1, s32[32,256]{1,0:T(8,128)} %grounded_in.1), custom_call_target="tpu_custom_call" | custom-call | tf_op jit(solution)/shard_map/arrange/pallas_call | solution.py:643
  3.2 7.4 %all-gather = f32[8,72,128]{2,1,0:T(8,128)S(1)} all-gather(f32[2,72,128]{2,1,0:T(8,128)S(1)} %get-tuple-element.22), channel_id=2, replica_groups=mesh['gx'=8,'gy'=4] {'gy'}, dimensions={0}, use_global_device_ids=true | all-gather | bytes 368640 | tf_op jit(solution)/shard_map/all_gather | solution.py:638
  10.7 1.3 %collective-permute-start.1 = (f32[352,128]{1,0:T(8,128)S(1)}, f32[352,128]{1,0:T(8,128)S(1)}, u32[]{:S(2)}, u32[]{:S(2)}) collective-permute-start(f32[352,128]{1,0:T(8,128)S(1)} %get-tuple-element.53), channel_id=1, source_target_pairs={{4,0},{8,4},{12,8},{16,12},{20,16},{24,20},{28,24},{5,1},{9,5},{13... | collective-permute-start | bytes 540680 | tf_op jit(solution)/shard_map/ppermute | solution.py:680
  12.0 4.6 %collective-permute-start = (f32[352,128]{1,0:T(8,128)S(1)}, f32[352,128]{1,0:T(8,128)S(1)}, u32[]{:S(2)}, u32[]{:S(2)}) collective-permute-start(f32[352,128]{1,0:T(8,128)S(1)} %get-tuple-element.54), channel_id=1, source_target_pairs={{0,4},{4,8},{8,12},{12,16},{16,20},{20,24},{24,28},{1,5},{5,9},{9,... | collective-permute-start | bytes 540680 | tf_op jit(solution)/shard_map/ppermute | solution.py:679
  16.6 2.8 %collective-permute-done.1.from_high = f32[352,128]{1,0:T(8,128)S(1)} collective-permute-done((f32[352,128]{1,0:T(8,128)S(1)}, f32[352,128]{1,0:T(8,128)S(1)}, u32[]{:S(2)}, u32[]{:S(2)}) %collective-permute-start.1) | collective-permute-done | bytes 180256 | tf_op jit(solution)/shard_map/ppermute | solution.py:680
  19.4 3.8 %collective-permute-done.from_low = f32[352,128]{1,0:T(8,128)S(1)} collective-permute-done((f32[352,128]{1,0:T(8,128)S(1)}, f32[352,128]{1,0:T(8,128)S(1)}, u32[]{:S(2)}, u32[]{:S(2)}) %collective-permute-start) | collective-permute-done | bytes 180256 | tf_op jit(solution)/shard_map/ppermute | solution.py:679
  23.2 7.9 %down0.1 = (f32[16,56,128]{2,1,0:T(8,128)S(1)}, f32[2,2,56,128]{3,2,1,0:T(8,128)S(1)}, f32[2,24,128]{2,1,0:T(8,128)S(1)}, f32[40,3,32,128]{3,2,1,0:T(8,128)}, f3...) custom-call(f32[32,2,56,128]{3,2,1,0:T(8,128)S(1)} %get-tuple-element.21.own, f32[72,128]{1,0:T(8,128)S(1)} %bitcast.49, ...), custom_call_target="tpu_custom_call" | custom-call | tf_op jit(solution)/shard_map/down0/pallas_call | solution.py:688
  31.1 6.8 %all-gather.1 = f32[8,2,56,128]{3,2,1,0:T(8,128)S(1)} all-gather(f32[2,2,56,128]{3,2,1,0:T(8,128)S(1)} %get-tuple-element.25), channel_id=3, replica_groups=mesh['gx'=8,'gy'=4] {'gy'}, dimensions={0}, use_global_device_ids=true | all-gather | bytes 573440 | tf_op jit(solution)/shard_map/all_gather | solution.py:638
  38.0 1.3 %collective-permute-start.3 = (f32[840,128]{1,0:T(8,128)S(1)}, f32[840,128]{1,0:T(8,128)S(1)}, u32[]{:S(2)}, u32[]{:S(2)}) collective-permute-start(f32[840,128]{1,0:T(8,128)S(1)} %get-tuple-element.49), channel_id=1, source_target_pairs={{4,0},{8,4},{12,8},{16,12},{20,16},{24,20},{28,24},{5,1},{9,5},{13... | collective-permute-start | bytes 1290248 | tf_op jit(solution)/shard_map/ppermute | solution.py:721
  39.3 5.0 %collective-permute-start.2 = (f32[840,128]{1,0:T(8,128)S(1)}, f32[840,128]{1,0:T(8,128)S(1)}, u32[]{:S(2)}, u32[]{:S(2)}) collective-permute-start(f32[840,128]{1,0:T(8,128)S(1)} %get-tuple-element.50), channel_id=1, source_target_pairs={{0,4},{4,8},{8,12},{12,16},{16,20},{20,24},{24,28},{1,5},{5,9},{9,... | collective-permute-start | bytes 1290248 | tf_op jit(solution)/shard_map/ppermute | solution.py:720
  44.3 8.4 %collective-permute-done.3.from_high = f32[840,128]{1,0:T(8,128)S(1)} collective-permute-done((f32[840,128]{1,0:T(8,128)S(1)}, f32[840,128]{1,0:T(8,128)S(1)}, u32[]{:S(2)}, u32[]{:S(2)}) %collective-permute-start.3) | collective-permute-done | bytes 430112 | tf_op jit(solution)/shard_map/ppermute | solution.py:721
  52.8 9.4 %collective-permute-done.2.from_low = f32[840,128]{1,0:T(8,128)S(1)} collective-permute-done((f32[840,128]{1,0:T(8,128)S(1)}, f32[840,128]{1,0:T(8,128)S(1)}, u32[]{:S(2)}, u32[]{:S(2)}) %collective-permute-start.2) | collective-permute-done | bytes 430112 | tf_op jit(solution)/shard_map/ppermute | solution.py:720
  62.2 8.6 %down12.1 = (f32[8,56,128]{2,1,0:T(8,128)}, f32[42,2,32,128]{3,2,1,0:T(8,128)}, f32[42,2,120,128]{3,2,1,0:T(8,128)}, f32[42,2,32,128]{3,2,1,0:T(8,128)}, f32[20,...) custom-call(f32[16,56,128]{2,1,0:T(8,128)S(1)} %get-tuple-element.24.own, ...), custom_call_target="tpu_custom_call" | custom-call | tf_op jit(solution)/shard_map/down12/pallas_call | solution.py:728
  70.8 5.8 %all-to-all-start = ((f32[8,56,128]{2,1,0:T(8,128)}), f32[8,56,128]{2,1,0:T(8,128)S(1)}, u32[]{:S(2)}, u32[]{:S(2)}) async-start(f32[8,56,128]{2,1,0:T(8,128)} %get-tuple-element.27), calls=%async_computation | async-start | bytes 458752 | tf_op jit(solution)/shard_map/all_to_all | solution.py:746
  76.6 0.6 pad_add_fusion.place
  77.2 8.0 %all-to-all-done = f32[8,56,128]{2,1,0:T(8,128)S(1)} async-done(((f32[8,56,128]{2,1,0:T(8,128)}), f32[8,56,128]{2,1,0:T(8,128)S(1)}, u32[]{:S(2)}, u32[]{:S(2)}) %all-to-all-start) | async-done | bytes 229408 | tf_op jit(solution)/shard_map/all_to_all | solution.py:746
  85.2 9.7 %all-gather.2 = f32[32,56,128]{2,1,0:T(8,128)} all-gather(f32[8,56,128]{2,1,0:T(8,128)S(1)} %all-to-all-done), channel_id=4, replica_groups=mesh['gx'=8,'gy'=4] {'gy'}, dimensions={0}, use_global_device_ids=true | all-gather | bytes 1146880 | tf_op jit(solution)/shard_map/all_gather | solution.py:746
  95.0 16.5 %up.1 = f32[16,2,32,256]{3,2,1,0:T(8,128)} custom-call(s32[2]{0:T(128)} %pad_add_fusion.place, f32[4,8,56,128]{3,2,1,0:T(8,128)} %bitcast.50, f32[40,3,32,128]{3,2,1,0:T(8,128)} %get-tuple-element.28.w0_in, f32[40,3,120,128]{3,2,1,0:T(8,128)} %get-tuple-element.29.coef0_in, f32[40,3,32,128]{3,2,1,0:T(8,128)} %get-tuple-element.30.scaled0_in, ...), custom_call_target="tpu_custom_call" | custom-call | tf_op jit(solution)/shard_map/up/pallas_call | solution.py:751
  (19 shorter events, 0.2 us)
Async XLA Ops:
  10.7 8.7 %collective-permute-start.1 = (f32[352,128]{1,0:T(8,128)S(1)}, f32[352,128]{1,0:T(8,128)S(1)}, u32[]{:S(2)}, u32[]{:S(2)}) collective-permute-start(f32[352,128]{1,0:T(8,128)S(1)} %get-tuple-element.53), channel_id=1, source_target_pairs={{4,0},{8,4},{12,8},{16,12},{20,16},{24,20},{28,24},{5,1},{9,5},{13... | collective-permute-start | bytes 540680 | tf_op jit(solution)/shard_map/ppermute | solution.py:680
  12.0 11.2 %collective-permute-start = (f32[352,128]{1,0:T(8,128)S(1)}, f32[352,128]{1,0:T(8,128)S(1)}, u32[]{:S(2)}, u32[]{:S(2)}) collective-permute-start(f32[352,128]{1,0:T(8,128)S(1)} %get-tuple-element.54), channel_id=1, source_target_pairs={{0,4},{4,8},{8,12},{12,16},{16,20},{20,24},{24,28},{1,5},{5,9},{9,... | collective-permute-start | bytes 540680 | tf_op jit(solution)/shard_map/ppermute | solution.py:679
  38.0 14.8 %collective-permute-start.3 = (f32[840,128]{1,0:T(8,128)S(1)}, f32[840,128]{1,0:T(8,128)S(1)}, u32[]{:S(2)}, u32[]{:S(2)}) collective-permute-start(f32[840,128]{1,0:T(8,128)S(1)} %get-tuple-element.49), channel_id=1, source_target_pairs={{4,0},{8,4},{12,8},{16,12},{20,16},{24,20},{28,24},{5,1},{9,5},{13... | collective-permute-start | bytes 1290248 | tf_op jit(solution)/shard_map/ppermute | solution.py:721
  39.3 22.9 %collective-permute-start.2 = (f32[840,128]{1,0:T(8,128)S(1)}, f32[840,128]{1,0:T(8,128)S(1)}, u32[]{:S(2)}, u32[]{:S(2)}) collective-permute-start(f32[840,128]{1,0:T(8,128)S(1)} %get-tuple-element.50), channel_id=1, source_target_pairs={{0,4},{4,8},{8,12},{12,16},{16,20},{20,24},{24,28},{1,5},{5,9},{9,... | collective-permute-start | bytes 1290248 | tf_op jit(solution)/shard_map/ppermute | solution.py:720
  70.8 14.4 %all-to-all-start = ((f32[8,56,128]{2,1,0:T(8,128)}), f32[8,56,128]{2,1,0:T(8,128)S(1)}, u32[]{:S(2)}, u32[]{:S(2)}) async-start(f32[8,56,128]{2,1,0:T(8,128)} %get-tuple-element.27), calls=%async_computation | async-start | bytes 458752 | tf_op jit(solution)/shard_map/all_to_all | solution.py:746

commit v6 on v5

--- a/solution.py
+++ b/solution.py
@@ -20,6 +20,7 @@
 STRIP1 = 16
 NC = 15
 PITCH = 40
+SPAN = 11
 VMEM_DOWN = 28 * 1024 * 1024
 VMEM_UP = 60 * 1024 * 1024
 F32 = jnp.float32
@@ -311,57 +312,106 @@
         edges[1, 8 * t : 8 * t + 8, :] = pair_rows([data[rows - RIM0 + 1 + r, t, 48:56, :] for r in range(RIM0 - 1)])
 
 
-def down0_kernel(own, left, right, from_low, from_high, coarse, strips1, edges1, w_out, coef_out, scaled_out,
-                 data, diag, slope, across, wa, coef, scaled, sems):
+def inner0_kernel(own, left, right, coarse, w_out, coef_out, scaled_out, data, diag, slope, across, wa, coef, scaled, sems):
     rows = own.shape[0]
-    total = rows + 2 * RIM0
+    first, last = RIM0, RIM0 + rows
 
     def copy_row(r):
         for t in range(2):
-            data[RIM0 + r, t] = own[r, t]
+            data[first + r, t] = own[r, t]
 
     rows_loop(0, rows, copy_row, 4)
     for r in range(rows):
-        data[RIM0 + r, 2] = unpack_rim(left[0:NP, :], right[0:NP, :], r * RIM0, RIM0)
+        data[first + r, 2] = unpack_rim(left[0:NP, :], right[0:NP, :], r * RIM0, RIM0)
+    half = first + rows // 2 - 1
+    make_coefs(data, coef, scaled, diag, first + 1, half, 1.0, False, UNROLL0[2])
+    copies = [copy_rows(coef, coef_out, sems.at[0], first + 1, half)]
+    make_coefs(data, coef, scaled, diag, half, last - 1, 1.0, False, UNROLL0[2])
+    copies.append(copy_rows(coef, coef_out, sems.at[1], half, last - 1))
+    copies.append(copy_rows(scaled, scaled_out, sems.at[2], first + 1, last - 1))
+    sweep(scaled, wa, coef, scaled, slope, across, first + 2, last - 2, False, UNROLL0)
+    copies.append(copy_rows(wa, w_out, sems.at[3], first + 2, last - 2))
+
+    def coefs_row(i):
+        coarse[i, 32:56, :] = restrict_row(data, slice(32, 56), first + 2 * i)
+
+    rows_loop(0, rows // 2, coefs_row, UNROLL_MOVE)
+    remainders(wa, diag, data, diag, coef, slope, across, first + 3, last - 3, UNROLL0, 2)
+
+    def target_row(i):
+        coarse[i, 0:32, :] = restrict_row(diag, slice(0, 32), first + 2 * i)
+
+    rows_loop(2, rows // 2 - 2, target_row, UNROLL_MOVE)
+    for copy in copies:
+        copy.wait()
+
+
+def outer0_kernel(own, left, right, from_low, from_high, inner_coarse, w_in, coef_in, scaled_in,
+                  coarse, strips1, edges1, w_out, coef_out, scaled_out,
+                  data, diag, slope, across, wa, coef, scaled, sems):
+    rows = own.shape[0]
+    mine = SPAN - RIM0
     inner = RIM0 - 1
     thick = 64 * inner
     thin = thick + 32 * RIM0
     corner = thin + 16
-    for face, base, skip in ((from_low, 0, 1), (from_high, RIM0 + rows, 0)):
+    copies = []
+    for face, start, rim_at, mine_at, x in (
+        (from_low, 0, 0, RIM0, 0),
+        (from_high, SPAN, SPAN + mine, SPAN, rows - mine),
+    ):
+        for r in range(mine):
+            for t in range(2):
+                data[mine_at + r, t] = own[x + r, t]
+            data[mine_at + r, 2] = unpack_rim(left[0:NP, :], right[0:NP, :], (x + r) * RIM0, RIM0)
+        skip = 1 if start == 0 else 0
         for t in range(2):
             for r in range(inner):
                 at = 32 * (2 * r + t)
-                data[base + skip + r, t, 0:32, :] = face[at : at + 32, :]
-                data[base + skip + r, t, 48:56, :] = pair_row(face[thin + 8 * t : thin + 8 * t + 8, :], r)
+                data[rim_at + skip + r, t, 0:32, :] = face[at : at + 32, :]
+                data[rim_at + skip + r, t, 48:56, :] = pair_row(face[thin + 8 * t : thin + 8 * t + 8, :], r)
             for r in range(RIM0):
                 at = thick + 16 * (2 * r + t)
-                data[base + r, t, 32:48, :] = face[at : at + 16, :]
+                data[rim_at + r, t, 32:48, :] = face[at : at + 16, :]
         for q in range(NP // 8):
             for r in range(RIM0):
                 at = RIM0 * (RIM0 * q + r)
-                data[base + r, 2, 8 * q : 8 * q + 8, :] = unpack_rim(
+                data[rim_at + r, 2, 8 * q : 8 * q + 8, :] = unpack_rim(
                     face[corner : corner + 8, :], face[corner + 8 : corner + 16, :], at, RIM0
                 )
-
-    half = total // 2 + 1
-    make_coefs(data, coef, scaled, diag, 1, half, 1.0, False, UNROLL0[2])
-    copies = [copy_rows(coef, coef_out, sems.at[0], 2, half)]
-    make_coefs(data, coef, scaled, diag, half, total - 1, 1.0, False, UNROLL0[2])
-    copies.append(copy_rows(coef, coef_out, sems.at[1], half, total - 2))
-    copies.append(copy_rows(scaled, scaled_out, sems.at[2], 3, total - 3))
-    sweep(scaled, wa, coef, scaled, slope, across, 2, total - 2, False, UNROLL0)
-    copies.append(copy_rows(wa, w_out, sems.at[3], 2, total - 2))
-
-    def coefs_row(i):
-        coarse[i, 32:56, :] = restrict_row(data, slice(32, 56), RIM0 + 2 * i)
-
-    rows_loop(0, rows // 2, coefs_row, UNROLL_MOVE)
-    remainders(wa, diag, data, diag, coef, slope, across, RIM0, RIM0 + rows, UNROLL0, 2)
-
-    def target_row(i):
+    for start in (0, SPAN):
+        make_coefs(data, coef, scaled, diag, start + 1, start + SPAN - 1, 1.0, False, 9)
+    total = rows + 2 * RIM0
+    shift = total - 2 * SPAN
+    ranges = ((2, RIM0 + 1), (3, RIM0 + 1), (2, RIM0 + 2))
+    arrays = ((coef, coef_out), (scaled, scaled_out), (wa, w_out))
+
+    def store(n):
+        (source, target), (low, high) = arrays[n], ranges[n]
+        for side in range(2):
+            begin = low if side == 0 else 2 * SPAN - high
+            place = begin + (0 if side == 0 else shift)
+            copy = pltpu.make_async_copy(
+                source.at[pl.ds(begin, high - low)], target.at[pl.ds(place, high - low)], sems.at[2 * n + side]
+            )
+            copy.start()
+            copies.append(copy)
+
+    store(0)
+    store(1)
+    for start in (0, SPAN):
+        sweep(scaled, wa, coef, scaled, slope, across, start + 2, start + SPAN - 2, False, (9, 7))
+    store(2)
+
+    def copy_coarse(i):
+        coarse[i] = inner_coarse[i]
+
+    rows_loop(0, rows // 2, copy_coarse, 4)
+    for start in (0, SPAN):
+        remainders(wa, diag, data, diag, coef, slope, across, start + 3, start + SPAN - 3, (7, 5), 2)
+    for i in range(2):
         coarse[i, 0:32, :] = restrict_row(diag, slice(0, 32), RIM0 + 2 * i)
-
-    rows_loop(0, rows // 2, target_row, UNROLL_MOVE)
+        coarse[rows // 2 - 2 + i, 0:32, :] = restrict_row(diag, slice(0, 32), SPAN + mine - 4 + 2 * i)
     group = LANES // STRIP1
     for side in range(2):
         for part in range(rows // 2 // group):
@@ -370,8 +420,8 @@
                 strip = jnp.zeros((8, LANES), F32)
                 for j in range(group):
                     at = j * STRIP1
-                    shift = at if side == 0 else at + STRIP1
-                    strip = put(strip, coarse[part * group + j, planes, :], shift, STRIP1, at)
+                    shift1 = at if side == 0 else at + STRIP1
+                    strip = put(strip, coarse[part * group + j, planes, :], shift1, STRIP1, at)
                 strips1[side, part, planes, :] = strip
     inner1 = RIM1 - 1
     for face, base in enumerate((0, rows // 2 - inner1)):
@@ -684,23 +734,33 @@
     rows1 = rows // 2
     group = LANES // STRIP1
     field0 = stored(total0, 3, 32, LANES)
+    up0 = (field0, stored(total0, 3, 8 * NC, LANES), field0)
     inner1 = RIM1 - 1
+    inner_coarse, *ups0 = pl.pallas_call(
+        inner0_kernel,
+        out_shape=(shape(rows1, NP, LANES),) + up0,
+        in_specs=[VM] * 3,
+        out_specs=(VM, HB, HB, HB),
+        scratch_shapes=buffers(total0, 3, names) + [pltpu.SemaphoreType.DMA((4,))],
+        compiler_params=PARAMS,
+        cost_estimate=pl.CostEstimate(flops=40_000_000, bytes_accessed=20_000_000, transcendentals=0),
+        name="inner0",
+    )(data0, left, right)
     data1, strips1, edges1, w0, coef0, scaled0 = pl.pallas_call(
-        down0_kernel,
+        outer0_kernel,
         out_shape=(
             shape(rows1, NP, LANES),
             shape(2, rows1 // group, NP, LANES),
             shape(2, 2 * inner1, LANES),
-            field0,
-            stored(total0, 3, 8 * NC, LANES),
-            field0,
-        ),
-        in_specs=[VM] * 5,
+        )
+        + up0,
+        in_specs=[VM] * 6 + [HB] * 3,
         out_specs=(VM, VM, VM, HB, HB, HB),
-        scratch_shapes=buffers(total0, 3, names) + [pltpu.SemaphoreType.DMA((4,))],
+        input_output_aliases={6: 3, 7: 4, 8: 5},
+        scratch_shapes=buffers(2 * SPAN, 3, names) + [pltpu.SemaphoreType.DMA((6,))],
         compiler_params=PARAMS,
-        name="down0",
-    )(data0, left, right, from_low, from_high)
+        name="outer0",
+    )(data0, left, right, from_low, from_high, inner_coarse, *in_hbm(ups0))
 
     left, right = beside(strips1)
     left, right = left.reshape(-1, LANES), right.reshape(-1, LANES)

time: 112 us -> 107 us (0.955)
  waiting for transfers between devices: 32.5 us -> 26.1 us
  Pallas kernels: 36.1 us -> 37.4 us
    ppermute x2, waiting for transfers between devices: 13.2 us -> 9.61 us  [per_device(): from_low = lax.ppermute(high_face, 'gx', upward)]
    ppermute x2, waiting for transfers between devices: 11.3 us -> 8.45 us  [per_device(): from_high = lax.ppermute(low_face, 'gx', downward)]
    pallas_call x1 -> x2, Pallas kernels: 7.85 us -> 9.19 us  [the longest x1 6.37 us: per_device(): pl.pallas_call(inner0_kernel, out_shape=(shape(rows1, NP, LANES),) + up0,...]
  transfers between devices with their start and end apart: 5 -> 5, of which waited for: 5 -> 4; matrix products, arithmetic and copies ran while one was open for 1% -> 1% of each run, Pallas kernels for 0% -> 6%
where the time goes in v6:
time: 107 us
  Pallas kernels  37.4 us (35%)
  waiting for transfers between devices  26.1 us (24%)
  blocking collectives  23.9 us (22%)
  starting transfers between devices  18 us (17%)
    pallas_call x1, Pallas kernels, per_device(): pl.pallas_call(up_kernel, out_shape=shape(16, 2, rows, columns), in_specs...  16.5 us
    all_gather x2, blocking collectives, beside(): every = lax.all_gather(strips, 'gy', axis=0)  14.2 us
    all_gather x1, blocking collectives, per_device(): pieces = lax.all_gather(lax.all_to_all(piece, 'gx', 0, 0), 'gy', axis=0)  9.72 us
    ppermute x2, waiting for transfers between devices, per_device(): from_low = lax.ppermute(high_face, 'gx', upward)  9.61 us
    ppermute x2, starting transfers between devices, per_device(): from_low = lax.ppermute(high_face, 'gx', upward)  9.6 us
    pallas_call x1, Pallas kernels, per_device(): pl.pallas_call(down12_kernel, out_shape=(shape(nx, NP, LANES), field1, st...  8.61 us
    ppermute x2, waiting for transfers between devices, per_device(): from_high = lax.ppermute(low_face, 'gx', downward)  8.45 us
    all_to_all x1, waiting for transfers between devices, per_device(): pieces = lax.all_gather(lax.all_to_all(piece, 'gx', 0, 0), 'gy', axis=0)  8.04 us
  transfers between devices with their start and end apart: 5, of which 4 were waited for; matrix products, arithmetic and copies ran while one was open for 1% of the time, Pallas kernels for 6%

profile of v6, /device:TPU:0, one launch (start us, length us, event | category | flops | bytes accessed | tf_op | source)
XLA Modules:
  0.0 106.6 jit_solution(6192688676479850889)
XLA Ops:
  0.0 3.1 %arrange.1 = (f32[32,2,56,128]{3,2,1,0:T(8,128)S(1)}, f32[2,72,128]{2,1,0:T(8,128)S(1)}, f32[2,16,128]{2,1,0:T(8,128)S(1)}) custom-call(f32[16,2,32,256]{3,2,1,0:T(8,128)} %bitcast.53, f32[8,2,32,256]{3,2,1,0:T(8,128)} %bitcast.57, f32[32,256]{1,0:T(8,128)} %friction_in.1, s32[32,256]{1,0:T(8,128)} %ice_mask_in.1, s32[32,256]{1,0:T(8,128)} %grounded_in.1), custom_call_target="tpu_custom_call" | custom-call | tf_op jit(solution)/shard_map/arrange/pallas_call | solution.py:693
  3.2 7.4 %all-gather = f32[8,72,128]{2,1,0:T(8,128)S(1)} all-gather(f32[2,72,128]{2,1,0:T(8,128)S(1)} %get-tuple-element.26), channel_id=2, replica_groups=mesh['gx'=8,'gy'=4] {'gy'}, dimensions={0}, use_global_device_ids=true | all-gather | bytes 368640 | tf_op jit(solution)/shard_map/all_gather | solution.py:688
  10.7 1.3 %collective-permute-start.1 = (f32[352,128]{1,0:T(8,128)S(1)}, f32[352,128]{1,0:T(8,128)S(1)}, u32[]{:S(2)}, u32[]{:S(2)}) collective-permute-start(f32[352,128]{1,0:T(8,128)S(1)} %get-tuple-element.61), channel_id=1, source_target_pairs={{4,0},{8,4},{12,8},{16,12},{20,16},{24,20},{28,24},{5,1},{9,5},{13... | collective-permute-start | bytes 540680 | tf_op jit(solution)/shard_map/ppermute | solution.py:730
  12.0 4.6 %collective-permute-start = (f32[352,128]{1,0:T(8,128)S(1)}, f32[352,128]{1,0:T(8,128)S(1)}, u32[]{:S(2)}, u32[]{:S(2)}) collective-permute-start(f32[352,128]{1,0:T(8,128)S(1)} %get-tuple-element.62), channel_id=1, source_target_pairs={{0,4},{4,8},{8,12},{12,16},{16,20},{20,24},{24,28},{1,5},{5,9},{9,... | collective-permute-start | bytes 540680 | tf_op jit(solution)/shard_map/ppermute | solution.py:729
  16.6 6.4 %inner0.1 = (f32[16,56,128]{2,1,0:T(8,128)S(1)}, f32[40,3,32,128]{3,2,1,0:T(8,128)}, f32[40,3,120,128]{3,2,1,0:T(8,128)}, f32[40,3,32,128]{3,2,1,0:T(8,128)}) custom-call(f32[32,2,56,128]{3,2,1,0:T(8,128)S(1)} %get-tuple-element.25.own, f32[72,128]{1,0:T(8,128)S(1)} %bitcast.50, f32[72,128]{1,0:T(8,128)S(1)} %bitcast.48), custom_call_target="tpu_custom_call" | custom-call | flops 40000000 | bytes 20000000 | tf_op jit(solution)/shard_map/inner0/pallas_call | solution.py:739
  22.9 0.0 collective-permute-done.1.from_high
  22.9 0.2 collective-permute-done.from_low
  23.2 2.8 %outer0.1 = (f32[16,56,128]{2,1,0:T(8,128)S(1)}, f32[2,2,56,128]{3,2,1,0:T(8,128)S(1)}, f32[2,24,128]{2,1,0:T(8,128)S(1)}, f32[40,3,32,128]{3,2,1,0:T(8,128)}, f...) custom-call(f32[32,2,56,128]{3,2,1,0:T(8,128)S(1)} %get-tuple-elemen, ...), custom_call_target="tpu_custom_call", output_to_operand_aliasing={{3}: (6, {}), {4}: (7, {}), {5}: (8, {})} | custom-call | tf_op jit(solution)/shard_map/outer0/pallas_call | solution.py:749
  26.1 6.8 %all-gather.1 = f32[8,2,56,128]{3,2,1,0:T(8,128)S(1)} all-gather(f32[2,2,56,128]{3,2,1,0:T(8,128)S(1)} %get-tuple-element.33), channel_id=3, replica_groups=mesh['gx'=8,'gy'=4] {'gy'}, dimensions={0}, use_global_device_ids=true | all-gather | bytes 573440 | tf_op jit(solution)/shard_map/all_gather | solution.py:688
  33.0 1.3 %collective-permute-start.3 = (f32[840,128]{1,0:T(8,128)S(1)}, f32[840,128]{1,0:T(8,128)S(1)}, u32[]{:S(2)}, u32[]{:S(2)}) collective-permute-start(f32[840,128]{1,0:T(8,128)S(1)} %get-tuple-element.57), channel_id=1, source_target_pairs={{4,0},{8,4},{12,8},{16,12},{20,16},{24,20},{28,24},{5,1},{9,5},{13... | collective-permute-start | bytes 1290248 | tf_op jit(solution)/shard_map/ppermute | solution.py:781
  34.3 5.0 %collective-permute-start.2 = (f32[840,128]{1,0:T(8,128)S(1)}, f32[840,128]{1,0:T(8,128)S(1)}, u32[]{:S(2)}, u32[]{:S(2)}) collective-permute-start(f32[840,128]{1,0:T(8,128)S(1)} %get-tuple-element.58), channel_id=1, source_target_pairs={{0,4},{4,8},{8,12},{12,16},{16,20},{20,24},{24,28},{1,5},{5,9},{9,... | collective-permute-start | bytes 1290248 | tf_op jit(solution)/shard_map/ppermute | solution.py:780
  39.3 8.4 %collective-permute-done.3.from_high = f32[840,128]{1,0:T(8,128)S(1)} collective-permute-done((f32[840,128]{1,0:T(8,128)S(1)}, f32[840,128]{1,0:T(8,128)S(1)}, u32[]{:S(2)}, u32[]{:S(2)}) %collective-permute-start.3) | collective-permute-done | bytes 430112 | tf_op jit(solution)/shard_map/ppermute | solution.py:781
  47.8 9.4 %collective-permute-done.2.from_low = f32[840,128]{1,0:T(8,128)S(1)} collective-permute-done((f32[840,128]{1,0:T(8,128)S(1)}, f32[840,128]{1,0:T(8,128)S(1)}, u32[]{:S(2)}, u32[]{:S(2)}) %collective-permute-start.2) | collective-permute-done | bytes 430112 | tf_op jit(solution)/shard_map/ppermute | solution.py:780
  57.2 8.6 %down12.1 = (f32[8,56,128]{2,1,0:T(8,128)}, f32[42,2,32,128]{3,2,1,0:T(8,128)}, f32[42,2,120,128]{3,2,1,0:T(8,128)}, f32[42,2,32,128]{3,2,1,0:T(8,128)}, f32[20,...) custom-call(f32[16,56,128]{2,1,0:T(8,128)S(1)} %get-tuple-element.32.own, ...), custom_call_target="tpu_custom_call" | custom-call | tf_op jit(solution)/shard_map/down12/pallas_call | solution.py:788
  65.8 5.8 %all-to-all-start = ((f32[8,56,128]{2,1,0:T(8,128)}), f32[8,56,128]{2,1,0:T(8,128)S(1)}, u32[]{:S(2)}, u32[]{:S(2)}) async-start(f32[8,56,128]{2,1,0:T(8,128)} %get-tuple-element.35), calls=%async_computation | async-start | bytes 458752 | tf_op jit(solution)/shard_map/all_to_all | solution.py:806
  71.5 0.6 pad_add_fusion.place
  72.2 8.0 %all-to-all-done = f32[8,56,128]{2,1,0:T(8,128)S(1)} async-done(((f32[8,56,128]{2,1,0:T(8,128)}), f32[8,56,128]{2,1,0:T(8,128)S(1)}, u32[]{:S(2)}, u32[]{:S(2)}) %all-to-all-start) | async-done | bytes 229408 | tf_op jit(solution)/shard_map/all_to_all | solution.py:806
  80.2 9.7 %all-gather.2 = f32[32,56,128]{2,1,0:T(8,128)} all-gather(f32[8,56,128]{2,1,0:T(8,128)S(1)} %all-to-all-done), channel_id=4, replica_groups=mesh['gx'=8,'gy'=4] {'gy'}, dimensions={0}, use_global_device_ids=true | all-gather | bytes 1146880 | tf_op jit(solution)/shard_map/all_gather | solution.py:806
  89.9 16.5 %up.1 = f32[16,2,32,256]{3,2,1,0:T(8,128)} custom-call(s32[2]{0:T(128)} %pad_add_fusion.place, f32[4,8,56,128]{3,2,1,0:T(8,128)} %bitcast.52, f32[40,3,32,128]{3,2,1,0:T(8,128)} %get-tuple-element.36.w0_in, f32[40,3,120,128]{3,2,1,0:T(8,128)} %get-tuple-element.37.coef0_in, f32[40,3,32,128]{3,2,1,0:T(8,128)} %get-tuple-element.38.scaled0_in, ...), custom_call_target="tpu_custom_call" | custom-call | tf_op jit(solution)/shard_map/up/pallas_call | solution.py:811
  (19 shorter events, 0.2 us)
Async XLA Ops:
  10.7 12.2 %collective-permute-start.1 = (f32[352,128]{1,0:T(8,128)S(1)}, f32[352,128]{1,0:T(8,128)S(1)}, u32[]{:S(2)}, u32[]{:S(2)}) collective-permute-start(f32[352,128]{1,0:T(8,128)S(1)} %get-tuple-element.61), channel_id=1, source_target_pairs={{4,0},{8,4},{12,8},{16,12},{20,16},{24,20},{28,24},{5,1},{9,5},{13... | collective-permute-start | bytes 540680 | tf_op jit(solution)/shard_map/ppermute | solution.py:730
  12.0 11.2 %collective-permute-start = (f32[352,128]{1,0:T(8,128)S(1)}, f32[352,128]{1,0:T(8,128)S(1)}, u32[]{:S(2)}, u32[]{:S(2)}) collective-permute-start(f32[352,128]{1,0:T(8,128)S(1)} %get-tuple-element.62), channel_id=1, source_target_pairs={{0,4},{4,8},{8,12},{12,16},{16,20},{20,24},{24,28},{1,5},{5,9},{9,... | collective-permute-start | bytes 540680 | tf_op jit(solution)/shard_map/ppermute | solution.py:729
  33.0 14.8 %collective-permute-start.3 = (f32[840,128]{1,0:T(8,128)S(1)}, f32[840,128]{1,0:T(8,128)S(1)}, u32[]{:S(2)}, u32[]{:S(2)}) collective-permute-start(f32[840,128]{1,0:T(8,128)S(1)} %get-tuple-element.57), channel_id=1, source_target_pairs={{4,0},{8,4},{12,8},{16,12},{20,16},{24,20},{28,24},{5,1},{9,5},{13... | collective-permute-start | bytes 1290248 | tf_op jit(solution)/shard_map/ppermute | solution.py:781
  34.3 22.9 %collective-permute-start.2 = (f32[840,128]{1,0:T(8,128)S(1)}, f32[840,128]{1,0:T(8,128)S(1)}, u32[]{:S(2)}, u32[]{:S(2)}) collective-permute-start(f32[840,128]{1,0:T(8,128)S(1)} %get-tuple-element.58), channel_id=1, source_target_pairs={{0,4},{4,8},{8,12},{12,16},{16,20},{20,24},{24,28},{1,5},{5,9},{9,... | collective-permute-start | bytes 1290248 | tf_op jit(solution)/shard_map/ppermute | solution.py:780
  65.8 14.4 %all-to-all-start = ((f32[8,56,128]{2,1,0:T(8,128)}), f32[8,56,128]{2,1,0:T(8,128)S(1)}, u32[]{:S(2)}, u32[]{:S(2)}) async-start(f32[8,56,128]{2,1,0:T(8,128)} %get-tuple-element.35), calls=%async_computation | async-start | bytes 458752 | tf_op jit(solution)/shard_map/all_to_all | solution.py:806

commit v7 on v6

--- a/solution.py
+++ b/solution.py
@@ -431,29 +431,31 @@
         copy.wait()
 
 
-def down12_kernel(own, left, right, from_low, from_high, piece, w1_out, coef1_out, scaled1_out, w2_out, coef2_out, scaled2_out,
+def down12_kernel(own, sides, from_low, from_high, sides_low, sides_high, piece, w1_out, coef1_out, scaled1_out, w2_out, coef2_out, scaled2_out,
                   data1, diag1, slope1, across1, wa1, coef1, scaled1, data2, diag2, slope2, across2, wa2, coef2, scaled2, sems):
     rows = own.shape[0]
     total = rows + 2 * RIM1
     group = LANES // STRIP1
     parts = rows // group
 
-    def rim(low, high, base, r):
+    def rim(strips, r):
         part, j = r // group, r % group
-        at = base + part * NP
-        return unpack_rim(low[at : at + NP, :], high[at : at + NP, :], j * STRIP1, STRIP1)
+        low, high = part * NP, (parts + part) * NP
+        return unpack_rim(strips[low : low + NP, :], strips[high : high + NP, :], j * STRIP1, STRIP1)
 
     def copy_row(r):
         data1[RIM1 + r, 0] = own[r]
 
     rows_loop(0, rows, copy_row, 4)
     for r in range(rows):
-        data1[RIM1 + r, 1] = rim(left, right, 0, r)
+        data1[RIM1 + r, 1] = rim(sides, r)
     inner = RIM1 - 1
     thick = 32 * inner
     thin = thick + 16 * RIM1
-    corner = thin + 2 * inner
-    for face, base, skip, first in ((from_low, 0, 1, rows - RIM1), (from_high, RIM1 + rows, 0, 0)):
+    for face, strips, base, skip, first in (
+        (from_low, sides_low, 0, 1, rows - RIM1),
+        (from_high, sides_high, RIM1 + rows, 0, 0),
+    ):
         for r in range(inner):
             data1[base + skip + r, 0, 0:32, :] = face[32 * r : 32 * r + 32, :]
             at = thin + 8 * (r // 4)
@@ -461,7 +463,7 @@
         for r in range(RIM1):
             at = thick + 16 * r
             data1[base + r, 0, 32:48, :] = face[at : at + 16, :]
-            data1[base + r, 1] = rim(face, face.at[pl.ds(parts * NP, face.shape[0] - parts * NP)], corner, first + r)
+            data1[base + r, 1] = rim(strips, first + r)
 
     make_coefs(data1, coef1, scaled1, diag1, 1, total - 1, 0.25, False, UNROLL1[2])
     copies = [copy_rows(coef1, coef1_out, sems.at[0], 10, total - 10)]
@@ -762,23 +764,16 @@
         name="outer0",
     )(data0, left, right, from_low, from_high, inner_coarse, *in_hbm(ups0))
 
-    left, right = beside(strips1)
-    left, right = left.reshape(-1, LANES), right.reshape(-1, LANES)
-
     def face1(which, first, first_inner):
-        parts = (
-            data1[first_inner : first_inner + inner1, 0:32],
-            data1[first : first + RIM1, 32:48],
-            edges1[which],
-            left,
-            right,
-        )
+        parts = (data1[first_inner : first_inner + inner1, 0:32], data1[first : first + RIM1, 32:48], edges1[which])
         return jnp.concatenate([v.reshape(-1, LANES) for v in parts], 0)
 
-    low_face = face1(0, 0, 0)
-    high_face = face1(1, rows1 - RIM1, rows1 - inner1)
-    from_low = lax.ppermute(high_face, "gx", upward)
-    from_high = lax.ppermute(low_face, "gx", downward)
+    from_low = lax.ppermute(face1(1, rows1 - RIM1, rows1 - inner1), "gx", upward)
+    from_high = lax.ppermute(face1(0, 0, 0), "gx", downward)
+    left, right = (v.reshape(-1, LANES) for v in beside(strips1))
+    sides = jnp.concatenate([left, right], 0)
+    sides_low = lax.ppermute(sides, "gx", upward)
+    sides_high = lax.ppermute(sides, "gx", downward)
 
     total1 = rows1 + 2 * RIM1
     rows2 = rows1 // 2
@@ -796,12 +791,12 @@
             stored(total2, 1, 8 * NC, LANES),
             field2,
         ),
-        in_specs=[VM] * 5,
+        in_specs=[VM] * 6,
         out_specs=(VM,) + (HB,) * 6,
         scratch_shapes=buffers(total1, 2, names) + buffers(total2, 1, names) + [pltpu.SemaphoreType.DMA((6,))],
         compiler_params=PARAMS,
         name="down12",
-    )(data1, left, right, from_low, from_high)
+    )(data1, sides, from_low, from_high, sides_low, sides_high)
 
     pieces = lax.all_gather(lax.all_to_all(piece, "gx", 0, 0), "gy", axis=0)
 

time: 107 us -> 106 us (level)
  waiting for transfers between devices: 26.1 us -> 19.2 us
  starting transfers between devices: 18 us -> 24 us
    ppermute x0 -> x4, starting transfers between devices: none -> 12.2 us  [the longest x1 5.18 us: per_device(): sides_low = lax.ppermute(sides, 'gx', upward)]
    ppermute x0 -> x4, waiting for transfers between devices: none -> 11 us  [the longest x1 5.93 us: per_device(): sides_high = lax.ppermute(sides, 'gx', downward)]
    ppermute x2 -> x1, waiting for transfers between devices: 9.61 us -> 0.22 us  [per_device(): from_low = lax.ppermute(high_face, 'gx', upward)]
    ppermute x2 -> x1, waiting for transfers between devices: 8.45 us -> 0.01 us  [per_device(): from_high = lax.ppermute(low_face, 'gx', downward)]
    ppermute x2 -> x1, starting transfers between devices: 9.6 us -> 4.56 us  [per_device(): from_low = lax.ppermute(high_face, 'gx', upward)]
    ppermute x2 -> x1, starting transfers between devices: 2.58 us -> 1.29 us  [per_device(): from_high = lax.ppermute(low_face, 'gx', downward)]
  transfers between devices with their start and end apart: 5 -> 7, of which waited for: 4 -> 4; matrix products, arithmetic and copies ran while one was open for 1% -> 1% of each run, Pallas kernels for 6% -> 6%
where the time goes in v7:
time: 106 us; the launch traced here: 105 us
  Pallas kernels  37.4 us (35%)
  starting transfers between devices  24 us (23%)
  blocking collectives  23.6 us (22%)
  waiting for transfers between devices  19.2 us (18%)
    pallas_call x1, Pallas kernels, per_device(): pl.pallas_call(up_kernel, out_shape=shape(16, 2, rows, columns), in_specs...  16.5 us
    all_gather x2, blocking collectives, beside(): every = lax.all_gather(strips, 'gy', axis=0)  14.2 us
    all_gather x1, blocking collectives, per_device(): pieces = lax.all_gather(lax.all_to_all(piece, 'gx', 0, 0), 'gy', axis=0)  9.44 us
    pallas_call x1, Pallas kernels, per_device(): pl.pallas_call(down12_kernel, out_shape=(shape(nx, NP, LANES), field1, st...  8.62 us
    all_to_all x1, waiting for transfers between devices, per_device(): pieces = lax.all_gather(lax.all_to_all(piece, 'gx', 0, 0), 'gy', axis=0)  8.04 us
    pallas_call x1, Pallas kernels, per_device(): pl.pallas_call(inner0_kernel, out_shape=(shape(rows1, NP, LANES),) + up0,...  6.37 us
    all_to_all x1, starting transfers between devices, per_device(): pieces = lax.all_gather(lax.all_to_all(piece, 'gx', 0, 0), 'gy', axis=0)  5.95 us
    ppermute x1, waiting for transfers between devices, per_device(): sides_high = lax.ppermute(sides, 'gx', downward)  5.93 us
  transfers between devices with their start and end apart: 7, of which 4 were waited for; matrix products, arithmetic and copies ran while one was open for 1% of the time, Pallas kernels for 6%

profile of v7, /device:TPU:0, one launch (start us, length us, event | category | flops | bytes accessed | tf_op | source)
XLA Modules:
  0.0 105.5 jit_solution(1121501745583476953)
XLA Ops:
  0.0 3.1 %arrange.1 = (f32[32,2,56,128]{3,2,1,0:T(8,128)S(1)}, f32[2,72,128]{2,1,0:T(8,128)S(1)}, f32[2,16,128]{2,1,0:T(8,128)S(1)}) custom-call(f32[16,2,32,256]{3,2,1,0:T(8,128)} %bitcast.49, f32[8,2,32,256]{3,2,1,0:T(8,128)} %bitcast.53, f32[32,256]{1,0:T(8,128)} %friction_in.1, s32[32,256]{1,0:T(8,128)} %ice_mask_in.1, s32[32,256]{1,0:T(8,128)} %grounded_in.1), custom_call_target="tpu_custom_call" | custom-call | tf_op jit(solution)/shard_map/arrange/pallas_call | solution.py:695
  3.2 7.4 %all-gather = f32[8,72,128]{2,1,0:T(8,128)S(1)} all-gather(f32[2,72,128]{2,1,0:T(8,128)S(1)} %get-tuple-element.26), channel_id=2, replica_groups=mesh['gx'=8,'gy'=4] {'gy'}, dimensions={0}, use_global_device_ids=true | all-gather | bytes 368640 | tf_op jit(solution)/shard_map/all_gather | solution.py:690
  10.7 1.3 %collective-permute-start.1 = (f32[352,128]{1,0:T(8,128)S(1)}, f32[352,128]{1,0:T(8,128)S(1)}, u32[]{:S(2)}, u32[]{:S(2)}) collective-permute-start(f32[352,128]{1,0:T(8,128)S(1)} %get-tuple-element.57), channel_id=1, source_target_pairs={{4,0},{8,4},{12,8},{16,12},{20,16},{24,20},{28,24},{5,1},{9,5},{13... | collective-permute-start | bytes 540680 | tf_op jit(solution)/shard_map/ppermute | solution.py:732
  12.0 4.6 %collective-permute-start = (f32[352,128]{1,0:T(8,128)S(1)}, f32[352,128]{1,0:T(8,128)S(1)}, u32[]{:S(2)}, u32[]{:S(2)}) collective-permute-start(f32[352,128]{1,0:T(8,128)S(1)} %get-tuple-element.58), channel_id=1, source_target_pairs={{0,4},{4,8},{8,12},{12,16},{16,20},{20,24},{24,28},{1,5},{5,9},{9,... | collective-permute-start | bytes 540680 | tf_op jit(solution)/shard_map/ppermute | solution.py:731
  16.6 6.4 %inner0.1 = (f32[16,56,128]{2,1,0:T(8,128)S(1)}, f32[40,3,32,128]{3,2,1,0:T(8,128)}, f32[40,3,120,128]{3,2,1,0:T(8,128)}, f32[40,3,32,128]{3,2,1,0:T(8,128)}) custom-call(f32[32,2,56,128]{3,2,1,0:T(8,128)S(1)} %get-tuple-element.25.own, f32[72,128]{1,0:T(8,128)S(1)} %bitcast.46, f32[72,128]{1,0:T(8,128)S(1)} %bitcast.44), custom_call_target="tpu_custom_call" | custom-call | flops 40000000 | bytes 20000000 | tf_op jit(solution)/shard_map/inner0/pallas_call | solution.py:741
  22.9 0.0 collective-permute-done.1.from_high
  22.9 0.2 collective-permute-done.from_low
  23.2 2.8 %outer0.1 = (f32[16,56,128]{2,1,0:T(8,128)S(1)}, f32[2,2,56,128]{3,2,1,0:T(8,128)S(1)}, f32[2,24,128]{2,1,0:T(8,128)S(1)}, f32[40,3,32,128]{3,2,1,0:T(8,128)}, f...) custom-call(f32[32,2,56,128]{3,2,1,0:T(8,128)S(1)} %get-tuple-elemen, ...), custom_call_target="tpu_custom_call", output_to_operand_aliasing={{3}: (6, {}), {4}: (7, {}), {5}: (8, {})} | custom-call | tf_op jit(solution)/shard_map/outer0/pallas_call | solution.py:751
  26.1 6.8 %all-gather.1 = f32[8,2,56,128]{3,2,1,0:T(8,128)S(1)} all-gather(f32[2,2,56,128]{3,2,1,0:T(8,128)S(1)} %get-tuple-element.33), channel_id=3, replica_groups=mesh['gx'=8,'gy'=4] {'gy'}, dimensions={0}, use_global_device_ids=true | all-gather | bytes 573440 | tf_op jit(solution)/shard_map/all_gather | solution.py:690
  32.9 4.4 %collective-permute-start.2 = (f32[616,128]{1,0:T(8,128)S(1)}, f32[616,128]{1,0:T(8,128)S(1)}, u32[]{:S(2)}, u32[]{:S(2)}) collective-permute-start(f32[616,128]{1,0:T(8,128)S(1)} %pad_maximum_fusion), channel_id=1, source_target_pairs={{0,4},{4,8},{8,12},{12,16},{16,20},{20,24},{24,28},{1,5},{5,9},{9,... | collective-permute-start | bytes 946184 | tf_op jit(solution)/shard_map/ppermute | solution.py:771
  37.3 1.3 %collective-permute-start.3 = (f32[616,128]{1,0:T(8,128)S(1)}, f32[616,128]{1,0:T(8,128)S(1)}, u32[]{:S(2)}, u32[]{:S(2)}) collective-permute-start(f32[616,128]{1,0:T(8,128)S(1)} %pad_maximum_fusion.1), channel_id=1, source_target_pairs={{4,0},{8,4},{12,8},{16,12},{20,16},{24,20},{28,24},{5,1},{9,5},{13... | collective-permute-start | bytes 946184 | tf_op jit(solution)/shard_map/ppermute | solution.py:772
  38.6 1.3 %collective-permute-start.5 = (f32[224,128]{1,0:T(8,128)S(1)}, f32[224,128]{1,0:T(8,128)S(1)}, u32[]{:S(2)}, u32[]{:S(2)}) collective-permute-start(f32[224,128]{1,0:T(8,128)S(1)} %pad_maximum_fusion.2.sides), channel_id=1, source_target_pairs={{4,0},{8,4},{12,8},{16,12},{20,16},{24,20},{28,24},{5,1},{9,5},{13... | collective-permute-start | bytes 344072 | tf_op jit(solution)/shard_map/ppermute | solution.py:776
  39.9 5.2 %collective-permute-start.4 = (f32[224,128]{1,0:T(8,128)S(1)}, f32[224,128]{1,0:T(8,128)S(1)}, u32[]{:S(2)}, u32[]{:S(2)}) collective-permute-start(f32[224,128]{1,0:T(8,128)S(1)} %pad_maximum_fusion.2.sides), channel_id=1, source_target_pairs={{0,4},{4,8},{8,12},{12,16},{16,20},{20,24},{24,28},{1,5},{5,9},{9,... | collective-permute-start | bytes 344072 | tf_op jit(solution)/shard_map/ppermute | solution.py:775
  45.1 5.9 %collective-permute-done.5.sides_high = f32[224,128]{1,0:T(8,128)S(1)} collective-permute-done((f32[224,128]{1,0:T(8,128)S(1)}, f32[224,128]{1,0:T(8,128)S(1)}, u32[]{:S(2)}, u32[]{:S(2)}) %collective-permute-start.5) | collective-permute-done | bytes 114720 | tf_op jit(solution)/shard_map/ppermute | solution.py:776
  51.1 5.1 %collective-permute-done.4.sides_low = f32[224,128]{1,0:T(8,128)S(1)} collective-permute-done((f32[224,128]{1,0:T(8,128)S(1)}, f32[224,128]{1,0:T(8,128)S(1)}, u32[]{:S(2)}, u32[]{:S(2)}) %collective-permute-start.4) | collective-permute-done | bytes 114720 | tf_op jit(solution)/shard_map/ppermute | solution.py:775
  56.1 0.0 collective-permute-done.2.from_low
  56.1 0.0 collective-permute-done.3.from_high
  56.1 8.6 %down12.1 = (f32[8,56,128]{2,1,0:T(8,128)}, f32[42,2,32,128]{3,2,1,0:T(8,128)}, f32[42,2,120,128]{3,2,1,0:T(8,128)}, f32[42,2,32,128]{3,2,1,0:T(8,128)}, f32[20,...) custom-call(f32[16,56,128]{2,1,0:T(8,128)S(1)} %get-tuple-element.32.own, ...), custom_call_target="tpu_custom_call" | custom-call | tf_op jit(solution)/shard_map/down12/pallas_call | solution.py:783
  64.8 5.9 %all-to-all-start = ((f32[8,56,128]{2,1,0:T(8,128)}), f32[8,56,128]{2,1,0:T(8,128)S(1)}, u32[]{:S(2)}, u32[]{:S(2)}) async-start(f32[8,56,128]{2,1,0:T(8,128)} %get-tuple-element.35), calls=%async_computation | async-start | bytes 458752 | tf_op jit(solution)/shard_map/all_to_all | solution.py:801
  70.7 0.6 pad_add_fusion.place
  71.3 8.0 %all-to-all-done = f32[8,56,128]{2,1,0:T(8,128)S(1)} async-done(((f32[8,56,128]{2,1,0:T(8,128)}), f32[8,56,128]{2,1,0:T(8,128)S(1)}, u32[]{:S(2)}, u32[]{:S(2)}) %all-to-all-start) | async-done | bytes 229408 | tf_op jit(solution)/shard_map/all_to_all | solution.py:801
  79.4 9.4 %all-gather.2 = f32[32,56,128]{2,1,0:T(8,128)} all-gather(f32[8,56,128]{2,1,0:T(8,128)S(1)} %all-to-all-done), channel_id=4, replica_groups=mesh['gx'=8,'gy'=4] {'gy'}, dimensions={0}, use_global_device_ids=true | all-gather | bytes 1146880 | tf_op jit(solution)/shard_map/all_gather | solution.py:801
  88.8 16.5 %up.1 = f32[16,2,32,256]{3,2,1,0:T(8,128)} custom-call(s32[2]{0:T(128)} %pad_add_fusion.place, f32[4,8,56,128]{3,2,1,0:T(8,128)} %bitcast.48, f32[40,3,32,128]{3,2,1,0:T(8,128)} %get-tuple-element.36.w0_in, f32[40,3,120,128]{3,2,1,0:T(8,128)} %get-tuple-element.37.coef0_in, f32[40,3,32,128]{3,2,1,0:T(8,128)} %get-tuple-element.38.scaled0_in, ...), custom_call_target="tpu_custom_call" | custom-call | tf_op jit(solution)/shard_map/up/pallas_call | solution.py:806
  (16 shorter events, 0.2 us)
Async XLA Ops:
  10.7 12.2 %collective-permute-start.1 = (f32[352,128]{1,0:T(8,128)S(1)}, f32[352,128]{1,0:T(8,128)S(1)}, u32[]{:S(2)}, u32[]{:S(2)}) collective-permute-start(f32[352,128]{1,0:T(8,128)S(1)} %get-tuple-element.57), channel_id=1, source_target_pairs={{4,0},{8,4},{12,8},{16,12},{20,16},{24,20},{28,24},{5,1},{9,5},{13... | collective-permute-start | bytes 540680 | tf_op jit(solution)/shard_map/ppermute | solution.py:732
  12.0 11.2 %collective-permute-start = (f32[352,128]{1,0:T(8,128)S(1)}, f32[352,128]{1,0:T(8,128)S(1)}, u32[]{:S(2)}, u32[]{:S(2)}) collective-permute-start(f32[352,128]{1,0:T(8,128)S(1)} %get-tuple-element.58), channel_id=1, source_target_pairs={{0,4},{4,8},{8,12},{12,16},{16,20},{20,24},{24,28},{1,5},{5,9},{9,... | collective-permute-start | bytes 540680 | tf_op jit(solution)/shard_map/ppermute | solution.py:731
  32.9 23.3 %collective-permute-start.2 = (f32[616,128]{1,0:T(8,128)S(1)}, f32[616,128]{1,0:T(8,128)S(1)}, u32[]{:S(2)}, u32[]{:S(2)}) collective-permute-start(f32[616,128]{1,0:T(8,128)S(1)} %pad_maximum_fusion), channel_id=1, source_target_pairs={{0,4},{4,8},{8,12},{12,16},{16,20},{20,24},{24,28},{1,5},{5,9},{9,... | collective-permute-start | bytes 946184 | tf_op jit(solution)/shard_map/ppermute | solution.py:771
  37.3 18.8 %collective-permute-start.3 = (f32[616,128]{1,0:T(8,128)S(1)}, f32[616,128]{1,0:T(8,128)S(1)}, u32[]{:S(2)}, u32[]{:S(2)}) collective-permute-start(f32[616,128]{1,0:T(8,128)S(1)} %pad_maximum_fusion.1), channel_id=1, source_target_pairs={{4,0},{8,4},{12,8},{16,12},{20,16},{24,20},{28,24},{5,1},{9,5},{13... | collective-permute-start | bytes 946184 | tf_op jit(solution)/shard_map/ppermute | solution.py:772
  38.6 12.4 %collective-permute-start.5 = (f32[224,128]{1,0:T(8,128)S(1)}, f32[224,128]{1,0:T(8,128)S(1)}, u32[]{:S(2)}, u32[]{:S(2)}) collective-permute-start(f32[224,128]{1,0:T(8,128)S(1)} %pad_maximum_fusion.2.sides), channel_id=1, source_target_pairs={{4,0},{8,4},{12,8},{16,12},{20,16},{24,20},{28,24},{5,1},{9,5},{13... | collective-permute-start | bytes 344072 | tf_op jit(solution)/shard_map/ppermute | solution.py:776
  39.9 16.2 %collective-permute-start.4 = (f32[224,128]{1,0:T(8,128)S(1)}, f32[224,128]{1,0:T(8,128)S(1)}, u32[]{:S(2)}, u32[]{:S(2)}) collective-permute-start(f32[224,128]{1,0:T(8,128)S(1)} %pad_maximum_fusion.2.sides), channel_id=1, source_target_pairs={{0,4},{4,8},{8,12},{12,16},{16,20},{20,24},{24,28},{1,5},{5,9},{9,... | collective-permute-start | bytes 344072 | tf_op jit(solution)/shard_map/ppermute | solution.py:775
  64.8 14.6 %all-to-all-start = ((f32[8,56,128]{2,1,0:T(8,128)}), f32[8,56,128]{2,1,0:T(8,128)S(1)}, u32[]{:S(2)}, u32[]{:S(2)}) async-start(f32[8,56,128]{2,1,0:T(8,128)} %get-tuple-element.35), calls=%async_computation | async-start | bytes 458752 | tf_op jit(solution)/shard_map/all_to_all | solution.py:801

commit v8 on v7

--- a/solution.py
+++ b/solution.py
@@ -25,10 +25,10 @@
 VMEM_UP = 60 * 1024 * 1024
 F32 = jnp.float32
 UNROLL0 = (18, 6, 4)
-UNROLL1 = (38, 12, 8)
-UNROLL2 = (18, 6, 4)
-UNROLL3 = (32, 32, 8)
-UNROLL0_UP = (18, 17)
+UNROLL1 = (38, 18, 20)
+UNROLL2 = (18, 16, 18)
+UNROLL3 = (32, 32, 16)
+UNROLL0_UP = (36, 34)
 UNROLL1_UP = (22, 20)
 UNROLL_MOVE = 8
 
@@ -532,15 +532,14 @@
             slope3[end, 0] = zero[:32]
             coef3[end, 0] = jnp.zeros((8 * NC, LANES), F32)
 
-    def assemble(d, carry):
+    def assemble(d):
         for i in range(rows3):
             line = jnp.zeros((NP, LANES), F32)
             for j in range(devices_y):
                 line = put(line, pieces[j, d], (j - i) * width, width, j * width)
             data3[RIM3 + d * rows3 + i, 0] = line
-        return carry
-
-    lax.fori_loop(0, devices_x, assemble, 0)
+
+    rows_loop(0, devices_x, assemble, 4)
     first, last = RIM3, RIM3 + whole
     make_coefs(data3, coef3, scaled3, None, first, last, 0.25 ** (LEVELS - 1), True, UNROLL3[2])
 
@@ -614,7 +613,7 @@
             for fine in (2 * r + 1, 2 * r + 2):
                 wa1[fine, t] = w1[fine, t] + adds[t]
 
-    rows_loop(4, total2 - 4, add1, UNROLL_MOVE)
+    rows_loop(4, total2 - 4, add1, 12)
     total1 = 2 * rows2 + 2 * RIM1
     sweep(wa1, wb1, coef1, scaled1, slope1, across1, 11, total1 - 11, False, UNROLL1_UP)
     sweep(wb1, wa1, coef1, scaled1, slope1, across1, 12, total1 - 12, False, UNROLL1_UP)
@@ -629,7 +628,7 @@
             for fine in (2 * r - 22, 2 * r - 21):
                 wa0[fine, t] = w0[fine, t] + adds[t]
 
-    rows_loop(12, total1 - 12, add0, UNROLL_MOVE)
+    rows_loop(12, total1 - 12, add0, 18)
     rows0 = 4 * rows2
     total0 = rows0 + 2 * RIM0
     sweep(wa0, wb0, coef0, scaled0, slope0, across0, 3, total0 - 3, False, UNROLL0_UP)

time: 106 us -> 103 us (0.972)
  Pallas kernels: 37.4 us -> 34.9 us
    pallas_call x1, Pallas kernels: 16.5 us -> 14.5 us  [per_device(): pl.pallas_call(up_kernel, out_shape=shape(16, 2, rows, columns), in_specs...]
where the time goes in v8:
time: 103 us
  Pallas kernels  34.9 us (34%)
  starting transfers between devices  24 us (23%)
  blocking collectives  23.6 us (23%)
  waiting for transfers between devices  19.2 us (19%)
    pallas_call x1, Pallas kernels, per_device(): pl.pallas_call(up_kernel, out_shape=shape(16, 2, rows, columns), in_specs...  14.5 us
    all_gather x2, blocking collectives, beside(): every = lax.all_gather(strips, 'gy', axis=0)  14.2 us
    all_gather x1, blocking collectives, per_device(): pieces = lax.all_gather(lax.all_to_all(piece, 'gx', 0, 0), 'gy', axis=0)  9.44 us
    pallas_call x1, Pallas kernels, per_device(): pl.pallas_call(down12_kernel, out_shape=(shape(nx, NP, LANES), field1, st...  8.11 us
    all_to_all x1, waiting for transfers between devices, per_device(): pieces = lax.all_gather(lax.all_to_all(piece, 'gx', 0, 0), 'gy', axis=0)  8.04 us
    pallas_call x1, Pallas kernels, per_device(): pl.pallas_call(inner0_kernel, out_shape=(shape(rows1, NP, LANES),) + up0,...  6.37 us
    all_to_all x1, starting transfers between devices, per_device(): pieces = lax.all_gather(lax.all_to_all(piece, 'gx', 0, 0), 'gy', axis=0)  5.95 us
    ppermute x1, waiting for transfers between devices, per_device(): sides_high = lax.ppermute(sides, 'gx', downward)  5.93 us
  transfers between devices with their start and end apart: 7, of which 4 were waited for; matrix products, arithmetic and copies ran while one was open for 1% of the time, Pallas kernels for 6%

profile of v8, /device:TPU:0, one launch (start us, length us, event | category | flops | bytes accessed | tf_op | source)
XLA Modules:
  0.0 102.9 jit_solution(13523999114212813085)
XLA Ops:
  0.0 3.1 %arrange.1 = (f32[32,2,56,128]{3,2,1,0:T(8,128)S(1)}, f32[2,72,128]{2,1,0:T(8,128)S(1)}, f32[2,16,128]{2,1,0:T(8,128)S(1)}) custom-call(f32[16,2,32,256]{3,2,1,0:T(8,128)} %bitcast.49, f32[8,2,32,256]{3,2,1,0:T(8,128)} %bitcast.53, f32[32,256]{1,0:T(8,128)} %friction_in.1, s32[32,256]{1,0:T(8,128)} %ice_mask_in.1, s32[32,256]{1,0:T(8,128)} %grounded_in.1), custom_call_target="tpu_custom_call" | custom-call | tf_op jit(solution)/shard_map/arrange/pallas_call | solution.py:694
  3.2 7.4 %all-gather = f32[8,72,128]{2,1,0:T(8,128)S(1)} all-gather(f32[2,72,128]{2,1,0:T(8,128)S(1)} %get-tuple-element.26), channel_id=2, replica_groups=mesh['gx'=8,'gy'=4] {'gy'}, dimensions={0}, use_global_device_ids=true | all-gather | bytes 368640 | tf_op jit(solution)/shard_map/all_gather | solution.py:689
  10.7 1.3 %collective-permute-start.1 = (f32[352,128]{1,0:T(8,128)S(1)}, f32[352,128]{1,0:T(8,128)S(1)}, u32[]{:S(2)}, u32[]{:S(2)}) collective-permute-start(f32[352,128]{1,0:T(8,128)S(1)} %get-tuple-element.57), channel_id=1, source_target_pairs={{4,0},{8,4},{12,8},{16,12},{20,16},{24,20},{28,24},{5,1},{9,5},{13... | collective-permute-start | bytes 540680 | tf_op jit(solution)/shard_map/ppermute | solution.py:731
  12.0 4.6 %collective-permute-start = (f32[352,128]{1,0:T(8,128)S(1)}, f32[352,128]{1,0:T(8,128)S(1)}, u32[]{:S(2)}, u32[]{:S(2)}) collective-permute-start(f32[352,128]{1,0:T(8,128)S(1)} %get-tuple-element.58), channel_id=1, source_target_pairs={{0,4},{4,8},{8,12},{12,16},{16,20},{20,24},{24,28},{1,5},{5,9},{9,... | collective-permute-start | bytes 540680 | tf_op jit(solution)/shard_map/ppermute | solution.py:730
  16.6 6.4 %inner0.1 = (f32[16,56,128]{2,1,0:T(8,128)S(1)}, f32[40,3,32,128]{3,2,1,0:T(8,128)}, f32[40,3,120,128]{3,2,1,0:T(8,128)}, f32[40,3,32,128]{3,2,1,0:T(8,128)}) custom-call(f32[32,2,56,128]{3,2,1,0:T(8,128)S(1)} %get-tuple-element.25.own, f32[72,128]{1,0:T(8,128)S(1)} %bitcast.46, f32[72,128]{1,0:T(8,128)S(1)} %bitcast.44), custom_call_target="tpu_custom_call" | custom-call | flops 40000000 | bytes 20000000 | tf_op jit(solution)/shard_map/inner0/pallas_call | solution.py:740
  22.9 0.0 collective-permute-done.1.from_high
  22.9 0.2 collective-permute-done.from_low
  23.2 2.8 %outer0.1 = (f32[16,56,128]{2,1,0:T(8,128)S(1)}, f32[2,2,56,128]{3,2,1,0:T(8,128)S(1)}, f32[2,24,128]{2,1,0:T(8,128)S(1)}, f32[40,3,32,128]{3,2,1,0:T(8,128)}, f...) custom-call(f32[32,2,56,128]{3,2,1,0:T(8,128)S(1)} %get-tuple-elemen, ...), custom_call_target="tpu_custom_call", output_to_operand_aliasing={{3}: (6, {}), {4}: (7, {}), {5}: (8, {})} | custom-call | tf_op jit(solution)/shard_map/outer0/pallas_call | solution.py:750
  26.1 6.8 %all-gather.1 = f32[8,2,56,128]{3,2,1,0:T(8,128)S(1)} all-gather(f32[2,2,56,128]{3,2,1,0:T(8,128)S(1)} %get-tuple-element.33), channel_id=3, replica_groups=mesh['gx'=8,'gy'=4] {'gy'}, dimensions={0}, use_global_device_ids=true | all-gather | bytes 573440 | tf_op jit(solution)/shard_map/all_gather | solution.py:689
  32.9 4.4 %collective-permute-start.2 = (f32[616,128]{1,0:T(8,128)S(1)}, f32[616,128]{1,0:T(8,128)S(1)}, u32[]{:S(2)}, u32[]{:S(2)}) collective-permute-start(f32[616,128]{1,0:T(8,128)S(1)} %pad_maximum_fusion), channel_id=1, source_target_pairs={{0,4},{4,8},{8,12},{12,16},{16,20},{20,24},{24,28},{1,5},{5,9},{9,... | collective-permute-start | bytes 946184 | tf_op jit(solution)/shard_map/ppermute | solution.py:770
  37.3 1.3 %collective-permute-start.3 = (f32[616,128]{1,0:T(8,128)S(1)}, f32[616,128]{1,0:T(8,128)S(1)}, u32[]{:S(2)}, u32[]{:S(2)}) collective-permute-start(f32[616,128]{1,0:T(8,128)S(1)} %pad_maximum_fusion.1), channel_id=1, source_target_pairs={{4,0},{8,4},{12,8},{16,12},{20,16},{24,20},{28,24},{5,1},{9,5},{13... | collective-permute-start | bytes 946184 | tf_op jit(solution)/shard_map/ppermute | solution.py:771
  38.6 1.3 %collective-permute-start.5 = (f32[224,128]{1,0:T(8,128)S(1)}, f32[224,128]{1,0:T(8,128)S(1)}, u32[]{:S(2)}, u32[]{:S(2)}) collective-permute-start(f32[224,128]{1,0:T(8,128)S(1)} %pad_maximum_fusion.2.sides), channel_id=1, source_target_pairs={{4,0},{8,4},{12,8},{16,12},{20,16},{24,20},{28,24},{5,1},{9,5},{13... | collective-permute-start | bytes 344072 | tf_op jit(solution)/shard_map/ppermute | solution.py:775
  39.9 5.2 %collective-permute-start.4 = (f32[224,128]{1,0:T(8,128)S(1)}, f32[224,128]{1,0:T(8,128)S(1)}, u32[]{:S(2)}, u32[]{:S(2)}) collective-permute-start(f32[224,128]{1,0:T(8,128)S(1)} %pad_maximum_fusion.2.sides), channel_id=1, source_target_pairs={{0,4},{4,8},{8,12},{12,16},{16,20},{20,24},{24,28},{1,5},{5,9},{9,... | collective-permute-start | bytes 344072 | tf_op jit(solution)/shard_map/ppermute | solution.py:774
  45.1 5.9 %collective-permute-done.5.sides_high = f32[224,128]{1,0:T(8,128)S(1)} collective-permute-done((f32[224,128]{1,0:T(8,128)S(1)}, f32[224,128]{1,0:T(8,128)S(1)}, u32[]{:S(2)}, u32[]{:S(2)}) %collective-permute-start.5) | collective-permute-done | bytes 114720 | tf_op jit(solution)/shard_map/ppermute | solution.py:775
  51.1 5.1 %collective-permute-done.4.sides_low = f32[224,128]{1,0:T(8,128)S(1)} collective-permute-done((f32[224,128]{1,0:T(8,128)S(1)}, f32[224,128]{1,0:T(8,128)S(1)}, u32[]{:S(2)}, u32[]{:S(2)}) %collective-permute-start.4) | collective-permute-done | bytes 114720 | tf_op jit(solution)/shard_map/ppermute | solution.py:774
  56.1 0.0 collective-permute-done.2.from_low
  56.1 0.0 collective-permute-done.3.from_high
  56.1 8.1 %down12.1 = (f32[8,56,128]{2,1,0:T(8,128)}, f32[42,2,32,128]{3,2,1,0:T(8,128)}, f32[42,2,120,128]{3,2,1,0:T(8,128)}, f32[42,2,32,128]{3,2,1,0:T(8,128)}, f32[20,...) custom-call(f32[16,56,128]{2,1,0:T(8,128)S(1)} %get-tuple-element.32.own, ...), custom_call_target="tpu_custom_call" | custom-call | tf_op jit(solution)/shard_map/down12/pallas_call | solution.py:782
  64.3 5.9 %all-to-all-start = ((f32[8,56,128]{2,1,0:T(8,128)}), f32[8,56,128]{2,1,0:T(8,128)S(1)}, u32[]{:S(2)}, u32[]{:S(2)}) async-start(f32[8,56,128]{2,1,0:T(8,128)} %get-tuple-element.35), calls=%async_computation | async-start | bytes 458752 | tf_op jit(solution)/shard_map/all_to_all | solution.py:800
  70.2 0.6 pad_add_fusion.place
  70.8 8.0 %all-to-all-done = f32[8,56,128]{2,1,0:T(8,128)S(1)} async-done(((f32[8,56,128]{2,1,0:T(8,128)}), f32[8,56,128]{2,1,0:T(8,128)S(1)}, u32[]{:S(2)}, u32[]{:S(2)}) %all-to-all-start) | async-done | bytes 229408 | tf_op jit(solution)/shard_map/all_to_all | solution.py:800
  78.9 9.4 %all-gather.2 = f32[32,56,128]{2,1,0:T(8,128)} all-gather(f32[8,56,128]{2,1,0:T(8,128)S(1)} %all-to-all-done), channel_id=4, replica_groups=mesh['gx'=8,'gy'=4] {'gy'}, dimensions={0}, use_global_device_ids=true | all-gather | bytes 1146880 | tf_op jit(solution)/shard_map/all_gather | solution.py:800
  88.3 14.5 %up.1 = f32[16,2,32,256]{3,2,1,0:T(8,128)} custom-call(s32[2]{0:T(128)} %pad_add_fusion.place, f32[4,8,56,128]{3,2,1,0:T(8,128)} %bitcast.48, f32[40,3,32,128]{3,2,1,0:T(8,128)} %get-tuple-element.36.w0_in, f32[40,3,120,128]{3,2,1,0:T(8,128)} %get-tuple-element.37.coef0_in, f32[40,3,32,128]{3,2,1,0:T(8,128)} %get-tuple-element.38.scaled0_in, ...), custom_call_target="tpu_custom_call" | custom-call | tf_op jit(solution)/shard_map/up/pallas_call | solution.py:805
  (16 shorter events, 0.2 us)
Async XLA Ops:
  10.7 12.2 %collective-permute-start.1 = (f32[352,128]{1,0:T(8,128)S(1)}, f32[352,128]{1,0:T(8,128)S(1)}, u32[]{:S(2)}, u32[]{:S(2)}) collective-permute-start(f32[352,128]{1,0:T(8,128)S(1)} %get-tuple-element.57), channel_id=1, source_target_pairs={{4,0},{8,4},{12,8},{16,12},{20,16},{24,20},{28,24},{5,1},{9,5},{13... | collective-permute-start | bytes 540680 | tf_op jit(solution)/shard_map/ppermute | solution.py:731
  12.0 11.2 %collective-permute-start = (f32[352,128]{1,0:T(8,128)S(1)}, f32[352,128]{1,0:T(8,128)S(1)}, u32[]{:S(2)}, u32[]{:S(2)}) collective-permute-start(f32[352,128]{1,0:T(8,128)S(1)} %get-tuple-element.58), channel_id=1, source_target_pairs={{0,4},{4,8},{8,12},{12,16},{16,20},{20,24},{24,28},{1,5},{5,9},{9,... | collective-permute-start | bytes 540680 | tf_op jit(solution)/shard_map/ppermute | solution.py:730
  32.9 23.3 %collective-permute-start.2 = (f32[616,128]{1,0:T(8,128)S(1)}, f32[616,128]{1,0:T(8,128)S(1)}, u32[]{:S(2)}, u32[]{:S(2)}) collective-permute-start(f32[616,128]{1,0:T(8,128)S(1)} %pad_maximum_fusion), channel_id=1, source_target_pairs={{0,4},{4,8},{8,12},{12,16},{16,20},{20,24},{24,28},{1,5},{5,9},{9,... | collective-permute-start | bytes 946184 | tf_op jit(solution)/shard_map/ppermute | solution.py:770
  37.3 18.8 %collective-permute-start.3 = (f32[616,128]{1,0:T(8,128)S(1)}, f32[616,128]{1,0:T(8,128)S(1)}, u32[]{:S(2)}, u32[]{:S(2)}) collective-permute-start(f32[616,128]{1,0:T(8,128)S(1)} %pad_maximum_fusion.1), channel_id=1, source_target_pairs={{4,0},{8,4},{12,8},{16,12},{20,16},{24,20},{28,24},{5,1},{9,5},{13... | collective-permute-start | bytes 946184 | tf_op jit(solution)/shard_map/ppermute | solution.py:771
  38.6 12.4 %collective-permute-start.5 = (f32[224,128]{1,0:T(8,128)S(1)}, f32[224,128]{1,0:T(8,128)S(1)}, u32[]{:S(2)}, u32[]{:S(2)}) collective-permute-start(f32[224,128]{1,0:T(8,128)S(1)} %pad_maximum_fusion.2.sides), channel_id=1, source_target_pairs={{4,0},{8,4},{12,8},{16,12},{20,16},{24,20},{28,24},{5,1},{9,5},{13... | collective-permute-start | bytes 344072 | tf_op jit(solution)/shard_map/ppermute | solution.py:775
  39.9 16.2 %collective-permute-start.4 = (f32[224,128]{1,0:T(8,128)S(1)}, f32[224,128]{1,0:T(8,128)S(1)}, u32[]{:S(2)}, u32[]{:S(2)}) collective-permute-start(f32[224,128]{1,0:T(8,128)S(1)} %pad_maximum_fusion.2.sides), channel_id=1, source_target_pairs={{0,4},{4,8},{8,12},{12,16},{16,20},{20,24},{24,28},{1,5},{5,9},{9,... | collective-permute-start | bytes 344072 | tf_op jit(solution)/shard_map/ppermute | solution.py:774
  64.3 14.6 %all-to-all-start = ((f32[8,56,128]{2,1,0:T(8,128)}), f32[8,56,128]{2,1,0:T(8,128)S(1)}, u32[]{:S(2)}, u32[]{:S(2)}) async-start(f32[8,56,128]{2,1,0:T(8,128)} %get-tuple-element.35), calls=%async_computation | async-start | bytes 458752 | tf_op jit(solution)/shard_map/all_to_all | solution.py:800

commit v9 on v8

--- a/solution.py
+++ b/solution.py
@@ -266,31 +266,33 @@
                 )
     for copy in copies:
         copy.start()
-    for copy in copies:
-        copy.wait()
     sub = lax.broadcasted_iota(jnp.int32, (8, LANES), 0)
     misfit_rows = misfit_half.reshape(4, -1, LANES)
     viscosity_rows = viscosity_half.reshape(4, -1, LANES)
 
-    def eight(i, carry):
+    def eight(t, i, carry):
         block = pl.ds(pl.multiple_of(8 * i, 8), 8)
-        for t in range(2):
-            lanes = pl.ds(t * LANES, LANES)
-            ices = ice_mask[block, lanes].astype(F32)
-            drags = friction[block, lanes] * grounded[block, lanes].astype(F32)
-            for j in range(8):
-                r = 8 * i + j
-                ice, drag = ices[j : j + 1], drags[j : j + 1]
-                for c in range(2):
-                    for p in range(2):
-                        v = misfit_rows[2 * t + p, pl.ds(8 * c * PITCH + r, 8, stride=PITCH), :]
-                        data[r, t, 16 * c + 8 * p : 16 * c + 8 * p + 8, :] = v * ice
+        lanes = pl.ds(t * LANES, LANES)
+        ices = ice_mask[block, lanes].astype(F32)
+        drags = friction[block, lanes] * grounded[block, lanes].astype(F32)
+        for j in range(8):
+            r = 8 * i + j
+            ice, drag = ices[j : j + 1], drags[j : j + 1]
+            for c in range(2):
                 for p in range(2):
-                    data[r, t, 32 + 8 * p : 40 + 8 * p, :] = viscosity_rows[2 * t + p, pl.ds(r, 8, stride=PITCH), :]
-                data[r, t, 48:56, :] = jnp.where(sub == 0, ice, jnp.where(sub == 1, drag, 0.0))
+                    v = misfit_rows[2 * t + p, pl.ds(8 * c * PITCH + r, 8, stride=PITCH), :]
+                    data[r, t, 16 * c + 8 * p : 16 * c + 8 * p + 8, :] = v * ice
+            for p in range(2):
+                data[r, t, 32 + 8 * p : 40 + 8 * p, :] = viscosity_rows[2 * t + p, pl.ds(r, 8, stride=PITCH), :]
+            data[r, t, 48:56, :] = jnp.where(sub == 0, ice, jnp.where(sub == 1, drag, 0.0))
         return carry
 
-    lax.fori_loop(0, rows // 8, eight, 0)
+    for copy in copies[:3]:
+        copy.wait()
+    for t in range(2):
+        for copy in copies[3 + 4 * t : 7 + 4 * t]:
+            copy.wait()
+        lax.fori_loop(0, rows // 8, functools.partial(eight, t), 0)
     corner = RIM0 * RIM0
     for side in range(2):
         low = jnp.zeros((8, LANES), F32)
@@ -769,7 +771,11 @@
 
     from_low = lax.ppermute(face1(1, rows1 - RIM1, rows1 - inner1), "gx", upward)
     from_high = lax.ppermute(face1(0, 0, 0), "gx", downward)
-    left, right = (v.reshape(-1, LANES) for v in beside(strips1))
+    slots = lax.broadcasted_iota(jnp.int32, (ny, 1, 1, 1), 0)
+    sent = jnp.where(slots == gy - 1, strips1[:1], jnp.where(slots == gy + 1, strips1[1:], 0.0).reshape((ny,) + strips1.shape[1:]))
+    got = lax.all_to_all(sent, "gy", 0, 0)
+    left = jnp.where(gy > 0, lax.dynamic_index_in_dim(got, jnp.maximum(gy - 1, 0), 0, keepdims=False), 0.0).reshape(-1, LANES)
+    right = jnp.where(gy < ny - 1, lax.dynamic_index_in_dim(got, jnp.minimum(gy + 1, ny - 1), 0, keepdims=False), 0.0).reshape(-1, LANES)
     sides = jnp.concatenate([left, right], 0)
     sides_low = lax.ppermute(sides, "gx", upward)
     sides_high = lax.ppermute(sides, "gx", downward)

time: 103 us -> 101 us (0.981)
  blocking collectives: 23.6 us -> 17.5 us
  starting transfers between devices: 24 us -> 27.4 us
    all_gather x2 -> x1, blocking collectives: 14.2 us -> 7.4 us  [beside(): every = lax.all_gather(strips, 'gy', axis=0)]
    all_to_all x0 -> x1, starting transfers between devices: none -> 3.39 us  [per_device(): got = lax.all_to_all(sent, 'gy', 0, 0)]
  transfers between devices with their start and end apart: 7 -> 8, of which waited for: 4 -> 4; matrix products, arithmetic and copies ran while one was open for 1% -> 1% of each run, Pallas kernels for 6% -> 6%
where the time goes in v9:
time: 101 us
  Pallas kernels  34.7 us (34%)
  starting transfers between devices  27.4 us (27%)
  waiting for transfers between devices  19.3 us (19%)
  blocking collectives  17.5 us (17%)
  other arithmetic  1.54 us (2%)
    pallas_call x1, Pallas kernels, per_device(): pl.pallas_call(up_kernel, out_shape=shape(16, 2, rows, columns), in_specs...  14.5 us
    all_gather x1, blocking collectives, per_device(): pieces = lax.all_gather(lax.all_to_all(piece, 'gx', 0, 0), 'gy', axis=0)  10.1 us
    pallas_call x1, Pallas kernels, per_device(): pl.pallas_call(down12_kernel, out_shape=(shape(nx, NP, LANES), field1, st...  8.09 us
    all_to_all x1, waiting for transfers between devices, per_device(): pieces = lax.all_gather(lax.all_to_all(piece, 'gx', 0, 0), 'gy', axis=0)  8 us
    all_gather x1, blocking collectives, beside(): every = lax.all_gather(strips, 'gy', axis=0)  7.4 us
    pallas_call x1, Pallas kernels, per_device(): pl.pallas_call(inner0_kernel, out_shape=(shape(rows1, NP, LANES),) + up0,...  6.37 us
    ppermute x1, waiting for transfers between devices, per_device(): sides_high = lax.ppermute(sides, 'gx', downward)  6.04 us
    all_to_all x1, starting transfers between devices, per_device(): pieces = lax.all_gather(lax.all_to_all(piece, 'gx', 0, 0), 'gy', axis=0)  5.95 us
  transfers between devices with their start and end apart: 8, of which 4 were waited for; matrix products, arithmetic and copies ran while one was open for 1% of the time, Pallas kernels for 6%

profile of v9, /device:TPU:0, one launch (start us, length us, event | category | flops | bytes accessed | tf_op | source)
XLA Modules:
  0.0 101.0 jit_solution(10196242831533259574)
XLA Ops:
  0.0 3.0 %arrange.1 = (f32[32,2,56,128]{3,2,1,0:T(8,128)S(1)}, f32[2,72,128]{2,1,0:T(8,128)S(1)}, f32[2,16,128]{2,1,0:T(8,128)S(1)}) custom-call(f32[16,2,32,256]{3,2,1,0:T(8,128)} %bitcast.52, f32[8,2,32,256]{3,2,1,0:T(8,128)} %bitcast.55, f32[32,256]{1,0:T(8,128)} %friction_in.1, s32[32,256]{1,0:T(8,128)} %ice_mask_in.1, s32[32,256]{1,0:T(8,128)} %grounded_in.1), custom_call_target="tpu_custom_call" | custom-call | tf_op jit(solution)/shard_map/arrange/pallas_call | solution.py:696
  3.1 7.4 %all-gather = f32[8,72,128]{2,1,0:T(8,128)S(1)} all-gather(f32[2,72,128]{2,1,0:T(8,128)S(1)} %get-tuple-element.26), channel_id=2, replica_groups=mesh['gx'=8,'gy'=4] {'gy'}, dimensions={0}, use_global_device_ids=true | all-gather | bytes 368640 | tf_op jit(solution)/shard_map/all_gather | solution.py:691
  10.5 1.3 %collective-permute-start.1 = (f32[352,128]{1,0:T(8,128)S(1)}, f32[352,128]{1,0:T(8,128)S(1)}, u32[]{:S(2)}, u32[]{:S(2)}) collective-permute-start(f32[352,128]{1,0:T(8,128)S(1)} %get-tuple-element.59), channel_id=1, source_target_pairs={{4,0},{8,4},{12,8},{16,12},{20,16},{24,20},{28,24},{5,1},{9,5},{13... | collective-permute-start | bytes 540680 | tf_op jit(solution)/shard_map/ppermute | solution.py:733
  11.8 4.6 %collective-permute-start = (f32[352,128]{1,0:T(8,128)S(1)}, f32[352,128]{1,0:T(8,128)S(1)}, u32[]{:S(2)}, u32[]{:S(2)}) collective-permute-start(f32[352,128]{1,0:T(8,128)S(1)} %get-tuple-element.60), channel_id=1, source_target_pairs={{0,4},{4,8},{8,12},{12,16},{16,20},{20,24},{24,28},{1,5},{5,9},{9,... | collective-permute-start | bytes 540680 | tf_op jit(solution)/shard_map/ppermute | solution.py:732
  16.4 6.4 %inner0.1 = (f32[16,56,128]{2,1,0:T(8,128)S(1)}, f32[40,3,32,128]{3,2,1,0:T(8,128)}, f32[40,3,120,128]{3,2,1,0:T(8,128)}, f32[40,3,32,128]{3,2,1,0:T(8,128)}) custom-call(f32[32,2,56,128]{3,2,1,0:T(8,128)S(1)} %get-tuple-element.25.own, f32[72,128]{1,0:T(8,128)S(1)} %bitcast.49, f32[72,128]{1,0:T(8,128)S(1)} %bitcast.47), custom_call_target="tpu_custom_call" | custom-call | flops 40000000 | bytes 20000000 | tf_op jit(solution)/shard_map/inner0/pallas_call | solution.py:742
  22.8 0.0 collective-permute-done.1.from_high
  22.8 0.2 collective-permute-done.from_low
  23.0 2.8 %outer0.1 = (f32[16,56,128]{2,1,0:T(8,128)S(1)}, f32[2,2,56,128]{3,2,1,0:T(8,128)S(1)}, f32[2,24,128]{2,1,0:T(8,128)S(1)}, f32[40,3,32,128]{3,2,1,0:T(8,128)}, f...) custom-call(f32[32,2,56,128]{3,2,1,0:T(8,128)S(1)} %get-tuple-elemen, ...), custom_call_target="tpu_custom_call", output_to_operand_aliasing={{3}: (6, {}), {4}: (7, {}), {5}: (8, {})} | custom-call | tf_op jit(solution)/shard_map/outer0/pallas_call | solution.py:752
  25.9 0.8 select_select_fusion
  26.7 3.4 %all-to-all-start = ((f32[4,2,56,128]{3,2,1,0:T(8,128)}), f32[4,2,56,128]{3,2,1,0:T(8,128)S(1)}, u32[]{:S(2)}, u32[]{:S(2)}) async-start(f32[4,2,56,128]{3,2,1,0:T(8,128)} %select_select_fusion), calls=%async_computation | async-start | bytes 458752 | tf_op jit(solution)/shard_map/all_to_all | solution.py:776
  30.1 4.4 %collective-permute-start.2 = (f32[616,128]{1,0:T(8,128)S(1)}, f32[616,128]{1,0:T(8,128)S(1)}, u32[]{:S(2)}, u32[]{:S(2)}) collective-permute-start(f32[616,128]{1,0:T(8,128)S(1)} %pad_maximum_fusion), channel_id=1, source_target_pairs={{0,4},{4,8},{8,12},{12,16},{16,20},{20,24},{24,28},{1,5},{5,9},{9,... | collective-permute-start | bytes 946184 | tf_op jit(solution)/shard_map/ppermute | solution.py:772
  34.6 1.3 %collective-permute-start.3 = (f32[616,128]{1,0:T(8,128)S(1)}, f32[616,128]{1,0:T(8,128)S(1)}, u32[]{:S(2)}, u32[]{:S(2)}) collective-permute-start(f32[616,128]{1,0:T(8,128)S(1)} %pad_maximum_fusion.1), channel_id=1, source_target_pairs={{4,0},{8,4},{12,8},{16,12},{20,16},{24,20},{28,24},{5,1},{9,5},{13... | collective-permute-start | bytes 946184 | tf_op jit(solution)/shard_map/ppermute | solution.py:773
  35.9 0.0 all-to-all-done
  35.9 1.3 %collective-permute-start.5 = (f32[224,128]{1,0:T(8,128)S(1)}, f32[224,128]{1,0:T(8,128)S(1)}, u32[]{:S(2)}, u32[]{:S(2)}) collective-permute-start(f32[224,128]{1,0:T(8,128)S(1)} %pad_maximum_fusion.2.sides), channel_id=1, source_target_pairs={{4,0},{8,4},{12,8},{16,12},{20,16},{24,20},{28,24},{5,1},{9,5},{13... | collective-permute-start | bytes 344072 | tf_op jit(solution)/shard_map/ppermute | solution.py:781
  37.2 5.2 %collective-permute-start.4 = (f32[224,128]{1,0:T(8,128)S(1)}, f32[224,128]{1,0:T(8,128)S(1)}, u32[]{:S(2)}, u32[]{:S(2)}) collective-permute-start(f32[224,128]{1,0:T(8,128)S(1)} %pad_maximum_fusion.2.sides), channel_id=1, source_target_pairs={{0,4},{4,8},{8,12},{12,16},{16,20},{20,24},{24,28},{1,5},{5,9},{9,... | collective-permute-start | bytes 344072 | tf_op jit(solution)/shard_map/ppermute | solution.py:780
  42.4 6.0 %collective-permute-done.5.sides_high = f32[224,128]{1,0:T(8,128)S(1)} collective-permute-done((f32[224,128]{1,0:T(8,128)S(1)}, f32[224,128]{1,0:T(8,128)S(1)}, u32[]{:S(2)}, u32[]{:S(2)}) %collective-permute-start.5) | collective-permute-done | bytes 114720 | tf_op jit(solution)/shard_map/ppermute | solution.py:781
  48.5 5.1 %collective-permute-done.4.sides_low = f32[224,128]{1,0:T(8,128)S(1)} collective-permute-done((f32[224,128]{1,0:T(8,128)S(1)}, f32[224,128]{1,0:T(8,128)S(1)}, u32[]{:S(2)}, u32[]{:S(2)}) %collective-permute-start.4) | collective-permute-done | bytes 114720 | tf_op jit(solution)/shard_map/ppermute | solution.py:780
  53.5 0.0 collective-permute-done.2.from_low
  53.5 0.0 collective-permute-done.3.from_high
  53.5 8.1 %down12.1 = (f32[8,56,128]{2,1,0:T(8,128)}, f32[42,2,32,128]{3,2,1,0:T(8,128)}, f32[42,2,120,128]{3,2,1,0:T(8,128)}, f32[42,2,32,128]{3,2,1,0:T(8,128)}, f32[20,...) custom-call(f32[16,56,128]{2,1,0:T(8,128)S(1)} %get-tuple-element.32.own, ...), custom_call_target="tpu_custom_call" | custom-call | tf_op jit(solution)/shard_map/down12/pallas_call | solution.py:788
  61.6 5.9 %all-to-all-start.1 = ((f32[8,56,128]{2,1,0:T(8,128)}), f32[8,56,128]{2,1,0:T(8,128)S(1)}, u32[]{:S(2)}, u32[]{:S(2)}) async-start(f32[8,56,128]{2,1,0:T(8,128)} %get-tuple-element.35), calls=%async_computation.1 | async-start | bytes 458752 | tf_op jit(solution)/shard_map/all_to_all | solution.py:806
  67.6 0.7 pad_add_fusion.place
  68.2 8.0 %all-to-all-done.1 = f32[8,56,128]{2,1,0:T(8,128)S(1)} async-done(((f32[8,56,128]{2,1,0:T(8,128)}), f32[8,56,128]{2,1,0:T(8,128)S(1)}, u32[]{:S(2)}, u32[]{:S(2)}) %all-to-all-start.1) | async-done | bytes 229408 | tf_op jit(solution)/shard_map/all_to_all | solution.py:806
  76.2 10.1 %all-gather.1 = f32[32,56,128]{2,1,0:T(8,128)} all-gather(f32[8,56,128]{2,1,0:T(8,128)S(1)} %all-to-all-done.1), channel_id=3, replica_groups=mesh['gx'=8,'gy'=4] {'gy'}, dimensions={0}, use_global_device_ids=true | all-gather | bytes 1146880 | tf_op jit(solution)/shard_map/all_gather | solution.py:806
  86.3 14.5 %up.1 = f32[16,2,32,256]{3,2,1,0:T(8,128)} custom-call(s32[2]{0:T(128)} %pad_add_fusion.place, f32[4,8,56,128]{3,2,1,0:T(8,128)} %bitcast.51, f32[40,3,32,128]{3,2,1,0:T(8,128)} %get-tuple-element.36.w0_in, f32[40,3,120,128]{3,2,1,0:T(8,128)} %get-tuple-element.37.coef0_in, f32[40,3,32,128]{3,2,1,0:T(8,128)} %get-tuple-element.38.scaled0_in, ...), custom_call_target="tpu_custom_call" | custom-call | tf_op jit(solution)/shard_map/up/pallas_call | solution.py:811
  (18 shorter events, 0.2 us)
Async XLA Ops:
  10.5 12.3 %collective-permute-start.1 = (f32[352,128]{1,0:T(8,128)S(1)}, f32[352,128]{1,0:T(8,128)S(1)}, u32[]{:S(2)}, u32[]{:S(2)}) collective-permute-start(f32[352,128]{1,0:T(8,128)S(1)} %get-tuple-element.59), channel_id=1, source_target_pairs={{4,0},{8,4},{12,8},{16,12},{20,16},{24,20},{28,24},{5,1},{9,5},{13... | collective-permute-start | bytes 540680 | tf_op jit(solution)/shard_map/ppermute | solution.py:733
  11.8 11.2 %collective-permute-start = (f32[352,128]{1,0:T(8,128)S(1)}, f32[352,128]{1,0:T(8,128)S(1)}, u32[]{:S(2)}, u32[]{:S(2)}) collective-permute-start(f32[352,128]{1,0:T(8,128)S(1)} %get-tuple-element.60), channel_id=1, source_target_pairs={{0,4},{4,8},{8,12},{12,16},{16,20},{20,24},{24,28},{1,5},{5,9},{9,... | collective-permute-start | bytes 540680 | tf_op jit(solution)/shard_map/ppermute | solution.py:732
  26.7 9.2 %all-to-all-start = ((f32[4,2,56,128]{3,2,1,0:T(8,128)}), f32[4,2,56,128]{3,2,1,0:T(8,128)S(1)}, u32[]{:S(2)}, u32[]{:S(2)}) async-start(f32[4,2,56,128]{3,2,1,0:T(8,128)} %select_select_fusion), calls=%async_computation | async-start | bytes 458752 | tf_op jit(solution)/shard_map/all_to_all | solution.py:776
  30.1 23.4 %collective-permute-start.2 = (f32[616,128]{1,0:T(8,128)S(1)}, f32[616,128]{1,0:T(8,128)S(1)}, u32[]{:S(2)}, u32[]{:S(2)}) collective-permute-start(f32[616,128]{1,0:T(8,128)S(1)} %pad_maximum_fusion), channel_id=1, source_target_pairs={{0,4},{4,8},{8,12},{12,16},{16,20},{20,24},{24,28},{1,5},{5,9},{9,... | collective-permute-start | bytes 946184 | tf_op jit(solution)/shard_map/ppermute | solution.py:772
  34.6 18.9 %collective-permute-start.3 = (f32[616,128]{1,0:T(8,128)S(1)}, f32[616,128]{1,0:T(8,128)S(1)}, u32[]{:S(2)}, u32[]{:S(2)}) collective-permute-start(f32[616,128]{1,0:T(8,128)S(1)} %pad_maximum_fusion.1), channel_id=1, source_target_pairs={{4,0},{8,4},{12,8},{16,12},{20,16},{24,20},{28,24},{5,1},{9,5},{13... | collective-permute-start | bytes 946184 | tf_op jit(solution)/shard_map/ppermute | solution.py:773
  35.9 12.5 %collective-permute-start.5 = (f32[224,128]{1,0:T(8,128)S(1)}, f32[224,128]{1,0:T(8,128)S(1)}, u32[]{:S(2)}, u32[]{:S(2)}) collective-permute-start(f32[224,128]{1,0:T(8,128)S(1)} %pad_maximum_fusion.2.sides), channel_id=1, source_target_pairs={{4,0},{8,4},{12,8},{16,12},{20,16},{24,20},{28,24},{5,1},{9,5},{13... | collective-permute-start | bytes 344072 | tf_op jit(solution)/shard_map/ppermute | solution.py:781
  37.2 16.3 %collective-permute-start.4 = (f32[224,128]{1,0:T(8,128)S(1)}, f32[224,128]{1,0:T(8,128)S(1)}, u32[]{:S(2)}, u32[]{:S(2)}) collective-permute-start(f32[224,128]{1,0:T(8,128)S(1)} %pad_maximum_fusion.2.sides), channel_id=1, source_target_pairs={{0,4},{4,8},{8,12},{12,16},{16,20},{20,24},{24,28},{1,5},{5,9},{9,... | collective-permute-start | bytes 344072 | tf_op jit(solution)/shard_map/ppermute | solution.py:780
  61.6 14.6 %all-to-all-start.1 = ((f32[8,56,128]{2,1,0:T(8,128)}), f32[8,56,128]{2,1,0:T(8,128)S(1)}, u32[]{:S(2)}, u32[]{:S(2)}) async-start(f32[8,56,128]{2,1,0:T(8,128)} %get-tuple-element.35), calls=%async_computation.1 | async-start | bytes 458752 | tf_op jit(solution)/shard_map/all_to_all | solution.py:806
